TPU v7x, 32 devices: a whole 2x2x4 slice. The times are simulated.
32 devices in a mesh: tm: 8 (over y, x, core), freq: 4 (over z).
Axes of the slice: x: 2, y: 2, z: 4, core: 2. Of those that a mesh axis runs over, the one named last changes fastest.
Arguments:
- spectrum: bfloat16 [1024, 6144], P('freq', 'tm'), may hold values from 0.0099487305 to 10
- decay_rate: float32 [1024], P('freq'), may hold values from 1e-07 to 0.03
- init_state: float32 [1024], P('freq'), may hold values from 0.3 to 3
- clip_ids: int32 [6144], P('tm'), may hold values from 0 to 5, never falling along the last dimension, each value on 1 to 2048 neighbouring positions
- encoder: bfloat16 [256, 1024], P(None, 'freq'), may hold values from -0.1875 to 0.1875
- gauss_noise: float32 [256, 6144], P(None, 'tm'), may hold values from -3 to 3
- uniform_noise: float32 [2, 256, 6144], P(None, None, 'tm'), may hold values from 0.02 to 1
- boost_count: int32 [256], replicated, may hold values from 1 to 2
- templates: bfloat16 [1024, 4096], P('freq'), may hold values from 0.0099487305 to 1
Outputs:
- frame_loss: float32 [6144], P('tm')
- template_grad: float32 [4096, 1024], P('tm', 'freq')
Inputs may be any that keep to these rules, and one draw needn't show every extreme that they name: `clip_ids`: clip numbers never fall along the frames; each clip holds 1 to 2048 frames, one exactly that many.
All inputs are finite; a program needn't handle non-finite values.
Results may differ from a plain program's by a relative error of at most 0.00033.
Values may be sent and summed in bfloat16 or wider, within the bound.
No kernel may reach another device: no remote copies, remote signals or barrier semaphores. Data moves between devices by JAX's collectives and lax.ppermute only.
A program may use at most 64 MiB of HBM per device.

v0:
```python
import jax
import jax.numpy as jnp
from jax import lax
from jax.sharding import PartitionSpec as P

F = 1024
K = 256
L = 16


def prefix(part, axis, combine, identity):
    place = lax.axis_index(axis)
    gathered = jax.tree.map(lambda a: lax.all_gather(a, axis), part)
    state = jax.tree.map(lambda a, e: jnp.zeros_like(a) + jnp.asarray(e, a.dtype), part, identity)

    def one(lap, state):
        return combine(
            state, jax.tree.map(lambda a: lax.dynamic_index_in_dim(a, lap, 0, False), gathered)
        )

    return lax.fori_loop(0, place, one, state)


def passed_along(value, axis, steps):
    count = lax.axis_size(axis)
    leading, last = (max(0, -steps), min(count, count - steps))
    return lax.ppermute(value, axis, [(source, source + steps) for source in range(leading, last)])


def compose(former, latter):
    return (former[0] * latter[0], latter[0] * former[1] + latter[1])


def linked(former, latter):
    p_one, q_one, first_one, last_one, start_one, mark_one = former
    p_two, q_two, first_two, last_two, start_two, mark_two = latter
    joined = (last_one >= 0.0) & (first_two >= 0.0) & (first_two != last_one)
    factor = jnp.where(joined, 0.8, 1.0)
    scaled = p_two * factor
    merged_p = scaled * p_one
    merged_q = scaled * q_one + q_two
    first_clip = jnp.where(first_one >= 0.0, first_one, first_two)
    start_frame = jnp.where(first_one >= 0.0, start_one, start_two)
    last_clip = jnp.where(last_two >= 0.0, last_two, last_one)
    latest = jnp.maximum(jnp.maximum(mark_one, jnp.where(joined, start_two, -1.0)), mark_two)
    return (merged_p, merged_q, first_clip, last_clip, start_frame, latest)


def topic_mixture(logits, gaussian, uniforms, boost_count):
    concentration = jax.nn.softplus(logits) + 0.5
    boosted = boost_count[:, None]
    shape_total = concentration + boosted.astype(jnp.float32)
    offset = shape_total - 1.0 / 3.0
    spread = lax.rsqrt(9.0 * offset)
    linear = 1.0 + spread * gaussian
    gamma_draw = offset * linear * linear * linear * jnp.exp(jnp.log(uniforms[0]) / concentration)
    gamma_draw = gamma_draw * jnp.where(
        boosted >= 2, jnp.exp(jnp.log(uniforms[1]) / (concentration + 1.0)), 1.0
    )
    return (gamma_draw / jnp.sum(gamma_draw, axis=0, keepdims=True)).astype(jnp.bfloat16)


def on_device(
    spectrum,
    decay_rate,
    init_state,
    clip_ids,
    encoder,
    gauss_noise,
    uniform_noise,
    boost_count,
    templates,
):
    frames = spectrum.shape[1]
    bins = spectrum.shape[0]
    rim_width = L - 1
    spectral = spectrum.astype(jnp.float32)
    changed = clip_ids[1:] != clip_ids[:-1]
    factor_row = jnp.concatenate(
        [jnp.ones((1,), jnp.float32), jnp.where(changed, 0.8, 1.0).astype(jnp.float32)]
    )
    rates = (1.0 - decay_rate)[:, None] * factor_row[None, :]
    inputs = decay_rate[:, None] * spectral
    running, summed = lax.associative_scan(compose, (rates, inputs), axis=1)
    anchor = lax.axis_index("tm") * frames
    positions = anchor + jnp.arange(frames, dtype=jnp.int32)
    marks = jnp.where(jnp.concatenate([jnp.zeros((1,), bool), changed]), positions, -1)
    clip_float = clip_ids.astype(jnp.float32)
    summary = (
        running[:, -1],
        summed[:, -1],
        clip_float[:1],
        clip_float[-1:],
        jnp.reshape(anchor.astype(jnp.float32), (1,)),
        jnp.reshape(jnp.max(marks).astype(jnp.float32), (1,)),
    )
    minus_one = jnp.full((1,), -1.0, jnp.float32)
    identity_tuple = (
        jnp.ones((bins,), jnp.float32),
        jnp.zeros((bins,), jnp.float32),
        minus_one,
        minus_one,
        minus_one,
        minus_one,
    )
    before = prefix(summary, "tm", linked, identity_tuple)
    junction = (before[3] >= 0.0) & (clip_float[:1] != before[3])
    entry = jnp.where(junction, 0.8, 1.0) * (before[0] * init_state + before[1])
    smooth = running * entry[:, None] + summed
    normed = (spectral * lax.rsqrt(smooth + 0.1)).astype(jnp.bfloat16)
    code_part = jnp.dot(encoder, normed, preferred_element_type=jnp.float32)
    logits = lax.psum(code_part, "freq")
    proportions = topic_mixture(logits, gauss_noise, uniform_noise, boost_count)
    topics = proportions.shape[0]
    rim = passed_along(proportions[:, frames - rim_width :], "tm", 1)
    extended = jnp.concatenate([rim, proportions], axis=1)
    flags = jnp.concatenate([junction, changed]).astype(jnp.int32)
    clean = jnp.cumsum(flags) == 0
    clip_pad = jnp.concatenate([jnp.full((rim_width,), -1, jnp.int32), clip_ids])
    lag_rows = []
    mask_rows = []
    for lag in range(L):
        begin = rim_width - lag
        lag_rows.append(extended[:, begin : begin + frames])
        source = jnp.arange(frames, dtype=jnp.int32) - lag
        same_clip = clip_pad[begin : begin + frames] == clip_ids
        earlier = clean & (before[5] <= (anchor + source).astype(jnp.float32))
        mask_rows.append(jnp.where(source >= 0, same_clip, earlier))
    valid = jnp.stack(mask_rows).astype(jnp.bfloat16)
    stacked = (jnp.stack(lag_rows, axis=1) * valid[None]).reshape(topics * L, frames)
    recon = jnp.dot(templates, stacked, preferred_element_type=jnp.float32)
    sums_part = (
        jnp.sum(recon, axis=0),
        jnp.sum(spectral, axis=0),
        jnp.sum(spectral * jnp.log(recon), axis=0),
    )
    recon_sum, spec_sum, log_sum = lax.psum((sums_part[0], sums_part[1], sums_part[2]), "freq")
    frame_loss = jnp.log(recon_sum) - log_sum / spec_sum
    scale_factor = F * K / (frames * lax.axis_size("tm"))
    ratio = (
        scale_factor * (1.0 / recon_sum[None, :] - spectral / (spec_sum[None, :] * recon))
    ).astype(jnp.bfloat16)
    template_grad = lax.psum_scatter(
        lax.dot_general(
            stacked, ratio, (((1,), (1,)), ((), ())), preferred_element_type=jnp.float32
        ),
        "tm",
        scatter_dimension=0,
        tiled=True,
    )
    return (frame_loss, template_grad)


def solution(mesh):
    placed = (
        P("freq", "tm"),
        P("freq"),
        P("freq"),
        P("tm"),
        P(None, "freq"),
        P(None, "tm"),
        P(None, None, "tm"),
        P(),
        P("freq", None),
    )
    return jax.shard_map(
        on_device, mesh=mesh, in_specs=placed, out_specs=(P("tm"), P("tm", "freq")), check_vma=False
    )
```

profile of v0, /device:TPU:0, one launch (start us, length us, event | category | flops | bytes accessed | tf_op | source)
XLA Modules:
  0.0 392.4 jit_solution(5322805944889457080)
XLA Ops:
  17.1 3.2 slice.440
  20.2 3.1 slice.439
  23.4 2.3 fusion.127
  29.0 1.7 slice.443
  32.4 1.9 fusion.128
  40.4 1.7 fusion.129
  95.9 1.7 slice.478
  98.3 3.2 slice.480
  115.5 2.3 pad.141
  119.5 1.9 add_multiply_fusion.3
  121.4 2.5 pad.144
  126.5 1.9 add.371
  129.2 2.3 add_multiply_fusion.1
  133.4 2.9 pad.128
  137.0 10.3 %all-gather = f32[2048,1]{0,1:T(1,128)S(1)} all-gather(f32[256,1]{0,1:T(1,128)S(1)} %slice_add_fusion.3), channel_id=2, replica_groups=mesh['tm'=8,'freq'=4] {'tm'}, dimensions={0}, use_global_device_ids=true | all-gather | bytes 9216 | tf_op jit(solution)/shard_map/all_gather | solution.py:13
  152.3 1.8 pad_maximum_fusion.2
  154.1 2.9 pad.145
  156.9 2.9 pad.146
  160.5 8.9 %all-gather.2 = f32[2048,1]{0,1:T(1,128)S(1)} all-gather(f32[256,1]{0,1:T(1,128)S(1)} %slice_add_fusion), channel_id=4, replica_groups=mesh['tm'=8,'freq'=4] {'tm'}, dimensions={0}, use_global_device_ids=true | all-gather | bytes 9216 | tf_op jit(solution)/shard_map/all_gather | solution.py:13
  171.4 13.2 %all-reduce.41 = (f32[8]{0:T(128)S(1)}, f32[8]{0:T(128)S(1)}, f32[8]{0:T(128)S(1)}, f32[8]{0:T(128)S(1)}) all-reduce(f32[8]{0:T(128)S(1)} %get-tuple-element.234, f32[8]{0:T(128)S(1)} %slice_dynamic-update-slice_fusion, f32[8]{0:T(128)S(1)} %dynamic-update-slice.2, f32[8]{0:T(128)S(1)} %dynamic-update-slice.3), channel_id=3, replica_groups=mesh['tm'=8,'freq'=4] {'tm'}, use_global_device_ids=true, to_apply=%add.37 | all-reduce | flops 32 | bytes 256
  185.3 2.9 convolution_bitcast_fusion
  188.3 2.4 fusion.126
  190.6 2.3 copy.87
  196.2 70.3 %all-reduce.45.cloned.1.call-done = f32[256,768]{0,1:T(8,128)} async-done(((f32[256,768]{0,1:T(8,128)}), f32[256,768]{0,1:T(8,128)}) %all-reduce.45.cloned.1.call-update) | async-done | bytes 786448 | tf_op jit(solution)/shard_map/psum | solution.py:112
  266.5 2.8 fusion.124
  270.3 1.8 collective-permute-start
  285.4 7.3 %broadcast_multiply_fusion = bf16[256,16,768]{0,2,1:T(8,128)(2,1)} fusion(bf16[256,16,768]{0,2,1:T(8,128)(2,1)} %fusion.57, bf16[16,768]{1,0:T(8,128)(2,1)S(1)} %convert_element_type.109), kind=kLoop, calls=%fused_computation.8 | loop fusion | flops 3145728 | bytes 12607488 | tf_op jit(solution)/shard_map/mul | solution.py:130
  292.6 9.1 %copy.83 = bf16[256,16,768]{2,1,0:T(8,128)(2,1)} copy(bf16[256,16,768]{0,2,1:T(8,128)(2,1)} %broadcast_multiply_fusion) | data formatting | bytes 12582912 | tf_op jit(solution)/shard_map/mul | solution.py:130
  301.7 5.5 %fusion.136 = (f32[768]{0:T(1024)S(1)}, f32[768,256]{0,1:T(8,128)}) fusion(bf16[256,4096]{1,0:T(8,128)(2,1)S(1)} %copy-done, bf16[4096,768]{1,0:T(8,128)(2,1)} %bitcast.127), kind=kOutput, calls=%fused_computation.277 | convolution fusion | flops 1610808576 | bytes 9178112 | tf_op jit(solution)/shard_map/dot_general | solution.py:131
  308.9 16.8 %all-reduce.42 = (f32[768]{0:T(1024)S(1)}, f32[768]{0:T(1024)S(1)}, f32[768]{0:T(1024)S(1)}) all-reduce(f32[768]{0:T(1024)S(1)} %get-tuple-element.137, f32[768]{0:T(1024)S(1)} %get-tuple-element.136, f32[768]{0:T(1024)S(1)} %get-tuple-element.243), channel_id=1, replica_groups=mesh['tm'=8,'freq'=4] {'freq'}, use_global_device_ids=true, to_apply=%region_10.11 | all-reduce | flops 2304 | bytes 18432 | tf_op jit(solution)/shard_map/psum | solution.py:137
  326.3 6.8 %fusion.11 = f32[4096,256]{1,0:T(8,128)} fusion(bf16[4096,768]{1,0:T(8,128)(2,1)} %bitcast.128, bf16[256,768]{0,1:T(8,128)(2,1)S(1)} %copy.79, f32[768,256]{1,0:T(8,128)S(1)} %copy.84, f32[768]{0:T(1024)S(1)} %get-tuple-element.167, f32[768]{0:T(1024)S(1)} %get-tuple-element.231), kind=kOutput, calls=%fused_computation.44 | convolution fusion | flops 1611792384 | bytes 11671552 | tf_op jit(solution)/shard_map/dot_general | solution.py:144
  333.2 52.4 %reduce-scatter.2.cloned.1.call-done = f32[512,256]{1,0:T(8,128)} async-done(((f32[4096,256]{1,0:T(8,128)}), f32[512,256]{1,0:T(8,128)}) %reduce-scatter.2.cloned.1.call-update) | async-done | bytes 524304 | tf_op jit(solution)/shard_map/reduce_scatter | solution.py:143
  (230 shorter events, 123.4 us)
Async XLA Ops:
  7.2 294.6 %copy-start = (bf16[256,4096]{1,0:T(8,128)(2,1)S(1)}, bf16[256,4096]{1,0:T(8,128)(2,1)}, u32[]{:S(2)}) copy-start(bf16[256,4096]{1,0:T(8,128)(2,1)} %param.19) | copy-start | bytes 6291460
  7.2 259.4 %all-reduce.45.cloned.1.call-start = ((), (), s32[]{:S(2)}) async-start(), calls=%async_computation.1 | async-start | bytes 1572864 | tf_op jit(solution)/shard_map/psum | solution.py:112
  9.7 92.5 %copy-start.1 = (f32[256,768]{0,1:T(8,128)}, f32[256,768]{0,1:T(8,128)S(1)}, u32[]{:S(2)}) copy-start(f32[256,768]{0,1:T(8,128)S(1)} %broadcast_multiply_fusion.1) | copy-start | bytes 2359300
  15.4 86.8 %copy-start.3 = (s32[768]{0:T(1024)S(1)}, s32[768]{0:T(1024)}, u32[]{:S(2)}) copy-start(s32[768]{0:T(1024)} %param.14) | copy-start | bytes 9220
  112.9 18.6 %slice-start = ((f32[256,768]{0,1:T(8,128)}), f32[256,1]{0,1:T(1,128)S(1)}, s32[]{:S(2)}) async-start(f32[256,768]{0,1:T(8,128)} %copy-done.1), calls=%async_computation.3 | async-start | bytes 2048 | tf_op jit(solution)/shard_map/slice | solution.py:84
  119.4 29.1 %copy-start.7 = (u32[32]{0:T(128)S(1)}, u32[32]{0:T(128)}, u32[]{:S(2)}) copy-start(u32[32]{0:T(128)} %constant.225) | copy-start | bytes 388
  119.4 31.5 %copy-start.4 = (pred[767]{0:T(1024)(128)(4,1)S(1)}, pred[767]{0:T(1024)(128)(4,1)}, u32[]{:S(2)}) copy-start(pred[767]{0:T(1024)(128)(4,1)} %get-tuple-element.180) | copy-start | bytes 2305
  119.4 32.8 %slice-start.1 = ((f32[256,768]{0,1:T(8,128)}), f32[256,1]{0,1:T(1,128)S(1)}, s32[]{:S(2)}) async-start(f32[256,768]{0,1:T(8,128)} %convert_multiply_fusion.2), calls=%async_computation.4 | async-start | bytes 2048 | tf_op jit(solution)/shard_map/slice | solution.py:84
  126.5 58.8 %copy-start.6 = (f32[256]{0:T(256)S(1)}, f32[256]{0:T(256)}, u32[]{:S(2)}) copy-start(f32[256]{0:T(256)} %param.13) | copy-start | bytes 3076
  126.5 58.8 %copy-start.2 = (bf16[256,256]{1,0:T(8,128)(2,1)S(1)}, bf16[256,256]{1,0:T(8,128)(2,1)}, u32[]{:S(2)}) copy-start(bf16[256,256]{1,0:T(8,128)(2,1)} %param.15) | copy-start | bytes 393220
  185.3 10.2 %copy-start.5 = (s32[256]{0:T(256)S(1)}, s32[256]{0:T(256)}, u32[]{:S(2)}) copy-start(s32[256]{0:T(256)} %param.18) | copy-start | bytes 3076
  188.2 197.3 %reduce-scatter.2.cloned.1.call-start = ((), (), s32[]{:S(2)}) async-start(), calls=%async_computation.2 | async-start | bytes 4718592 | tf_op jit(solution)/shard_map/reduce_scatter | solution.py:143
  270.3 2.5 collective-permute-start
Sparse Core Ops, SparseCore 0:
  188.4 78.1 all-reduce.44
  333.3 52.2 reduce-scatter.1
where the time goes:
time: 397 us; the launch traced here: 392 us
  waiting for transfers between devices  123 us (31%)
  local copies, waits for them, and re-layouts  119 us (30%)
  other arithmetic  68.1 us (17%)
  blocking collectives  49.2 us (12%)
  between operations  16 us (4%)
  matrix products  15.2 us (4%)
    slice x66, local copies, waits for them, and re-layouts, on_device(): running, summed = lax.associative_scan(compose, (rates, inputs), axis=1)  78 us
    psum x1, waiting for transfers between devices, on_device(): logits = lax.psum(code_part, 'freq')  70.3 us
    reduce_scatter x1, waiting for transfers between devices, on_device(): lax.psum_scatter(lax.dot_general(stacked, ratio, (((1,), (1,)), ((), ()))...  52.4 us
    mul x17, other arithmetic, compose(): return (former[0] * latter[0], latter[0] * former[1] + latter[1])  22 us
    all_gather x2, blocking collectives, prefix(): gathered = jax.tree.map(lambda a: lax.all_gather(a, axis), part)  19.2 us
    pad x34, local copies, waits for them, and re-layouts, on_device(): running, summed = lax.associative_scan(compose, (rates, inputs), axis=1)  17.5 us
    psum x1, blocking collectives, on_device(): lax.psum((sums_part[0], sums_part[1], sums_part[2]), 'freq')  16.8 us
    unnamed x1, blocking collectives  13.2 us
  transfers between devices with their start and end apart: 3, of which 3 were waited for; matrix products, arithmetic and copies ran while one was open for 2% of the time, Pallas kernels for 0%

commit v1 on v0

v1 whole, which is shorter than its diff:
```python
import functools

import jax
import jax.numpy as jnp
from jax import lax
from jax.experimental import pallas as pl
from jax.experimental.pallas import tpu as pltpu
from jax.sharding import PartitionSpec as P

F = 1024
K = 256
L = 16
TOP_CLIP = 5
TAIL = 16
LANES = 128
VMEM = pl.BlockSpec(memory_space=pltpu.VMEM)
SMEM = pl.BlockSpec(memory_space=pltpu.SMEM)
f32 = jnp.float32
bf16 = jnp.bfloat16


def call(kernel, name, outs, scratch, *args, scalars=0, limit=48 << 20):
    return pl.pallas_call(
        kernel,
        name=name,
        out_shape=[jax.ShapeDtypeStruct(shape, dtype) for shape, dtype in outs],
        in_specs=[SMEM] * scalars + [VMEM] * (len(args) - scalars),
        out_specs=[VMEM] * len(outs),
        scratch_shapes=[pltpu.VMEM(shape, dtype) for shape, dtype in scratch],
        compiler_params=pltpu.CompilerParams(vmem_limit_bytes=limit),
    )(*args)


def log_keep(decay):
    gap = 1.0 - (1.0 - decay)
    series = gap * (1.0 / 7.0)
    for order in range(6, 0, -1):
        series = gap * (1.0 / order + series)
    return -series


def column(row, lanes=LANES):
    return jnp.transpose(jnp.broadcast_to(row, (lanes, row.shape[1])))


def wide(col, lanes):
    return jnp.concatenate([col] * (lanes // col.shape[1]), axis=1)


def steps_down(size):
    return (size - 1 - lax.broadcasted_iota(jnp.int32, (size, 1), 0)).astype(f32)


def summary_kernel(nf, place, spectrum, decay, clips, encoder, *refs):
    messages, (own, gains, states, tm_message), (frames_first,) = (
        refs[: nf - 1],
        refs[nf - 1 : nf + 3],
        refs[nf + 3 :],
    )
    bins, frames = spectrum.shape
    piece = frames // nf
    here = place[0, 0]
    clip_row = clips[...].astype(f32)
    clip_col = column(clip_row)
    first = clip_row[:, :1]
    gain = jnp.ones_like(clip_col)
    for value in range(1, TOP_CLIP + 1):
        seen = jnp.max(jnp.where(clip_row == value, 1.0, 0.0), axis=1, keepdims=True)
        counts = (seen > 0.0) & (first < value)
        gain = jnp.where(counts & (clip_col >= value), gain * 0.8, gain)
    frames_first[...] = jnp.transpose(spectrum[...].astype(f32))
    rate = decay[...]
    keep = log_keep(rate)
    scaled = frames_first[...] * wide(1.0 / gain, bins) * rate
    weights = jnp.exp(steps_down(piece) * keep)
    state = jnp.zeros((1, bins), f32)
    states[...] = jnp.zeros_like(states)
    for index in range(nf):
        states[index : index + 1, :] = state
        rows = scaled[index * piece : (index + 1) * piece]
        if index < nf - 1:
            state = jnp.exp(piece * keep) * state + jnp.sum(rows * weights, axis=0, keepdims=True)
    body = piece - TAIL
    state = jnp.exp(body * keep) * state + jnp.sum(
        rows[:body] * weights[TAIL:], axis=0, keepdims=True
    )
    states[nf : nf + 1, :] = state
    state = jnp.exp(TAIL * keep) * state + jnp.sum(
        rows[body:] * weights[body:], axis=0, keepdims=True
    )
    tm_message[0:1, :] = state
    for row in range(frames // bins):
        tm_message[row + 1 : row + 2, :] = clip_row[:, row * bins : (row + 1) * bins]
    for step in range(nf):
        target = own if step == 0 else messages[step - 1]
        start = pl.multiple_of((here ^ step) * piece, piece)
        target[0:piece, :] = frames_first[pl.ds(start, piece), :].astype(bf16)
        target[piece : piece + TAIL, :] = frames_first[frames - TAIL :, :].astype(bf16)
        if step:
            target[piece + TAIL :, :] = encoder[...]
    start = pl.multiple_of(here * piece, piece)
    frames_first[:, 0:LANES] = gain
    gains[0:piece, :] = frames_first[pl.ds(start, piece), 0:LANES]
    gains[piece:, :] = gain[frames - TAIL :]


def totals_kernel(templates, spectrum, stats):
    bins, frames = spectrum.shape
    stats[...] = jnp.zeros_like(stats)
    columns = templates.shape[1]
    for row in range(columns // bins):
        part = templates[:, row * bins : (row + 1) * bins].astype(f32)
        stats[row : row + 1, :] = jnp.sum(part, axis=0, keepdims=True)
    for row in range(frames // bins):
        part = spectrum[:, row * bins : (row + 1) * bins].astype(f32)
        at = columns // bins + row
        stats[at : at + 1, :] = jnp.sum(part, axis=0, keepdims=True)


def entry_kernel(nt, nf, place, decay, init, states, stats, *refs):
    pairs, messages, (own, clips_wide), (blocks, gains) = (
        refs[: nt // 2],
        refs[nt // 2 : nt // 2 + nf - 1],
        refs[nt // 2 + nf - 1 : nt // 2 + nf + 1],
        refs[nt // 2 + nf + 1 :],
    )
    bins = decay.shape[1]
    height = blocks.shape[1]
    frames = (height - 1) * bins
    piece = frames // nf
    here, lap = place[0, 0], place[0, 1]
    for index, pair in enumerate(pairs):
        blocks[2 * index] = pair[0:height]
        blocks[2 * index + 1] = pair[height:]
    ids = blocks[:, 1:, :]
    kinds = jnp.zeros((nt, 1, 1), f32)
    for value in range(TOP_CLIP + 1):
        kinds += jnp.max(jnp.where(ids == value, 1.0, 0.0), axis=(1, 2), keepdims=True)
    gain = jnp.ones_like(kinds)
    for value in range(2, TOP_CLIP + 2):
        gain = jnp.where(kinds >= value, gain * 0.8, gain)
    gains[...] = jnp.broadcast_to(gain, gains.shape)
    keep = log_keep(decay[...])
    through = jnp.exp(frames * keep)
    state = init[...]
    for block in range(nt - 1):
        at, after = block ^ lap, (block + 1) ^ lap
        last = blocks[at, height - 1 : height, bins - 1 : bins]
        first = blocks[after, 1:2, 0:1]
        joint = jnp.where(first != last, 0.8, 1.0)
        passed = joint * (gains[at] * (through * state + blocks[at, 0:1, :]))
        state = jnp.where(block < lap, passed, state)
    tail = jnp.exp((frames - TAIL) * keep) * state + states[nf : nf + 1, :]
    for step in range(nf):
        target = own if step == 0 else messages[step - 1]
        other = here ^ step
        power = jnp.exp((other * piece).astype(f32) * keep)
        target[...] = jnp.zeros_like(target)
        target[0:1, :] = power * state + states[pl.ds(other, 1), :]
        target[1:2, :] = tail
        target[2:3, :] = decay[...]
        if step:
            target[8:, :] = stats[...]
    previous = blocks[jnp.maximum(lap - 1, 0) ^ lap, height - 1 : height, bins - LANES : bins]
    clips_wide[:, 0:LANES] = jnp.where(lap > 0, previous, -1.0)
    for row in range(frames // bins):
        low = LANES + row * bins
        clips_wide[:, low : low + bins] = blocks[0, row + 1 : row + 2, :]


def noise_kernel(nf, place, gauss, uniform, boost, normal, first, second, boosts):
    topics, frames = gauss.shape
    piece = frames // nf
    here = place[0, 0]
    width = normal.shape[1]
    counts = wide(column(boost[...].astype(f32)), width)
    boosts[...] = counts
    normal[...] = jnp.zeros_like(normal)
    first[...] = jnp.ones_like(first)
    second[...] = jnp.ones_like(second)
    pairs = ((gauss, normal), (uniform.at[0], first), (uniform.at[1], second))
    for index in range(nf):

        @pl.when(here == index)
        def _():
            for source, target in pairs:
                target[:, 0:piece] = source[:, index * piece : (index + 1) * piece]

    for source, target in pairs:
        target[:, piece : piece + TAIL] = source[:, frames - TAIL :]
    first[...] = jnp.log(first[...])
    second[...] = jnp.where(counts >= 2.0, jnp.log(second[...]), 0.0)


def sampler_kernel(nf, own, encoder, own_state, gains, normal, first, second, boosts, *refs):
    messages, arrivals, (packed, tail), scratch = (
        refs[: nf - 1],
        refs[nf - 1 : 2 * nf - 2],
        refs[2 * nf - 2 : 2 * nf],
        refs[2 * nf :],
    )
    inputs, running, normed = scratch
    rows, bins = own.shape
    piece = rows - TAIL
    segment = piece // 8
    topics, width = normal.shape
    gain = gains[...]
    inverse = 1.0 / gain
    powers = (1 + lax.broadcasted_iota(jnp.int32, (segment, 1), 0)).astype(f32)
    logits = jnp.zeros((topics, width), f32)
    normed[...] = jnp.zeros_like(normed)
    for step in range(nf):
        state = own_state if step == 0 else arrivals[step - 1]
        block = own if step == 0 else messages[step - 1]
        weights = encoder[...] if step == 0 else messages[step - 1][rows:, :]
        for part in range(bins // LANES):
            at = step * (bins // LANES) + part
            lanes = slice(part * LANES, (part + 1) * LANES)
            spectral = block[0:rows, lanes].astype(f32)
            rate = state[2:3, lanes]
            keep = log_keep(rate)
            fade = 1.0 - rate
            inputs[at] = spectral * inverse * rate
            total = jnp.zeros((8, LANES), f32)
            for row in range(segment):
                total = fade * total + inputs[at, pl.ds(row, 8, stride=segment), :]
                running[at, pl.ds(row, 8, stride=segment), :] = total
            carry = state[0:1, lanes]
            through = jnp.exp(segment * keep)
            fading = jnp.exp(powers * keep)
            for index in range(8):
                low = index * segment
                running[at, low : low + segment, :] += fading * carry
                carry = through * carry + total[index : index + 1, :]
            carry = state[1:2, lanes]
            for row in range(piece, rows):
                carry = fade * carry + inputs[at, row : row + 1, :]
                running[at, row : row + 1, :] = carry
            smooth = running[at] * gain
            normed[step, 0:rows, lanes] = (spectral * lax.rsqrt(smooth + 0.1)).astype(bf16)
        logits += lax.dot_general(
            weights, normed[step], (((1,), (1,)), ((), ())), preferred_element_type=f32
        )
    concentration = jnp.maximum(logits, 0.0) + jnp.log1p(jnp.exp(-jnp.abs(logits))) + 0.5
    offset = concentration + boosts[...] - 1.0 / 3.0
    linear = 1.0 + lax.rsqrt(9.0 * offset) * normal[...]
    draw = offset * linear * linear * linear
    draw = draw * jnp.exp(first[...] / concentration + second[...] / (concentration + 1.0))
    proportions = draw / jnp.sum(draw, axis=0, keepdims=True)
    full, rest = piece // LANES, piece % LANES
    for index in range(full):
        tile = proportions[:, index * LANES : (index + 1) * LANES]
        packed[index * topics : (index + 1) * topics, :] = tile.astype(bf16)
    tile = proportions[:, full * LANES : (full + 1) * LANES]
    if rest:
        half = topics // 2
        lane = lax.broadcasted_iota(jnp.int32, (half, LANES), 1)
        joined = jnp.where(lane < rest, tile[:half], pltpu.roll(tile[half:], rest, 1))
        packed[full * topics :, :] = joined.astype(bf16)
    tail[...] = pltpu.roll(tile, LANES - TAIL - rest, 1).astype(bf16)


def gradient_kernel(nt, nf, place, own, rim, clips, templates, spectrum, stats, *refs):
    messages, arrivals, (away, kept, sums), scratch = (
        refs[: nf - 1],
        refs[nf - 1 : 2 * nf - 2],
        refs[2 * nf - 2 : 2 * nf + 1],
        refs[2 * nf + 1 :],
    )
    extended, heads, stacked, valid, recon, ratio = scratch
    bins, frames = spectrum.shape
    here, lap = place[0, 0], place[0, 1]
    piece = frames // nf
    topics = extended.shape[0]
    tile = stacked.shape[1]
    full, rest = piece // LANES, piece % LANES
    extended[:, 0:LANES] = rim[...].astype(f32)
    for step in range(nf):
        source = own if step == 0 else messages[step - 1]
        for index in range(nf):

            @pl.when((here ^ step) == index)
            def _():
                low = LANES + index * piece
                for part in range(full):
                    values = source[part * topics : (part + 1) * topics, :].astype(f32)
                    extended[:, low + part * LANES : low + (part + 1) * LANES] = values
                if rest:
                    values = source[full * topics :, :].astype(f32)
                    low += full * LANES
                    half = topics // 2
                    extended[0:half, low : low + rest] = values[:, 0:rest]
                    extended[half:, low : low + rest] = values[:, rest:]

    total = stats[...]
    for arrival in arrivals:
        total = total + arrival[8:, :]
    columns = templates.shape[1]
    wide_rows = columns // bins
    heads[...] = jnp.zeros_like(heads)
    for row in range(wide_rows):
        value = total[row : row + 1, :]
        for index in range(3):
            rounded = value.astype(bf16)
            heads[index : index + 1, row * bins : (row + 1) * bins] = rounded
            value = value - rounded.astype(f32)
    for row in range(frames // bins):
        at = wide_rows + row
        sums[2:3, row * bins : (row + 1) * bins] = total[at : at + 1, :]
    scale = F * K / (frames * nt)
    group = 32
    for start in range(0, frames, tile):
        span = slice(start, start + LANES + tile)
        ids = jnp.broadcast_to(clips[:, span], (L, LANES + tile))
        shifted = pltpu.roll(ids, 0, 1, stride=1, stride_axis=0)
        valid[...] = jnp.where(shifted == ids, 1.0, 0.0)[:, LANES:]
        for low in range(0, topics, group):

            def one(index, _):
                topic = low + index
                row = extended[pl.ds(topic, 1), span]
                lagged = pltpu.roll(
                    jnp.broadcast_to(row, (L, LANES + tile)), 0, 1, stride=1, stride_axis=0
                )
                at = pl.multiple_of(topic * L, L)
                stacked[pl.ds(at, L), :] = (lagged[:, LANES:] * valid[...]).astype(bf16)
                return 0

            lax.fori_loop(0, group, one, 0, unroll=4)
            part = slice(low * L, (low + group) * L)
            left = jnp.concatenate([templates[:, part], heads[:, part]], axis=0)
            product = jnp.dot(left, stacked[part, :], preferred_element_type=f32)
            if low == 0:
                recon[...] = product
            else:
                recon[...] += product
        here_frames = slice(start, start + tile)
        rebuilt = recon[0:bins, :]
        recon_sum = recon[bins : bins + 1] + recon[bins + 1 : bins + 2] + recon[bins + 2 : bins + 3]
        spectral = spectrum[:, here_frames].astype(f32)
        spec_sum = sums[2:3, here_frames]
        sums[0:1, here_frames] = recon_sum
        sums[1:2, here_frames] = jnp.sum(spectral * jnp.log(rebuilt), axis=0, keepdims=True)
        ratio[...] = (scale * (1.0 / recon_sum - spectral / (spec_sum * rebuilt))).astype(bf16)
        height = away.shape[1]
        for target, side in ((away, 1), (kept, 0)):
            for step in range(nt // 2):
                owner = lap ^ (2 * step + side)
                at = pl.multiple_of(owner * height, height)
                product = lax.dot_general(
                    stacked[pl.ds(at, height), :],
                    ratio[...],
                    (((1,), (1,)), ((), ())),
                    preferred_element_type=f32,
                )
                if start == 0:
                    target[step] = product
                else:
                    target[step] += product


def exchanged(value, axis, step):
    size = lax.axis_size(axis)
    return lax.ppermute(value, axis, [(index, index ^ step) for index in range(size)])


def on_device(
    spectrum,
    decay_rate,
    init_state,
    clip_ids,
    encoder,
    gauss_noise,
    uniform_noise,
    boost_count,
    templates,
):
    nt, nf = lax.axis_size("tm"), lax.axis_size("freq")
    bins, frames = spectrum.shape
    topics = encoder.shape[0]
    columns = templates.shape[1]
    piece = frames // nf
    rows = piece + TAIL
    width = -(-rows // LANES) * LANES
    place = jnp.stack([lax.axis_index("freq"), lax.axis_index("tm")]).astype(jnp.int32)[None]
    decay = decay_rate[None]
    state_rows = -(-(nf + 1) // 8) * 8
    height = 1 + frames // bins

    *messages, own, gains, states, tm_message = call(
        functools.partial(summary_kernel, nf),
        "summary",
        [((rows + topics, bins), bf16)] * (nf - 1)
        + [
            ((rows, bins), bf16),
            ((rows, LANES), f32),
            ((state_rows, bins), f32),
            ((height, bins), f32),
        ],
        [((frames, bins), f32)],
        place,
        spectrum,
        decay,
        clip_ids[None],
        encoder,
        scalars=1,
    )
    messages = [exchanged(messages[step - 1], "freq", step) for step in range(1, nf)]
    pair = jnp.concatenate([tm_message, exchanged(tm_message, "tm", 1)], axis=0)
    pairs = [pair] + [exchanged(pair, "tm", step) for step in range(2, nt, 2)]
    stat_rows = -(-(columns // bins + frames // bins) // 8) * 8
    (stats,) = call(
        totals_kernel, "totals", [((stat_rows, bins), f32)], [], templates, spectrum
    )
    *arrivals, own_state, clips_wide = call(
        functools.partial(entry_kernel, nt, nf),
        "entry",
        [((8 + stat_rows, bins), f32)] * (nf - 1)
        + [((8, bins), f32), ((1, LANES + frames), f32)],
        [((nt, height, bins), f32), ((nt, 1, bins), f32)],
        place,
        decay,
        init_state[None],
        states,
        stats,
        *pairs,
        scalars=1,
    )
    arrivals = [exchanged(arrivals[step - 1], "freq", step) for step in range(1, nf)]
    noises = call(
        functools.partial(noise_kernel, nf),
        "noise",
        [((topics, width), f32)] * 4,
        [],
        place,
        gauss_noise,
        uniform_noise,
        boost_count[None],
        scalars=1,
    )
    packed, tail = call(
        functools.partial(sampler_kernel, nf),
        "sampler",
        [((topics * piece // LANES, LANES), bf16), ((topics, LANES), bf16)],
        [((nf * bins // LANES, rows, LANES), f32)] * 2 + [((nf, width, bins), bf16)],
        own,
        encoder,
        own_state,
        gains,
        *noises,
        *messages,
        *arrivals,
    )
    shares = [exchanged(packed, "freq", step) for step in range(1, nf)]
    rim = lax.ppermute(tail, "tm", [(index, index + 1) for index in range(nt - 1)])
    tile = 768 if frames % 768 == 0 else frames
    height = columns // nt
    away, kept, sums = call(
        functools.partial(gradient_kernel, nt, nf),
        "gradient",
        [((nt // 2, height, bins), f32)] * 2 + [((8, frames), f32)],
        [
            ((topics, LANES + frames), f32),
            ((16, columns), bf16),
            ((columns, tile), bf16),
            ((L, tile), f32),
            ((bins + 16, tile), f32),
            ((bins, tile), bf16),
        ],
        place,
        packed,
        rim,
        clips_wide,
        templates,
        spectrum,
        stats,
        *shares,
        *arrivals,
        scalars=1,
    )
    both = kept + exchanged(away, "tm", 1)
    parts = [exchanged(both[step], "tm", 2 * step) for step in range(1, nt // 2)]
    log_part = sums[1]
    log_sum = log_part + sum(exchanged(log_part, "freq", step) for step in range(1, nf))
    frame_loss = jnp.log(sums[0]) - log_sum / sums[2]
    return (frame_loss, both[0] + sum(parts))


def solution(mesh):
    placed = (
        P("freq", "tm"),
        P("freq"),
        P("freq"),
        P("tm"),
        P(None, "freq"),
        P(None, "tm"),
        P(None, None, "tm"),
        P(),
        P("freq", None),
    )
    return jax.shard_map(
        on_device, mesh=mesh, in_specs=placed, out_specs=(P("tm"), P("tm", "freq")), check_vma=False
    )
```

time: 397 us -> 94.6 us (0.24); the launches traced: 392 us -> 94.3 us
  local copies, waits for them, and re-layouts: 119 us -> 6.03 us
  waiting for transfers between devices: 123 us -> 35.4 us
  other arithmetic: 68.1 us -> 2.01 us
  blocking collectives: 49.2 us -> 0 us
  starting transfers between devices: 1.9 us -> 29.7 us
  Pallas kernels: 0 us -> 20.3 us
  between operations: 16 us -> 0.79 us
  matrix products: 15.2 us -> 0 us
    slice x70 -> x1, local copies, waits for them, and re-layouts: 81.5 us -> 0.03 us  [on_device(): log_part = sums[1]]
    psum x1 -> x0, waiting for transfers between devices: 70.3 us -> none  [on_device(): logits = lax.psum(code_part, 'freq')]
    reduce_scatter x1 -> x0, waiting for transfers between devices: 52.4 us -> none  [on_device(): lax.psum_scatter(lax.dot_general(stacked, ratio, (((1,), (1,)), ((), ()))...]
    ppermute x1 -> x21, waiting for transfers between devices: 0.16 us -> 35.4 us  [the longest x20 34.5 us: exchanged(): lax.ppermute(value, axis, [(index, index ^ step) for index in range(size)])]
    mul x21 -> x0, other arithmetic: 31 us -> none  [the longest x17 22 us: compose(): return (former[0] * latter[0], latter[0] * former[1] + latter[1])]
    ppermute x1 -> x21, starting transfers between devices: 1.83 us -> 29.7 us  [the longest x20 28.5 us: exchanged(): lax.ppermute(value, axis, [(index, index ^ step) for index in range(size)])]
    pallas_call x0 -> x6, Pallas kernels: none -> 20.3 us  [call(): pl.pallas_call(kernel, name=name, out_shape=[jax.ShapeDtypeStruct(shape,...]
    all_gather x2 -> x0, blocking collectives: 19.2 us -> none  [prefix(): gathered = jax.tree.map(lambda a: lax.all_gather(a, axis), part)]
  transfers between devices with their start and end apart: 3 -> 21, of which waited for: 3 -> 13; matrix products, arithmetic and copies ran while one was open for 2% -> 1% of each run, Pallas kernels for 0% -> 2%
where the time goes in v1:
time: 94.6 us; the launch traced here: 94.3 us
  waiting for transfers between devices  35.4 us (37%)
  starting transfers between devices  29.7 us (31%)
  Pallas kernels  20.3 us (21%)
  local copies, waits for them, and re-layouts  6.03 us (6%)
  other arithmetic  2.01 us (2%)
    ppermute x20, waiting for transfers between devices, exchanged(): lax.ppermute(value, axis, [(index, index ^ step) for index in range(size)])  34.5 us
    ppermute x20, starting transfers between devices, exchanged(): lax.ppermute(value, axis, [(index, index ^ step) for index in range(size)])  28.5 us
    pallas_call x6, Pallas kernels, call(): pl.pallas_call(kernel, name=name, out_shape=[jax.ShapeDtypeStruct(shape,...  20.3 us
    unnamed x24, local copies, waits for them, and re-layouts  5.19 us
  transfers between devices with their start and end apart: 21, of which 13 were waited for; matrix products, arithmetic and copies ran while one was open for 1% of the time, Pallas kernels for 2%

profile of v1, /device:TPU:0, one launch (start us, length us, event | category | flops | bytes accessed | tf_op | source)
XLA Modules:
  0.0 94.3 jit_solution(10914315971677910754)
XLA Ops:
  1.4 1.0 %copy-done.1 = bf16[256,768]{1,0:T(8,128)(2,1)S(1)} copy-done((bf16[256,768]{1,0:T(8,128)(2,1)S(1)}, bf16[256,768]{1,0:T(8,128)(2,1)}, u32[]{:S(2)}) %copy-start.1) | copy-done | bytes 393240
  2.4 0.9 copy-done.6
  4.0 1.2 %summary.1 = (bf16[464,256]{1,0:T(8,128)(2,1)S(1)}, bf16[464,256]{1,0:T(8,128)(2,1)S(1)}, bf16[464,256]{1,0:T(8,128)(2,1)S(1)}, bf16[208,256]{1,0:T(8,128)(2,1)S...) custom-call(s32[1,2]{1,0:T(1,128)S(1)} %add_bitcast_fusion.place, ...), custom_call_target="tpu_custom_call" | custom-call | tf_op jit(solution)/shard_map/summary/pallas_call | solution.py:23
  5.2 3.1 %collective-permute-start.4 = (bf16[464,256]{1,0:T(8,128)(2,1)S(1)}, bf16[464,256]{1,0:T(8,128)(2,1)S(1)}, u32[]{:S(2)}, u32[]{:S(2)}) collective-permute-start(bf16[464,256]{1,0:T(8,128)(2,1)S(1)} %get-tuple-element.32), channel_id=1, source_target_pairs={{0,1},{1,0},{2,3},{3,2},{4,5},{5,4},{6,7},{7,6},{8,9},{9,8},{10,11... | collective-permute-start | bytes 712712 | tf_op jit(solution)/shard_map/ppermute | solution.py:364
  8.3 2.6 %collective-permute-start.5 = (bf16[464,256]{1,0:T(8,128)(2,1)S(1)}, bf16[464,256]{1,0:T(8,128)(2,1)S(1)}, u32[]{:S(2)}, u32[]{:S(2)}) collective-permute-start(bf16[464,256]{1,0:T(8,128)(2,1)S(1)} %get-tuple-element.33), channel_id=1, source_target_pairs={{0,2},{1,3},{2,0},{3,1},{4,6},{5,7},{6,4},{7,5},{8,10},{9,11},{10,... | collective-permute-start | bytes 712712 | tf_op jit(solution)/shard_map/ppermute | solution.py:364
  10.9 1.2 %collective-permute-done = f32[4,256]{1,0:T(4,128)S(1)} collective-permute-done((f32[4,256]{1,0:T(4,128)S(1)}, f32[4,256]{1,0:T(4,128)S(1)}, u32[]{:S(2)}, u32[]{:S(2)}) %collective-permute-start) | collective-permute-done | bytes 4128 | tf_op jit(solution)/shard_map/ppermute | solution.py:364
  12.1 2.7 %collective-permute-start.3 = (f32[8,256]{1,0:T(8,128)S(1)}, f32[8,256]{1,0:T(8,128)S(1)}, u32[]{:S(2)}, u32[]{:S(2)}) collective-permute-start(f32[8,256]{1,0:T(8,128)S(1)} %pad_maximum_fusion.refs_0_), channel_id=1, source_target_pairs={{0,24},{4,28},{8,16},{12,20},{16,8},{20,12},{24,0},{28,4},{1,25},{... | collective-permute-start | bytes 24584 | tf_op jit(solution)/shard_map/ppermute | solution.py:364
  15.3 1.4 %collective-permute-done.3.refs_3_ = f32[8,256]{1,0:T(8,128)S(1)} collective-permute-done((f32[8,256]{1,0:T(8,128)S(1)}, f32[8,256]{1,0:T(8,128)S(1)}, u32[]{:S(2)}, u32[]{:S(2)}) %collective-permute-start.3) | collective-permute-done | bytes 8224 | tf_op jit(solution)/shard_map/ppermute | solution.py:364
  16.7 1.7 %collective-permute-start.1 = (f32[8,256]{1,0:T(8,128)S(1)}, f32[8,256]{1,0:T(8,128)S(1)}, u32[]{:S(2)}, u32[]{:S(2)}) collective-permute-start(f32[8,256]{1,0:T(8,128)S(1)} %pad_maximum_fusion.refs_0_), channel_id=1, source_target_pairs={{0,8},{4,12},{8,0},{12,4},{16,24},{20,28},{24,16},{28,20},{1,9},{5... | collective-permute-start | bytes 24584 | tf_op jit(solution)/shard_map/ppermute | solution.py:364
  18.4 1.6 %copy-done = bf16[256,4096]{1,0:T(8,128)(2,1)S(1)} copy-done((bf16[256,4096]{1,0:T(8,128)(2,1)S(1)}, bf16[256,4096]{1,0:T(8,128)(2,1)}, u32[]{:S(2)}) %copy-start) | copy-done | bytes 2097176
  20.0 1.0 %copy-done.2 = bf16[256,768]{1,0:T(8,128)(2,1)S(1)} copy-done((bf16[256,768]{1,0:T(8,128)(2,1)S(1)}, bf16[256,768]{1,0:T(8,128)(2,1)}, u32[]{:S(2)}) %copy-start.2) | copy-done | bytes 393240
  23.0 3.5 %collective-permute-start.8 = (f32[32,256]{1,0:T(8,128)S(1)}, f32[32,256]{1,0:T(8,128)S(1)}, u32[]{:S(2)}, u32[]{:S(2)}) collective-permute-start(f32[32,256]{1,0:T(8,128)S(1)} %get-tuple-element.36), channel_id=1, source_target_pairs={{0,2},{1,3},{2,0},{3,1},{4,6},{5,7},{6,4},{7,5},{8,10},{9,11},{10,... | collective-permute-start | bytes 98312 | tf_op jit(solution)/shard_map/ppermute | solution.py:364
  26.4 1.2 %collective-permute-done.7.refs_3_ = f32[32,256]{1,0:T(8,128)S(1)} collective-permute-done((f32[32,256]{1,0:T(8,128)S(1)}, f32[32,256]{1,0:T(8,128)S(1)}, u32[]{:S(2)}, u32[]{:S(2)}) %collective-permute-start.7) | collective-permute-done | bytes 32800 | tf_op jit(solution)/shard_map/ppermute | solution.py:364
  27.6 2.3 %collective-permute-start.9 = (f32[32,256]{1,0:T(8,128)S(1)}, f32[32,256]{1,0:T(8,128)S(1)}, u32[]{:S(2)}, u32[]{:S(2)}) collective-permute-start(f32[32,256]{1,0:T(8,128)S(1)} %get-tuple-element.37), channel_id=1, source_target_pairs={{0,3},{1,2},{2,1},{3,0},{4,7},{5,6},{6,5},{7,4},{8,11},{9,10},{10,... | collective-permute-start | bytes 98312 | tf_op jit(solution)/shard_map/ppermute | solution.py:364
  30.8 3.5 %collective-permute-done.8.refs_4_ = f32[32,256]{1,0:T(8,128)S(1)} collective-permute-done((f32[32,256]{1,0:T(8,128)S(1)}, f32[32,256]{1,0:T(8,128)S(1)}, u32[]{:S(2)}, u32[]{:S(2)}) %collective-permute-start.8) | collective-permute-done | bytes 32800 | tf_op jit(solution)/shard_map/ppermute | solution.py:364
  34.3 1.3 %sampler.1 = (bf16[384,128]{1,0:T(8,128)(2,1)S(1)}, bf16[256,128]{1,0:T(8,128)(2,1)S(1)}) custom-call(bf16[208,256]{1,0:T(8,128)(2,1)S(1)} %get-tuple-element.23.own, bf16[256,256]{1,0:T(8,128)(2,1)S(1)} %copy-done.7, f32[8,256]{1,0:T(8,128)S(1)} %get-tuple-element.26.own_state, f32[208,128]{1,0:T(8,128)S(1)} %get-tuple-element.27.gains, ...), custom_call_target="tpu_custom_call" | custom-call | tf_op jit(solution)/shard_map/sampler/pallas_call | solution.py:23
  35.7 2.5 %collective-permute-start.13 = (bf16[384,128]{1,0:T(8,128)(2,1)S(1)}, bf16[384,128]{1,0:T(8,128)(2,1)S(1)}, u32[]{:S(2)}, u32[]{:S(2)}) collective-permute-start(bf16[384,128]{1,0:T(8,128)(2,1)S(1)} %get-tuple-element.38.own), channel_id=1, source_target_pairs={{0,3},{1,2},{2,1},{3,0},{4,7},{5,6},{6,5},{7,4},{8,11},{9,10},{10,... | collective-permute-start | bytes 294920 | tf_op jit(solution)/shard_map/ppermute | solution.py:364
  38.2 2.0 %collective-permute-start.11 = (bf16[384,128]{1,0:T(8,128)(2,1)S(1)}, bf16[384,128]{1,0:T(8,128)(2,1)S(1)}, u32[]{:S(2)}, u32[]{:S(2)}) collective-permute-start(bf16[384,128]{1,0:T(8,128)(2,1)S(1)} %get-tuple-element.38.own), channel_id=1, source_target_pairs={{0,1},{1,0},{2,3},{3,2},{4,5},{5,4},{6,7},{7,6},{8,9},{9,8},{10,11... | collective-permute-start | bytes 294920 | tf_op jit(solution)/shard_map/ppermute | solution.py:364
  40.1 1.3 %collective-permute-start.10 = (bf16[256,128]{1,0:T(8,128)(2,1)S(1)}, bf16[256,128]{1,0:T(8,128)(2,1)S(1)}, u32[]{:S(2)}, u32[]{:S(2)}) collective-permute-start(bf16[256,128]{1,0:T(8,128)(2,1)S(1)} %get-tuple-element.39), channel_id=1, source_target_pairs={{0,4},{4,8},{8,12},{12,16},{16,20},{20,24},{24,28},{1,5},{5,9},{9,... | collective-permute-start | bytes 196616 | tf_op jit(solution)/shard_map/ppermute | solution.py:455
  41.4 0.9 collective-permute-done.10.rim
  42.4 3.0 %collective-permute-done.12.refs_1_ = bf16[384,128]{1,0:T(8,128)(2,1)S(1)} collective-permute-done((bf16[384,128]{1,0:T(8,128)(2,1)S(1)}, bf16[384,128]{1,0:T(8,128)(2,1)S(1)}, u32[]{:S(2)}, u32[]{:S(2)}) %collective-permute-start.12) | collective-permute-done | bytes 98336 | tf_op jit(solution)/shard_map/ppermute | solution.py:364
  45.4 15.6 %gradient.1 = (f32[4,512,256]{2,1,0:T(8,128)S(1)}, f32[4,512,256]{2,1,0:T(8,128)S(1)}, f32[8,768]{1,0:T(8,128)S(1)}) custom-call(s32[1,2]{1,0:T(1,128)S(1)} %add_bitcast_fusion.place, bf16[384,128]{1,0:T(8,128)(2,1)S(1)} %get-tuple-element.38.own, bf16[256,128]{1,0:T(8,128)(2,1)S(1)} %collective-permute-done.10.rim, f32[1,896]{1,0:T(1,128)S(1)} %get-tuple-element.40.clips, ...), custom_call_target="tpu_custom_call" | custom-call | tf_op jit(solution)/shard_map/gradient/pallas_call | solution.py:23
  61.2 4.1 %collective-permute-done.17 = f32[4,512,256]{2,1,0:T(8,128)S(1)} collective-permute-done((f32[4,512,256]{2,1,0:T(8,128)S(1)}, f32[4,512,256]{2,1,0:T(8,128)S(1)}, u32[]{:S(2)}, u32[]{:S(2)}) %collective-permute-start.17) | collective-permute-done | bytes 2097184 | tf_op jit(solution)/shard_map/ppermute | solution.py:364
  65.8 2.8 %collective-permute-start.19 = (f32[512,256]{1,0:T(8,128)S(1)}, f32[512,256]{1,0:T(8,128)S(1)}, u32[]{:S(2)}, u32[]{:S(2)}) collective-permute-start(f32[512,256]{1,0:T(8,128)S(1)} %get-tuple-element.47), channel_id=1, source_target_pairs={{0,16},{4,20},{8,24},{12,28},{16,0},{20,4},{24,8},{28,12},{1,17},{... | collective-permute-start | bytes 1572872 | tf_op jit(solution)/shard_map/ppermute | solution.py:364
  69.2 0.9 collective-permute-start.18
  70.2 2.5 %collective-permute-start.16 = (f32[768]{0:T(1024)S(1)}, f32[768]{0:T(1024)S(1)}, u32[]{:S(2)}, u32[]{:S(2)}) collective-permute-start(f32[768]{0:T(1024)S(1)} %get-tuple-element.44), channel_id=1, source_target_pairs={{0,3},{1,2},{2,1},{3,0},{4,7},{5,6},{6,5},{7,4},{8,11},{9,10},{10,... | collective-permute-start | bytes 9224 | tf_op jit(solution)/shard_map/ppermute | solution.py:364
  72.7 3.0 %collective-permute-done.16 = f32[768]{0:T(1024)S(1)} collective-permute-done((f32[768]{0:T(1024)S(1)}, f32[768]{0:T(1024)S(1)}, u32[]{:S(2)}, u32[]{:S(2)}) %collective-permute-start.16) | collective-permute-done | bytes 3104 | tf_op jit(solution)/shard_map/ppermute | solution.py:364
  75.6 1.5 %collective-permute-done.15 = f32[768]{0:T(1024)S(1)} collective-permute-done((f32[768]{0:T(1024)S(1)}, f32[768]{0:T(1024)S(1)}, u32[]{:S(2)}, u32[]{:S(2)}) %collective-permute-start.15) | collective-permute-done | bytes 3104 | tf_op jit(solution)/shard_map/ppermute | solution.py:364
  77.2 2.1 %collective-permute-done.14 = f32[768]{0:T(1024)S(1)} collective-permute-done((f32[768]{0:T(1024)S(1)}, f32[768]{0:T(1024)S(1)}, u32[]{:S(2)}, u32[]{:S(2)}) %collective-permute-start.14) | collective-permute-done | bytes 3104 | tf_op jit(solution)/shard_map/ppermute | solution.py:364
  79.8 12.2 %collective-permute-done.19 = f32[512,256]{1,0:T(8,128)S(1)} collective-permute-done((f32[512,256]{1,0:T(8,128)S(1)}, f32[512,256]{1,0:T(8,128)S(1)}, u32[]{:S(2)}, u32[]{:S(2)}) %collective-permute-start.19) | collective-permute-done | bytes 524320 | tf_op jit(solution)/shard_map/ppermute | solution.py:364
  92.0 1.3 %collective-permute-done.18 = f32[512,256]{1,0:T(8,128)S(1)} collective-permute-done((f32[512,256]{1,0:T(8,128)S(1)}, f32[512,256]{1,0:T(8,128)S(1)}, u32[]{:S(2)}, u32[]{:S(2)}) %collective-permute-start.18) | collective-permute-done | bytes 524320 | tf_op jit(solution)/shard_map/ppermute | solution.py:364
  93.3 0.9 fusion
  (48 shorter events, 6.8 us)
Async XLA Ops:
  0.6 20.7 %copy-start.9 = (f32[256]{0:T(256)S(1)}, f32[256]{0:T(256)}, u32[]{:S(2)}) copy-start(f32[256]{0:T(256)} %param.10) | copy-start | bytes 3076
  0.6 20.7 %copy-start.10 = (f32[256]{0:T(256)S(1)}, f32[256]{0:T(256)}, u32[]{:S(2)}) copy-start(f32[256]{0:T(256)} %param.11) | copy-start | bytes 3076
  0.7 29.3 %copy-start.11 = (s32[256]{0:T(256)S(1)}, s32[256]{0:T(256)}, u32[]{:S(2)}) copy-start(s32[256]{0:T(256)} %param.16) | copy-start | bytes 3076
  1.4 1.0 %copy-start.1 = (bf16[256,768]{1,0:T(8,128)(2,1)S(1)}, bf16[256,768]{1,0:T(8,128)(2,1)}, u32[]{:S(2)}) copy-start(bf16[256,768]{1,0:T(8,128)(2,1)} %spectrum.5) | copy-start | bytes 1179652
  2.4 0.9 copy-start.6
  5.2 29.1 %collective-permute-start.4 = (bf16[464,256]{1,0:T(8,128)(2,1)S(1)}, bf16[464,256]{1,0:T(8,128)(2,1)S(1)}, u32[]{:S(2)}, u32[]{:S(2)}) collective-permute-start(bf16[464,256]{1,0:T(8,128)(2,1)S(1)} %get-tuple-element.32), channel_id=1, source_target_pairs={{0,1},{1,0},{2,3},{3,2},{4,5},{5,4},{6,7},{7,6},{8,9},{9,8},{10,11... | collective-permute-start | bytes 712712 | tf_op jit(solution)/shard_map/ppermute | solution.py:364
  8.3 26.0 %collective-permute-start.5 = (bf16[464,256]{1,0:T(8,128)(2,1)S(1)}, bf16[464,256]{1,0:T(8,128)(2,1)S(1)}, u32[]{:S(2)}, u32[]{:S(2)}) collective-permute-start(bf16[464,256]{1,0:T(8,128)(2,1)S(1)} %get-tuple-element.33), channel_id=1, source_target_pairs={{0,2},{1,3},{2,0},{3,1},{4,6},{5,7},{6,4},{7,5},{8,10},{9,11},{10,... | collective-permute-start | bytes 712712 | tf_op jit(solution)/shard_map/ppermute | solution.py:364
  10.9 23.4 %collective-permute-start.6 = (bf16[464,256]{1,0:T(8,128)(2,1)S(1)}, bf16[464,256]{1,0:T(8,128)(2,1)S(1)}, u32[]{:S(2)}, u32[]{:S(2)}) collective-permute-start(bf16[464,256]{1,0:T(8,128)(2,1)S(1)} %get-tuple-element.34), channel_id=1, source_target_pairs={{0,3},{1,2},{2,1},{3,0},{4,7},{5,6},{6,5},{7,4},{8,11},{9,10},{10,... | collective-permute-start | bytes 712712 | tf_op jit(solution)/shard_map/ppermute | solution.py:364
  10.9 1.2 %collective-permute-start = (f32[4,256]{1,0:T(4,128)S(1)}, f32[4,256]{1,0:T(4,128)S(1)}, u32[]{:S(2)}, u32[]{:S(2)}) collective-permute-start(f32[4,256]{1,0:T(4,128)S(1)} %get-tuple-element.25), channel_id=1, source_target_pairs={{0,4},{4,0},{8,12},{12,8},{16,20},{20,16},{24,28},{28,24},{1,5},{5... | collective-permute-start | bytes 12296 | tf_op jit(solution)/shard_map/ppermute | solution.py:364
  12.1 4.5 %collective-permute-start.3 = (f32[8,256]{1,0:T(8,128)S(1)}, f32[8,256]{1,0:T(8,128)S(1)}, u32[]{:S(2)}, u32[]{:S(2)}) collective-permute-start(f32[8,256]{1,0:T(8,128)S(1)} %pad_maximum_fusion.refs_0_), channel_id=1, source_target_pairs={{0,24},{4,28},{8,16},{12,20},{16,8},{20,12},{24,0},{28,4},{1,25},{... | collective-permute-start | bytes 24584 | tf_op jit(solution)/shard_map/ppermute | solution.py:364
  14.8 6.6 %collective-permute-start.2 = (f32[8,256]{1,0:T(8,128)S(1)}, f32[8,256]{1,0:T(8,128)S(1)}, u32[]{:S(2)}, u32[]{:S(2)}) collective-permute-start(f32[8,256]{1,0:T(8,128)S(1)} %pad_maximum_fusion.refs_0_), channel_id=1, source_target_pairs={{0,16},{4,20},{8,24},{12,28},{16,0},{20,4},{24,8},{28,12},{1,17},{... | collective-permute-start | bytes 24584 | tf_op jit(solution)/shard_map/ppermute | solution.py:364
  16.7 4.7 %collective-permute-start.1 = (f32[8,256]{1,0:T(8,128)S(1)}, f32[8,256]{1,0:T(8,128)S(1)}, u32[]{:S(2)}, u32[]{:S(2)}) collective-permute-start(f32[8,256]{1,0:T(8,128)S(1)} %pad_maximum_fusion.refs_0_), channel_id=1, source_target_pairs={{0,8},{4,12},{8,0},{12,4},{16,24},{20,28},{24,16},{28,20},{1,9},{5... | collective-permute-start | bytes 24584 | tf_op jit(solution)/shard_map/ppermute | solution.py:364
  18.4 1.6 %copy-start = (bf16[256,4096]{1,0:T(8,128)(2,1)S(1)}, bf16[256,4096]{1,0:T(8,128)(2,1)}, u32[]{:S(2)}) copy-start(bf16[256,4096]{1,0:T(8,128)(2,1)} %templates.3) | copy-start | bytes 6291460
  20.0 1.0 %copy-start.2 = (bf16[256,768]{1,0:T(8,128)(2,1)S(1)}, bf16[256,768]{1,0:T(8,128)(2,1)}, u32[]{:S(2)}) copy-start(bf16[256,768]{1,0:T(8,128)(2,1)} %spectrum.5) | copy-start | bytes 1179652
  21.0 9.0 %copy-start.4 = (f32[2,256,768]{2,1,0:T(8,128)S(1)}, f32[2,256,768]{2,1,0:T(8,128)}, u32[]{:S(2)}) copy-start(f32[2,256,768]{2,1,0:T(8,128)} %uniform.1) | copy-start | bytes 4718596
  21.0 9.0 %copy-start.5 = (f32[256,768]{1,0:T(8,128)S(1)}, f32[256,768]{1,0:T(8,128)}, u32[]{:S(2)}) copy-start(f32[256,768]{1,0:T(8,128)} %gauss.1) | copy-start | bytes 2359300
  21.0 13.4 %copy-start.7 = (bf16[256,256]{1,0:T(8,128)(2,1)S(1)}, bf16[256,256]{1,0:T(8,128)(2,1)}, u32[]{:S(2)}) copy-start(bf16[256,256]{1,0:T(8,128)(2,1)} %encoder.3) | copy-start | bytes 393220
  22.2 5.4 %collective-permute-start.7 = (f32[32,256]{1,0:T(8,128)S(1)}, f32[32,256]{1,0:T(8,128)S(1)}, u32[]{:S(2)}, u32[]{:S(2)}) collective-permute-start(f32[32,256]{1,0:T(8,128)S(1)} %get-tuple-element.35), channel_id=1, source_target_pairs={{0,1},{1,0},{2,3},{3,2},{4,5},{5,4},{6,7},{7,6},{8,9},{9,8},{10,11... | collective-permute-start | bytes 98312 | tf_op jit(solution)/shard_map/ppermute | solution.py:364
  23.0 11.3 %collective-permute-start.8 = (f32[32,256]{1,0:T(8,128)S(1)}, f32[32,256]{1,0:T(8,128)S(1)}, u32[]{:S(2)}, u32[]{:S(2)}) collective-permute-start(f32[32,256]{1,0:T(8,128)S(1)} %get-tuple-element.36), channel_id=1, source_target_pairs={{0,2},{1,3},{2,0},{3,1},{4,6},{5,7},{6,4},{7,5},{8,10},{9,11},{10,... | collective-permute-start | bytes 98312 | tf_op jit(solution)/shard_map/ppermute | solution.py:364
  27.6 6.7 %collective-permute-start.9 = (f32[32,256]{1,0:T(8,128)S(1)}, f32[32,256]{1,0:T(8,128)S(1)}, u32[]{:S(2)}, u32[]{:S(2)}) collective-permute-start(f32[32,256]{1,0:T(8,128)S(1)} %get-tuple-element.37), channel_id=1, source_target_pairs={{0,3},{1,2},{2,1},{3,0},{4,7},{5,6},{6,5},{7,4},{8,11},{9,10},{10,... | collective-permute-start | bytes 98312 | tf_op jit(solution)/shard_map/ppermute | solution.py:364
  29.9 15.5 %copy-start.3 = (bf16[256,768]{1,0:T(8,128)(2,1)S(1)}, bf16[256,768]{1,0:T(8,128)(2,1)}, u32[]{:S(2)}) copy-start(bf16[256,768]{1,0:T(8,128)(2,1)} %spectrum.5) | copy-start | bytes 1179652
  35.7 6.8 %collective-permute-start.13 = (bf16[384,128]{1,0:T(8,128)(2,1)S(1)}, bf16[384,128]{1,0:T(8,128)(2,1)S(1)}, u32[]{:S(2)}, u32[]{:S(2)}) collective-permute-start(bf16[384,128]{1,0:T(8,128)(2,1)S(1)} %get-tuple-element.38.own), channel_id=1, source_target_pairs={{0,3},{1,2},{2,1},{3,0},{4,7},{5,6},{6,5},{7,4},{8,11},{9,10},{10,... | collective-permute-start | bytes 294920 | tf_op jit(solution)/shard_map/ppermute | solution.py:364
  38.2 7.3 %collective-permute-start.12 = (bf16[384,128]{1,0:T(8,128)(2,1)S(1)}, bf16[384,128]{1,0:T(8,128)(2,1)S(1)}, u32[]{:S(2)}, u32[]{:S(2)}) collective-permute-start(bf16[384,128]{1,0:T(8,128)(2,1)S(1)} %get-tuple-element.38.own), channel_id=1, source_target_pairs={{0,2},{1,3},{2,0},{3,1},{4,6},{5,7},{6,4},{7,5},{8,10},{9,11},{10,... | collective-permute-start | bytes 294920 | tf_op jit(solution)/shard_map/ppermute | solution.py:364
  38.2 7.3 %collective-permute-start.11 = (bf16[384,128]{1,0:T(8,128)(2,1)S(1)}, bf16[384,128]{1,0:T(8,128)(2,1)S(1)}, u32[]{:S(2)}, u32[]{:S(2)}) collective-permute-start(bf16[384,128]{1,0:T(8,128)(2,1)S(1)} %get-tuple-element.38.own), channel_id=1, source_target_pairs={{0,1},{1,0},{2,3},{3,2},{4,5},{5,4},{6,7},{7,6},{8,9},{9,8},{10,11... | collective-permute-start | bytes 294920 | tf_op jit(solution)/shard_map/ppermute | solution.py:364
  40.1 2.2 %collective-permute-start.10 = (bf16[256,128]{1,0:T(8,128)(2,1)S(1)}, bf16[256,128]{1,0:T(8,128)(2,1)S(1)}, u32[]{:S(2)}, u32[]{:S(2)}) collective-permute-start(bf16[256,128]{1,0:T(8,128)(2,1)S(1)} %get-tuple-element.39), channel_id=1, source_target_pairs={{0,4},{4,8},{8,12},{12,16},{16,20},{20,24},{24,28},{1,5},{5,9},{9,... | collective-permute-start | bytes 196616 | tf_op jit(solution)/shard_map/ppermute | solution.py:455
  61.1 4.2 %collective-permute-start.17 = (f32[4,512,256]{2,1,0:T(8,128)S(1)}, f32[4,512,256]{2,1,0:T(8,128)S(1)}, u32[]{:S(2)}, u32[]{:S(2)}) collective-permute-start(f32[4,512,256]{2,1,0:T(8,128)S(1)} %get-tuple-element.43), channel_id=1, source_target_pairs={{0,4},{4,0},{8,12},{12,8},{16,20},{20,16},{24,28},{28,24},{1,5},{5... | collective-permute-start | bytes 6291464 | tf_op jit(solution)/shard_map/ppermute | solution.py:364
  65.8 26.2 %collective-permute-start.19 = (f32[512,256]{1,0:T(8,128)S(1)}, f32[512,256]{1,0:T(8,128)S(1)}, u32[]{:S(2)}, u32[]{:S(2)}) collective-permute-start(f32[512,256]{1,0:T(8,128)S(1)} %get-tuple-element.47), channel_id=1, source_target_pairs={{0,16},{4,20},{8,24},{12,28},{16,0},{20,4},{24,8},{28,12},{1,17},{... | collective-permute-start | bytes 1572872 | tf_op jit(solution)/shard_map/ppermute | solution.py:364
  68.6 23.5 %collective-permute-start.20 = (f32[512,256]{1,0:T(8,128)S(1)}, f32[512,256]{1,0:T(8,128)S(1)}, u32[]{:S(2)}, u32[]{:S(2)}) collective-permute-start(f32[512,256]{1,0:T(8,128)S(1)} %get-tuple-element.48), channel_id=1, source_target_pairs={{0,24},{4,28},{8,16},{12,20},{16,8},{20,12},{24,0},{28,4},{1,25},{... | collective-permute-start | bytes 1572872 | tf_op jit(solution)/shard_map/ppermute | solution.py:364
  69.2 24.2 %collective-permute-start.18 = (f32[512,256]{1,0:T(8,128)S(1)}, f32[512,256]{1,0:T(8,128)S(1)}, u32[]{:S(2)}, u32[]{:S(2)}) collective-permute-start(f32[512,256]{1,0:T(8,128)S(1)} %get-tuple-element.49), channel_id=1, source_target_pairs={{0,8},{4,12},{8,0},{12,4},{16,24},{20,28},{24,16},{28,20},{1,9},{5... | collective-permute-start | bytes 1572872 | tf_op jit(solution)/shard_map/ppermute | solution.py:364
  70.2 5.5 %collective-permute-start.16 = (f32[768]{0:T(1024)S(1)}, f32[768]{0:T(1024)S(1)}, u32[]{:S(2)}, u32[]{:S(2)}) collective-permute-start(f32[768]{0:T(1024)S(1)} %get-tuple-element.44), channel_id=1, source_target_pairs={{0,3},{1,2},{2,1},{3,0},{4,7},{5,6},{6,5},{7,4},{8,11},{9,10},{10,... | collective-permute-start | bytes 9224 | tf_op jit(solution)/shard_map/ppermute | solution.py:364
  72.7 4.5 %collective-permute-start.15 = (f32[768]{0:T(1024)S(1)}, f32[768]{0:T(1024)S(1)}, u32[]{:S(2)}, u32[]{:S(2)}) collective-permute-start(f32[768]{0:T(1024)S(1)} %get-tuple-element.44), channel_id=1, source_target_pairs={{0,2},{1,3},{2,0},{3,1},{4,6},{5,7},{6,4},{7,5},{8,10},{9,11},{10,... | collective-permute-start | bytes 9224 | tf_op jit(solution)/shard_map/ppermute | solution.py:364
  75.6 3.6 %collective-permute-start.14 = (f32[768]{0:T(1024)S(1)}, f32[768]{0:T(1024)S(1)}, u32[]{:S(2)}, u32[]{:S(2)}) collective-permute-start(f32[768]{0:T(1024)S(1)} %get-tuple-element.44), channel_id=1, source_target_pairs={{0,1},{1,0},{2,3},{3,2},{4,5},{5,4},{6,7},{7,6},{8,9},{9,8},{10,11... | collective-permute-start | bytes 9224 | tf_op jit(solution)/shard_map/ppermute | solution.py:364
  (1 other events, 0.7 us)

commit v2 on v1

--- a/solution.py
+++ b/solution.py
@@ -19,7 +19,7 @@
 bf16 = jnp.bfloat16
 
 
-def call(kernel, name, outs, scratch, *args, scalars=0, limit=48 << 20):
+def call(kernel, name, outs, scratch, *args, scalars=0, limit=12 << 20):
     return pl.pallas_call(
         kernel,
         name=name,
@@ -28,6 +28,7 @@
         out_specs=[VMEM] * len(outs),
         scratch_shapes=[pltpu.VMEM(shape, dtype) for shape, dtype in scratch],
         compiler_params=pltpu.CompilerParams(vmem_limit_bytes=limit),
+        cost_estimate=pl.CostEstimate(flops=0, bytes_accessed=0, transcendentals=0),
     )(*args)
 
 
@@ -51,16 +52,26 @@
     return (size - 1 - lax.broadcasted_iota(jnp.int32, (size, 1), 0)).astype(f32)
 
 
-def summary_kernel(nf, place, spectrum, decay, clips, encoder, *refs):
-    messages, (own, gains, states, tm_message), (frames_first,) = (
-        refs[: nf - 1],
-        refs[nf - 1 : nf + 3],
-        refs[nf + 3 :],
-    )
+def summary_kernel(nf, place, *refs):
+    sources, messages, (own, gains, states, tm_message, frame_sums), (frames_first, *held, copied) = (
+        refs[:3],
+        refs[3 : nf + 2],
+        refs[nf + 2 : nf + 7],
+        refs[nf + 7 :],
+    )
+    copies = [
+        pltpu.make_async_copy(source, target, copied.at[index])
+        for index, (source, target) in enumerate(zip(sources, held))
+    ]
+    for copy in copies:
+        copy.start()
+    for copy in copies:
+        copy.wait()
+    spectrum, small, encoder = held
     bins, frames = spectrum.shape
     piece = frames // nf
     here = place[0, 0]
-    clip_row = clips[...].astype(f32)
+    clip_row = small[:, bins:]
     clip_col = column(clip_row)
     first = clip_row[:, :1]
     gain = jnp.ones_like(clip_col)
@@ -68,8 +79,12 @@
         seen = jnp.max(jnp.where(clip_row == value, 1.0, 0.0), axis=1, keepdims=True)
         counts = (seen > 0.0) & (first < value)
         gain = jnp.where(counts & (clip_col >= value), gain * 0.8, gain)
-    frames_first[...] = jnp.transpose(spectrum[...].astype(f32))
-    rate = decay[...]
+    spectral = spectrum[...].astype(f32)
+    frames_first[...] = jnp.transpose(spectral)
+    total = jnp.sum(spectral, axis=0, keepdims=True)
+    for row in range(frames // bins):
+        frame_sums[row : row + 1, :] = total[:, row * bins : (row + 1) * bins]
+    rate = small[:, 0:bins]
     keep = log_keep(rate)
     scaled = frames_first[...] * wide(1.0 / gain, bins) * rate
     weights = jnp.exp(steps_down(piece) * keep)
@@ -97,24 +112,28 @@
         target[0:piece, :] = frames_first[pl.ds(start, piece), :].astype(bf16)
         target[piece : piece + TAIL, :] = frames_first[frames - TAIL :, :].astype(bf16)
         if step:
-            target[piece + TAIL :, :] = encoder[...]
+            half = encoder.shape[0] // 2
+            low = pl.multiple_of((place[0, 1] & 1) * half, half)
+            target[piece + TAIL :, :] = encoder[pl.ds(low, half), :]
     start = pl.multiple_of(here * piece, piece)
     frames_first[:, 0:LANES] = gain
     gains[0:piece, :] = frames_first[pl.ds(start, piece), 0:LANES]
     gains[piece:, :] = gain[frames - TAIL :]
 
 
-def totals_kernel(templates, spectrum, stats):
-    bins, frames = spectrum.shape
-    stats[...] = jnp.zeros_like(stats)
-    columns = templates.shape[1]
+def halves_kernel(rows, *refs):
+    messages = refs[len(refs) // 2 : -1]
+    half = messages[0].shape[0] - rows
+    for index, message in enumerate(messages):
+        refs[-1][index * half : (index + 1) * half, :] = message[rows:, :]
+
+
+def totals_kernel(templates, frame_sums, stats):
+    bins, columns = templates.shape
     for row in range(columns // bins):
         part = templates[:, row * bins : (row + 1) * bins].astype(f32)
         stats[row : row + 1, :] = jnp.sum(part, axis=0, keepdims=True)
-    for row in range(frames // bins):
-        part = spectrum[:, row * bins : (row + 1) * bins].astype(f32)
-        at = columns // bins + row
-        stats[at : at + 1, :] = jnp.sum(part, axis=0, keepdims=True)
+    stats[columns // bins : columns // bins + frame_sums.shape[0], :] = frame_sums[...]
 
 
 def entry_kernel(nt, nf, place, decay, init, states, stats, *refs):
@@ -155,12 +174,11 @@
         target = own if step == 0 else messages[step - 1]
         other = here ^ step
         power = jnp.exp((other * piece).astype(f32) * keep)
-        target[...] = jnp.zeros_like(target)
         target[0:1, :] = power * state + states[pl.ds(other, 1), :]
         target[1:2, :] = tail
         target[2:3, :] = decay[...]
         if step:
-            target[8:, :] = stats[...]
+            target[3:, :] = stats[...]
     previous = blocks[jnp.maximum(lap - 1, 0) ^ lap, height - 1 : height, bins - LANES : bins]
     clips_wide[:, 0:LANES] = jnp.where(lap > 0, previous, -1.0)
     for row in range(frames // bins):
@@ -192,27 +210,22 @@
     second[...] = jnp.where(counts >= 2.0, jnp.log(second[...]), 0.0)
 
 
-def sampler_kernel(nf, own, encoder, own_state, gains, normal, first, second, boosts, *refs):
-    messages, arrivals, (packed, tail), scratch = (
+def normed_kernel(nf, own, own_state, gains, *refs):
+    messages, arrivals, (normed, inputs, running) = (
         refs[: nf - 1],
         refs[nf - 1 : 2 * nf - 2],
-        refs[2 * nf - 2 : 2 * nf],
-        refs[2 * nf :],
-    )
-    inputs, running, normed = scratch
+        refs[2 * nf - 2 :],
+    )
     rows, bins = own.shape
     piece = rows - TAIL
     segment = piece // 8
-    topics, width = normal.shape
     gain = gains[...]
     inverse = 1.0 / gain
     powers = (1 + lax.broadcasted_iota(jnp.int32, (segment, 1), 0)).astype(f32)
-    logits = jnp.zeros((topics, width), f32)
-    normed[...] = jnp.zeros_like(normed)
+    normed[:, rows:, :] = jnp.zeros_like(normed[:, rows:, :])
     for step in range(nf):
         state = own_state if step == 0 else arrivals[step - 1]
         block = own if step == 0 else messages[step - 1]
-        weights = encoder[...] if step == 0 else messages[step - 1][rows:, :]
         for part in range(bins // LANES):
             at = step * (bins // LANES) + part
             lanes = slice(part * LANES, (part + 1) * LANES)
@@ -238,6 +251,24 @@
                 running[at, row : row + 1, :] = carry
             smooth = running[at] * gain
             normed[step, 0:rows, lanes] = (spectral * lax.rsqrt(smooth + 0.1)).astype(bf16)
+
+
+def sampler_kernel(nf, piece, place, normed, encoder, halves, normal, first, second, boosts, *refs):
+    messages, (packed, tail) = refs[: nf - 1], refs[nf - 1 :]
+    core = place[0, 1] & 1
+    topics, width = normal.shape
+    half = topics // 2
+    rows = piece + TAIL
+    logits = jnp.zeros((topics, width), f32)
+    for step in range(nf):
+        if step == 0:
+            weights = encoder[...]
+        else:
+            mine = messages[step - 1][rows:, :]
+            other = halves[(step - 1) * half : step * half, :]
+            lower = jnp.where(core == 0, mine, other)
+            upper = jnp.where(core == 0, other, mine)
+            weights = jnp.concatenate([lower, upper], axis=0)
         logits += lax.dot_general(
             weights, normed[step], (((1,), (1,)), ((), ())), preferred_element_type=f32
         )
@@ -253,26 +284,23 @@
         packed[index * topics : (index + 1) * topics, :] = tile.astype(bf16)
     tile = proportions[:, full * LANES : (full + 1) * LANES]
     if rest:
-        half = topics // 2
         lane = lax.broadcasted_iota(jnp.int32, (half, LANES), 1)
         joined = jnp.where(lane < rest, tile[:half], pltpu.roll(tile[half:], rest, 1))
         packed[full * topics :, :] = joined.astype(bf16)
     tail[...] = pltpu.roll(tile, LANES - TAIL - rest, 1).astype(bf16)
 
 
-def gradient_kernel(nt, nf, place, own, rim, clips, templates, spectrum, stats, *refs):
-    messages, arrivals, (away, kept, sums), scratch = (
+def rebuild_kernel(nt, nf, place, own, rim, clips, templates, spectrum, stats, *refs):
+    messages, arrivals, (stacked, ratio, sums, bound), (extended, heads, recon) = (
         refs[: nf - 1],
         refs[nf - 1 : 2 * nf - 2],
-        refs[2 * nf - 2 : 2 * nf + 1],
-        refs[2 * nf + 1 :],
-    )
-    extended, heads, stacked, valid, recon, ratio = scratch
+        refs[2 * nf - 2 : 2 * nf + 2],
+        refs[2 * nf + 2 :],
+    )
     bins, frames = spectrum.shape
-    here, lap = place[0, 0], place[0, 1]
+    here = place[0, 0]
     piece = frames // nf
     topics = extended.shape[0]
-    tile = stacked.shape[1]
     full, rest = piece // LANES, piece % LANES
     extended[:, 0:LANES] = rim[...].astype(f32)
     for step in range(nf):
@@ -294,7 +322,7 @@
 
     total = stats[...]
     for arrival in arrivals:
-        total = total + arrival[8:, :]
+        total = total + arrival[3:, :]
     columns = templates.shape[1]
     wide_rows = columns // bins
     heads[...] = jnp.zeros_like(heads)
@@ -307,56 +335,62 @@
     for row in range(frames // bins):
         at = wide_rows + row
         sums[2:3, row * bins : (row + 1) * bins] = total[at : at + 1, :]
+    ids = jnp.broadcast_to(clips[...], (L, LANES + frames))
+    shifted = pltpu.roll(ids, 0, 1, stride=1, stride_axis=0)
+    valid = jnp.where(shifted == ids, 1.0, 0.0)[:, LANES:]
+    group = 32
+    for low in range(0, topics, group):
+        for topic in range(low, low + group):
+            row = jnp.broadcast_to(extended[topic : topic + 1, :], (L, LANES + frames))
+            lagged = pltpu.roll(row, 0, 1, stride=1, stride_axis=0)[:, LANES:]
+            stacked[topic * L : (topic + 1) * L, :] = (lagged * valid).astype(bf16)
+        part = slice(low * L, (low + group) * L)
+        left = jnp.concatenate([templates[:, part], heads[:, part]], axis=0)
+        product = jnp.dot(left, stacked[part, :], preferred_element_type=f32)
+        if low == 0:
+            recon[...] = product
+        else:
+            recon[...] += product
+    rebuilt = recon[0:bins, :]
+    recon_sum = recon[bins : bins + 1] + recon[bins + 1 : bins + 2] + recon[bins + 2 : bins + 3]
+    spectral = spectrum[...].astype(f32)
     scale = F * K / (frames * nt)
-    group = 32
-    for start in range(0, frames, tile):
-        span = slice(start, start + LANES + tile)
-        ids = jnp.broadcast_to(clips[:, span], (L, LANES + tile))
-        shifted = pltpu.roll(ids, 0, 1, stride=1, stride_axis=0)
-        valid[...] = jnp.where(shifted == ids, 1.0, 0.0)[:, LANES:]
-        for low in range(0, topics, group):
-
-            def one(index, _):
-                topic = low + index
-                row = extended[pl.ds(topic, 1), span]
-                lagged = pltpu.roll(
-                    jnp.broadcast_to(row, (L, LANES + tile)), 0, 1, stride=1, stride_axis=0
-                )
-                at = pl.multiple_of(topic * L, L)
-                stacked[pl.ds(at, L), :] = (lagged[:, LANES:] * valid[...]).astype(bf16)
-                return 0
-
-            lax.fori_loop(0, group, one, 0, unroll=4)
-            part = slice(low * L, (low + group) * L)
-            left = jnp.concatenate([templates[:, part], heads[:, part]], axis=0)
-            product = jnp.dot(left, stacked[part, :], preferred_element_type=f32)
-            if low == 0:
-                recon[...] = product
-            else:
-                recon[...] += product
-        here_frames = slice(start, start + tile)
-        rebuilt = recon[0:bins, :]
-        recon_sum = recon[bins : bins + 1] + recon[bins + 1 : bins + 2] + recon[bins + 2 : bins + 3]
-        spectral = spectrum[:, here_frames].astype(f32)
-        spec_sum = sums[2:3, here_frames]
-        sums[0:1, here_frames] = recon_sum
-        sums[1:2, here_frames] = jnp.sum(spectral * jnp.log(rebuilt), axis=0, keepdims=True)
-        ratio[...] = (scale * (1.0 / recon_sum - spectral / (spec_sum * rebuilt))).astype(bf16)
-        height = away.shape[1]
-        for target, side in ((away, 1), (kept, 0)):
-            for step in range(nt // 2):
-                owner = lap ^ (2 * step + side)
-                at = pl.multiple_of(owner * height, height)
-                product = lax.dot_general(
-                    stacked[pl.ds(at, height), :],
-                    ratio[...],
-                    (((1,), (1,)), ((), ())),
-                    preferred_element_type=f32,
-                )
-                if start == 0:
-                    target[step] = product
-                else:
-                    target[step] += product
+    rounded = (scale * (1.0 / recon_sum - spectral / (sums[2:3, :] * rebuilt))).astype(bf16)
+    turned = jnp.transpose(rounded.astype(f32))
+    ratio[...] = turned.astype(bf16)
+    reach = jnp.sum(jnp.abs(turned), axis=0, keepdims=True)
+    bound[...] = jnp.broadcast_to(jnp.max(reach, axis=1, keepdims=True), bound.shape)
+    sums[0:1, :] = recon_sum
+    sums[1:2, :] = jnp.sum(spectral * jnp.log(rebuilt), axis=0, keepdims=True)
+
+
+def product_kernel(side, steps, place, stacked, ratio, bound, *targets):
+    height = targets[0].shape[0] - 8 * side
+    lap = place[0, 1]
+    for step, target in zip(steps, targets):
+        at = pl.multiple_of((lap ^ (2 * step + side)) * height, height)
+        target[0:height, :] = jnp.dot(
+            stacked[pl.ds(at, height), :], ratio[...], preferred_element_type=f32
+        )
+        if side:
+            target[height:, :] = bound[...]
+
+
+def message_kernel(bound, kept, crossed, message):
+    height = kept.shape[0]
+    limit = (bound[0:1, :] + crossed[height : height + 1, :]) * (1.02 / 32768.0)
+    unit = jnp.maximum(limit, 2.0**-14).astype(bf16).astype(f32)
+    message[0:height, :] = (kept[...] + crossed[0:height, :]) * (1.0 / unit)
+    message[height:, :] = jnp.broadcast_to(unit, (16, kept.shape[1]))
+
+
+def total_kernel(kept, crossed, *refs):
+    parts, total = refs[:-1], refs[-1]
+    height = kept.shape[0]
+    value = kept[...] + crossed[0:height, :]
+    for part in parts:
+        value = value + part[0:height, :] * part[height : height + 1, :]
+    total[...] = value
 
 
 def exchanged(value, axis, step):
@@ -387,36 +421,42 @@
     state_rows = -(-(nf + 1) // 8) * 8
     height = 1 + frames // bins
 
-    *messages, own, gains, states, tm_message = call(
+    small = jnp.pad(decay_rate, (0, frames)) + jnp.pad(clip_ids, (bins, 0)).astype(f32)
+    small = small[None]
+    *messages, own, gains, states, tm_message, frame_sums = pl.pallas_call(
         functools.partial(summary_kernel, nf),
-        "summary",
-        [((rows + topics, bins), bf16)] * (nf - 1)
+        name="summary",
+        out_shape=[jax.ShapeDtypeStruct((rows + topics // 2, bins), bf16)] * (nf - 1)
         + [
-            ((rows, bins), bf16),
-            ((rows, LANES), f32),
-            ((state_rows, bins), f32),
-            ((height, bins), f32),
+            jax.ShapeDtypeStruct((rows, bins), bf16),
+            jax.ShapeDtypeStruct((rows, LANES), f32),
+            jax.ShapeDtypeStruct((state_rows, bins), f32),
+            jax.ShapeDtypeStruct((height, bins), f32),
+            jax.ShapeDtypeStruct((frames // bins, bins), f32),
         ],
-        [((frames, bins), f32)],
-        place,
-        spectrum,
-        decay,
-        clip_ids[None],
-        encoder,
-        scalars=1,
-    )
+        in_specs=[SMEM] + [pl.BlockSpec(memory_space=pltpu.HBM)] * 3,
+        out_specs=[VMEM] * (nf + 4),
+        scratch_shapes=[
+            pltpu.VMEM((frames, bins), f32),
+            pltpu.VMEM((bins, frames), bf16),
+            pltpu.VMEM((1, bins + frames), f32),
+            pltpu.VMEM((topics, bins), bf16),
+            pltpu.SemaphoreType.DMA((3,)),
+        ],
+        compiler_params=pltpu.CompilerParams(vmem_limit_bytes=12 << 20),
+    )(place, spectrum, small, encoder)
     messages = [exchanged(messages[step - 1], "freq", step) for step in range(1, nf)]
     pair = jnp.concatenate([tm_message, exchanged(tm_message, "tm", 1)], axis=0)
     pairs = [pair] + [exchanged(pair, "tm", step) for step in range(2, nt, 2)]
-    stat_rows = -(-(columns // bins + frames // bins) // 8) * 8
+    stat_rows = columns // bins + frames // bins
     (stats,) = call(
-        totals_kernel, "totals", [((stat_rows, bins), f32)], [], templates, spectrum
+        totals_kernel, "totals", [((stat_rows, bins), f32)], [], templates, frame_sums
     )
     *arrivals, own_state, clips_wide = call(
         functools.partial(entry_kernel, nt, nf),
         "entry",
-        [((8 + stat_rows, bins), f32)] * (nf - 1)
-        + [((8, bins), f32), ((1, LANES + frames), f32)],
+        [((3 + stat_rows, bins), f32)] * (nf - 1)
+        + [((3, bins), f32), ((1, LANES + frames), f32)],
         [((nt, height, bins), f32), ((nt, 1, bins), f32)],
         place,
         decay,
@@ -427,6 +467,15 @@
         scalars=1,
     )
     arrivals = [exchanged(arrivals[step - 1], "freq", step) for step in range(1, nf)]
+    (halves,) = call(
+        functools.partial(halves_kernel, rows),
+        "halves",
+        [(((nf - 1) * topics // 2, bins), bf16)],
+        [],
+        *arrivals,
+        *messages,
+    )
+    halves = exchanged(halves, "tm", 1)
     noises = call(
         functools.partial(noise_kernel, nf),
         "noise",
@@ -438,35 +487,37 @@
         boost_count[None],
         scalars=1,
     )
+    (normed,) = call(
+        functools.partial(normed_kernel, nf),
+        "normed",
+        [((nf, width, bins), bf16)],
+        [((nf * bins // LANES, rows, LANES), f32)] * 2,
+        own,
+        own_state,
+        gains,
+        *messages,
+        *arrivals,
+    )
     packed, tail = call(
-        functools.partial(sampler_kernel, nf),
+        functools.partial(sampler_kernel, nf, piece),
         "sampler",
         [((topics * piece // LANES, LANES), bf16), ((topics, LANES), bf16)],
-        [((nf * bins // LANES, rows, LANES), f32)] * 2 + [((nf, width, bins), bf16)],
-        own,
+        [],
+        place,
+        normed,
         encoder,
-        own_state,
-        gains,
+        halves,
         *noises,
         *messages,
-        *arrivals,
+        scalars=1,
     )
     shares = [exchanged(packed, "freq", step) for step in range(1, nf)]
     rim = lax.ppermute(tail, "tm", [(index, index + 1) for index in range(nt - 1)])
-    tile = 768 if frames % 768 == 0 else frames
-    height = columns // nt
-    away, kept, sums = call(
-        functools.partial(gradient_kernel, nt, nf),
-        "gradient",
-        [((nt // 2, height, bins), f32)] * 2 + [((8, frames), f32)],
-        [
-            ((topics, LANES + frames), f32),
-            ((16, columns), bf16),
-            ((columns, tile), bf16),
-            ((L, tile), f32),
-            ((bins + 16, tile), f32),
-            ((bins, tile), bf16),
-        ],
+    stacked, ratio, sums, bound = call(
+        functools.partial(rebuild_kernel, nt, nf),
+        "rebuild",
+        [((columns, frames), bf16), ((frames, bins), bf16), ((8, frames), f32), ((8, bins), f32)],
+        [((topics, LANES + frames), f32), ((16, columns), bf16), ((bins + 16, frames), f32)],
         place,
         packed,
         rim,
@@ -478,12 +529,44 @@
         *arrivals,
         scalars=1,
     )
-    both = kept + exchanged(away, "tm", 1)
-    parts = [exchanged(both[step], "tm", 2 * step) for step in range(1, nt // 2)]
+    height = columns // nt
+    order = list(range(1, nt // 2)) + [0]
+    away, kept = (
+        call(
+            functools.partial(product_kernel, side, order),
+            name,
+            [((height + 8 * side, bins), f32)] * len(order),
+            [],
+            place,
+            stacked,
+            ratio,
+            bound,
+            scalars=1,
+        )
+        for side, name in ((1, "away"), (0, "kept"))
+    )
+    kept = dict(zip(order, kept))
+    crossed = {step: exchanged(block, "tm", 1) for step, block in zip(order, away)}
+    parts = []
+    for step in order[:-1]:
+        (message,) = call(
+            message_kernel,
+            "message",
+            [((height + 16, bins), f32)],
+            [],
+            bound,
+            kept[step],
+            crossed[step],
+        )
+        part = exchanged(message.astype(jnp.float16), "tm", 2 * step)
+        parts.append(part.astype(f32))
+    (result,) = call(
+        total_kernel, "total", [((height, bins), f32)], [], kept[0], crossed[0], *parts
+    )
     log_part = sums[1]
     log_sum = log_part + sum(exchanged(log_part, "freq", step) for step in range(1, nf))
     frame_loss = jnp.log(sums[0]) - log_sum / sums[2]
-    return (frame_loss, both[0] + sum(parts))
+    return (frame_loss, result)
 
 
 def solution(mesh):

time: 94.6 us -> 74 us (0.78)
  waiting for transfers between devices: 35.4 us -> 19.5 us
  Pallas kernels: 20.3 us -> 15.7 us
  starting transfers between devices: 29.7 us -> 32.4 us
  local copies, waits for them, and re-layouts: 6.03 us -> 3.56 us
    ppermute x20 -> x24, waiting for transfers between devices: 34.5 us -> 18.6 us  [exchanged(): lax.ppermute(value, axis, [(index, index ^ step) for index in range(size)])]
    pallas_call x6 -> x13, Pallas kernels: 20.3 us -> 14.1 us  [call(): pl.pallas_call(kernel, name=name, out_shape=[jax.ShapeDtypeStruct(shape,...]
    ppermute x20 -> x24, starting transfers between devices: 28.5 us -> 30.8 us  [exchanged(): lax.ppermute(value, axis, [(index, index ^ step) for index in range(size)])]
    unnamed x24 -> x22, local copies, waits for them, and re-layouts: 5.19 us -> 3.53 us
    pallas_call x0 -> x1, Pallas kernels: none -> 1.63 us  [on_device(): pl.pallas_call(functools.partial(summary_kernel, nf), name='summary', out...]
  transfers between devices with their start and end apart: 21 -> 25, of which waited for: 13 -> 9; matrix products, arithmetic and copies ran while one was open for 1% -> 1% of each run, Pallas kernels for 2% -> 6%
where the time goes in v2:
time: 74 us; the launch traced here: 73.7 us
  starting transfers between devices  32.4 us (44%)
  waiting for transfers between devices  19.5 us (26%)
  Pallas kernels  15.7 us (21%)
  local copies, waits for them, and re-layouts  3.56 us (5%)
  other arithmetic  1.63 us (2%)
  between operations  0.91 us (1%)
    ppermute x24, starting transfers between devices, exchanged(): lax.ppermute(value, axis, [(index, index ^ step) for index in range(size)])  30.8 us
    ppermute x24, waiting for transfers between devices, exchanged(): lax.ppermute(value, axis, [(index, index ^ step) for index in range(size)])  18.6 us
    pallas_call x13, Pallas kernels, call(): pl.pallas_call(kernel, name=name, out_shape=[jax.ShapeDtypeStruct(shape,...  14.1 us
    unnamed x22, local copies, waits for them, and re-layouts  3.53 us
    pallas_call x1, Pallas kernels, on_device(): pl.pallas_call(functools.partial(summary_kernel, nf), name='summary', out...  1.63 us
    ppermute x1, starting transfers between devices, on_device(): lax.ppermute(tail, 'tm', [(index, index + 1) for index in range(nt - 1)])  1.57 us
  transfers between devices with their start and end apart: 25, of which 9 were waited for; matrix products, arithmetic and copies ran while one was open for 1% of the time, Pallas kernels for 6%

profile of v2, /device:TPU:0, one launch (start us, length us, event | category | flops | bytes accessed | tf_op | source)
XLA Modules:
  0.0 73.7 jit_solution(13988057570046244465)
XLA Ops:
  0.7 0.7 convert_add_fusion
  1.4 1.0 %copy-done.3 = bf16[256,768]{1,0:T(8,128)(2,1)S(1)} copy-done((bf16[256,768]{1,0:T(8,128)(2,1)S(1)}, bf16[256,768]{1,0:T(8,128)(2,1)}, u32[]{:S(2)}) %copy-start.3) | copy-done | bytes 393240
  2.4 0.9 %copy-done.6 = bf16[256,256]{1,0:T(8,128)(2,1)S(1)} copy-done((bf16[256,256]{1,0:T(8,128)(2,1)S(1)}, bf16[256,256]{1,0:T(8,128)(2,1)}, u32[]{:S(2)}) %copy-start.6) | copy-done | bytes 131096
  3.3 1.6 %summary.1 = (bf16[336,256]{1,0:T(8,128)(2,1)S(1)}, bf16[336,256]{1,0:T(8,128)(2,1)S(1)}, bf16[336,256]{1,0:T(8,128)(2,1)S(1)}, bf16[208,256]{1,0:T(8,128)(2,1)S...) custom-call(s32[1,2]{1,0:T(1,128)S(1)} %add_bitcast_fusion.place, ...), custom_call_target="tpu_custom_call" | custom-call | tf_op jit(solution)/shard_map/summary/pallas_call | solution.py:426
  5.5 2.6 %collective-permute-start.4 = (bf16[336,256]{1,0:T(8,128)(2,1)S(1)}, bf16[336,256]{1,0:T(8,128)(2,1)S(1)}, u32[]{:S(2)}, u32[]{:S(2)}) collective-permute-start(bf16[336,256]{1,0:T(8,128)(2,1)S(1)} %get-tuple-element.39), channel_id=1, source_target_pairs={{0,1},{1,0},{2,3},{3,2},{4,5},{5,4},{6,7},{7,6},{8,9},{9,8},{10,11... | collective-permute-start | bytes 516104 | tf_op jit(solution)/shard_map/ppermute | solution.py:398
  8.2 2.6 %collective-permute-start.5 = (bf16[336,256]{1,0:T(8,128)(2,1)S(1)}, bf16[336,256]{1,0:T(8,128)(2,1)S(1)}, u32[]{:S(2)}, u32[]{:S(2)}) collective-permute-start(bf16[336,256]{1,0:T(8,128)(2,1)S(1)} %get-tuple-element.40), channel_id=1, source_target_pairs={{0,2},{1,3},{2,0},{3,1},{4,6},{5,7},{6,4},{7,5},{8,10},{9,11},{10,... | collective-permute-start | bytes 516104 | tf_op jit(solution)/shard_map/ppermute | solution.py:398
  10.8 2.7 %collective-permute-start.3 = (f32[8,256]{1,0:T(8,128)S(1)}, f32[8,256]{1,0:T(8,128)S(1)}, u32[]{:S(2)}, u32[]{:S(2)}) collective-permute-start(f32[8,256]{1,0:T(8,128)S(1)} %pad_maximum_fusion.refs_0_), channel_id=1, source_target_pairs={{0,24},{4,28},{8,16},{12,20},{16,8},{20,12},{24,0},{28,4},{1,25},{... | collective-permute-start | bytes 24584 | tf_op jit(solution)/shard_map/ppermute | solution.py:398
  14.0 1.4 %collective-permute-done.3.refs_3_ = f32[8,256]{1,0:T(8,128)S(1)} collective-permute-done((f32[8,256]{1,0:T(8,128)S(1)}, f32[8,256]{1,0:T(8,128)S(1)}, u32[]{:S(2)}, u32[]{:S(2)}) %collective-permute-start.3) | collective-permute-done | bytes 8224 | tf_op jit(solution)/shard_map/ppermute | solution.py:398
  15.4 1.7 %collective-permute-start.1 = (f32[8,256]{1,0:T(8,128)S(1)}, f32[8,256]{1,0:T(8,128)S(1)}, u32[]{:S(2)}, u32[]{:S(2)}) collective-permute-start(f32[8,256]{1,0:T(8,128)S(1)} %pad_maximum_fusion.refs_0_), channel_id=1, source_target_pairs={{0,8},{4,12},{8,0},{12,4},{16,24},{20,28},{24,16},{28,20},{1,9},{5... | collective-permute-start | bytes 24584 | tf_op jit(solution)/shard_map/ppermute | solution.py:398
  17.1 1.6 %copy-done = bf16[256,4096]{1,0:T(8,128)(2,1)S(1)} copy-done((bf16[256,4096]{1,0:T(8,128)(2,1)S(1)}, bf16[256,4096]{1,0:T(8,128)(2,1)}, u32[]{:S(2)}) %copy-start) | copy-done | bytes 2097176
  19.0 0.8 %entry.1 = (f32[22,256]{1,0:T(8,128)S(1)}, f32[22,256]{1,0:T(8,128)S(1)}, f32[22,256]{1,0:T(8,128)S(1)}, f32[3,256]{1,0:T(4,128)S(1)}, f32[1,896]{1,0:T(1,128)S(1)}) custom-call(s32[1,2]{1,0:T(1,128)S(1)} %add_bitcast_fusion.place, f32[1,256]{1,0:T(1,128)S(1)} %bitcast.9, f32[1,256]{1,0:T(1,128)S(1)} %bitcast.10, f32[8,256]{1,0:T(8,128)S(1)} %get-tuple-element.34.states, ...), custom_call_target="tpu_custom_call" | custom-call | tf_op jit(solution)/shard_map/entry/pallas_call | solution.py:23
  19.9 1.0 %collective-permute-start.7 = (f32[22,256]{1,0:T(8,128)S(1)}, f32[22,256]{1,0:T(8,128)S(1)}, u32[]{:S(2)}, u32[]{:S(2)}) collective-permute-start(f32[22,256]{1,0:T(8,128)S(1)} %get-tuple-element.42), channel_id=1, source_target_pairs={{0,1},{1,0},{2,3},{3,2},{4,5},{5,4},{6,7},{7,6},{8,9},{9,8},{10,11... | collective-permute-start | bytes 67592 | tf_op jit(solution)/shard_map/ppermute | solution.py:398
  20.8 3.5 %collective-permute-start.8 = (f32[22,256]{1,0:T(8,128)S(1)}, f32[22,256]{1,0:T(8,128)S(1)}, u32[]{:S(2)}, u32[]{:S(2)}) collective-permute-start(f32[22,256]{1,0:T(8,128)S(1)} %get-tuple-element.43), channel_id=1, source_target_pairs={{0,2},{1,3},{2,0},{3,1},{4,6},{5,7},{6,4},{7,5},{8,10},{9,11},{10,... | collective-permute-start | bytes 67592 | tf_op jit(solution)/shard_map/ppermute | solution.py:398
  24.3 3.3 %collective-permute-start.9 = (f32[22,256]{1,0:T(8,128)S(1)}, f32[22,256]{1,0:T(8,128)S(1)}, u32[]{:S(2)}, u32[]{:S(2)}) collective-permute-start(f32[22,256]{1,0:T(8,128)S(1)} %get-tuple-element.44), channel_id=1, source_target_pairs={{0,3},{1,2},{2,1},{3,0},{4,7},{5,6},{6,5},{7,4},{8,11},{9,10},{10,... | collective-permute-start | bytes 67592 | tf_op jit(solution)/shard_map/ppermute | solution.py:398
  28.2 1.7 %collective-permute-done.9.refs_5_.refs_2_ = f32[22,256]{1,0:T(8,128)S(1)} collective-permute-done((f32[22,256]{1,0:T(8,128)S(1)}, f32[22,256]{1,0:T(8,128)S(1)}, u32[]{:S(2)}, u32[]{:S(2)}) %collective-permute-start.9) | collective-permute-done | bytes 22560 | tf_op jit(solution)/shard_map/ppermute | solution.py:398
  30.1 0.9 %noise.1 = (f32[256,256]{1,0:T(8,128)S(1)}, f32[256,256]{1,0:T(8,128)S(1)}, f32[256,256]{1,0:T(8,128)S(1)}, f32[256,256]{1,0:T(8,128)S(1)}) custom-call(s32[1,2]{1,0:T(1,128)S(1)} %add_bitcast_fusion.place, f32[256,768]{1,0:T(8,128)S(1)} %copy-done.5, f32[2,256,768]{2,1,0:T(8,128)S(1)} %copy-done.2, s32[1,256]{1,0:T(1,128)S(1)} %bitcast.11), custom_call_target="tpu_custom_call" | custom-call | tf_op jit(solution)/shard_map/noise/pallas_call | solution.py:23
  31.7 1.3 %sampler.1 = (bf16[384,128]{1,0:T(8,128)(2,1)S(1)}, bf16[256,128]{1,0:T(8,128)(2,1)S(1)}) custom-call(s32[1,2]{1,0:T(1,128)S(1)} %add_bitcast_fusion.place, bf16[4,256,256]{2,1,0:T(8,128)(2,1)S(1)} %normed.1, bf16[256,256]{1,0:T(8,128)(2,1)S(1)} %copy-done.7, bf16[384,256]{1,0:T(8,128)(2,1)S(1)} %collective-permute-done.10.halves, ...), custom_call_target="tpu_custom_call" | custom-call | tf_op jit(solution)/shard_map/sampler/pallas_call | solution.py:23
  33.0 3.6 %collective-permute-start.14 = (bf16[384,128]{1,0:T(8,128)(2,1)S(1)}, bf16[384,128]{1,0:T(8,128)(2,1)S(1)}, u32[]{:S(2)}, u32[]{:S(2)}) collective-permute-start(bf16[384,128]{1,0:T(8,128)(2,1)S(1)} %get-tuple-element.49.own), channel_id=1, source_target_pairs={{0,3},{1,2},{2,1},{3,0},{4,7},{5,6},{6,5},{7,4},{8,11},{9,10},{10,... | collective-permute-start | bytes 294920 | tf_op jit(solution)/shard_map/ppermute | solution.py:398
  36.6 0.9 %collective-permute-start.12 = (bf16[384,128]{1,0:T(8,128)(2,1)S(1)}, bf16[384,128]{1,0:T(8,128)(2,1)S(1)}, u32[]{:S(2)}, u32[]{:S(2)}) collective-permute-start(bf16[384,128]{1,0:T(8,128)(2,1)S(1)} %get-tuple-element.49.own), channel_id=1, source_target_pairs={{0,1},{1,0},{2,3},{3,2},{4,5},{5,4},{6,7},{7,6},{8,9},{9,8},{10,11... | collective-permute-start | bytes 294920 | tf_op jit(solution)/shard_map/ppermute | solution.py:398
  37.4 1.6 %collective-permute-start.11 = (bf16[256,128]{1,0:T(8,128)(2,1)S(1)}, bf16[256,128]{1,0:T(8,128)(2,1)S(1)}, u32[]{:S(2)}, u32[]{:S(2)}) collective-permute-start(bf16[256,128]{1,0:T(8,128)(2,1)S(1)} %get-tuple-element.50), channel_id=1, source_target_pairs={{0,4},{4,8},{8,12},{12,16},{16,20},{20,24},{24,28},{1,5},{5,9},{9,... | collective-permute-start | bytes 196616 | tf_op jit(solution)/shard_map/ppermute | solution.py:515
  39.0 0.9 %collective-permute-done.11.rim = bf16[256,128]{1,0:T(8,128)(2,1)S(1)} collective-permute-done((bf16[256,128]{1,0:T(8,128)(2,1)S(1)}, bf16[256,128]{1,0:T(8,128)(2,1)S(1)}, u32[]{:S(2)}, u32[]{:S(2)}) %collective-permute-start.11) | collective-permute-done | bytes 65568 | tf_op jit(solution)/shard_map/ppermute | solution.py:515
  40.5 3.8 %collective-permute-done.13.refs_1_ = bf16[384,128]{1,0:T(8,128)(2,1)S(1)} collective-permute-done((bf16[384,128]{1,0:T(8,128)(2,1)S(1)}, bf16[384,128]{1,0:T(8,128)(2,1)S(1)}, u32[]{:S(2)}, u32[]{:S(2)}) %collective-permute-start.13) | collective-permute-done | bytes 98336 | tf_op jit(solution)/shard_map/ppermute | solution.py:398
  44.3 5.9 %rebuild.1 = (bf16[4096,768]{1,0:T(8,128)(2,1)S(1)}, bf16[768,256]{1,0:T(8,128)(2,1)S(1)}, f32[8,768]{1,0:T(8,128)S(1)}, f32[8,256]{1,0:T(8,128)S(1)}) custom-call(s32[1,2]{1,0:T(1,128)S(1)} %add_bitcast_fusion.place, bf16[384,128]{1,0:T(8,128)(2,1)S(1)} %get-tuple-element.49.own, bf16[256,128]{1,0:T(8,128)(2,1)S(1)} %collective-permute-done.11.rim, ...), custom_call_target="tpu_custom_call" | custom-call | tf_op jit(solution)/shard_map/rebuild/pallas_call | solution.py:23
  50.2 1.5 %away.1 = (f32[520,256]{1,0:T(8,128)S(1)}, f32[520,256]{1,0:T(8,128)S(1)}, f32[520,256]{1,0:T(8,128)S(1)}, f32[520,256]{1,0:T(8,128)S(1)}) custom-call(s32[1,2]{1,0:T(1,128)S(1)} %add_bitcast_fusion.place, bf16[4096,768]{1,0:T(8,128)(2,1)S(1)} %get-tuple-element.53.stacked, bf16[768,256]{1,0:T(8,128)(2,1)S(1)} %get-tuple-element.54.ratio, ...), custom_call_target="tpu_custom_call" | custom-call | tf_op jit(solution)/shard_map/away/pallas_call | solution.py:23
  52.8 1.5 %kept.1 = (f32[512,256]{1,0:T(8,128)S(1)}, f32[512,256]{1,0:T(8,128)S(1)}, f32[512,256]{1,0:T(8,128)S(1)}, f32[512,256]{1,0:T(8,128)S(1)}) custom-call(s32[1,2]{1,0:T(1,128)S(1)} %add_bitcast_fusion.place, bf16[4096,768]{1,0:T(8,128)(2,1)S(1)} %get-tuple-element.53.stacked, bf16[768,256]{1,0:T(8,128)(2,1)S(1)} %get-tuple-element.54.ratio, ...), custom_call_target="tpu_custom_call" | custom-call | tf_op jit(solution)/shard_map/kept/pallas_call | solution.py:23
  54.4 1.6 %collective-permute-start.20 = (f16[528,256]{1,0:T(8,128)(2,1)S(1)}, f16[528,256]{1,0:T(8,128)(2,1)S(1)}, u32[]{:S(2)}, u32[]{:S(2)}) collective-permute-start(f16[528,256]{1,0:T(8,128)(2,1)S(1)} %convert_element_type.24), channel_id=1, source_target_pairs={{0,8},{4,12},{8,0},{12,4},{16,24},{20,28},{24,16},{28,20},{1,9},{5... | collective-permute-start | bytes 811016 | tf_op jit(solution)/shard_map/ppermute | solution.py:398
  56.1 1.6 %collective-permute-start.22 = (f16[528,256]{1,0:T(8,128)(2,1)S(1)}, f16[528,256]{1,0:T(8,128)(2,1)S(1)}, u32[]{:S(2)}, u32[]{:S(2)}) collective-permute-start(f16[528,256]{1,0:T(8,128)(2,1)S(1)} %convert_element_type.26), channel_id=1, source_target_pairs={{0,16},{4,20},{8,24},{12,28},{16,0},{20,4},{24,8},{28,12},{1,17},{... | collective-permute-start | bytes 811016 | tf_op jit(solution)/shard_map/ppermute | solution.py:398
  58.4 2.8 %collective-permute-start.17 = (f32[768]{0:T(1024)S(1)}, f32[768]{0:T(1024)S(1)}, u32[]{:S(2)}, u32[]{:S(2)}) collective-permute-start(f32[768]{0:T(1024)S(1)} %get-tuple-element.64), channel_id=1, source_target_pairs={{0,3},{1,2},{2,1},{3,0},{4,7},{5,6},{6,5},{7,4},{8,11},{9,10},{10,... | collective-permute-start | bytes 9224 | tf_op jit(solution)/shard_map/ppermute | solution.py:398
  61.2 2.7 %collective-permute-done.17 = f32[768]{0:T(1024)S(1)} collective-permute-done((f32[768]{0:T(1024)S(1)}, f32[768]{0:T(1024)S(1)}, u32[]{:S(2)}, u32[]{:S(2)}) %collective-permute-start.17) | collective-permute-done | bytes 3104 | tf_op jit(solution)/shard_map/ppermute | solution.py:398
  63.9 4.5 %collective-permute-done.16 = f32[768]{0:T(1024)S(1)} collective-permute-done((f32[768]{0:T(1024)S(1)}, f32[768]{0:T(1024)S(1)}, u32[]{:S(2)}, u32[]{:S(2)}) %collective-permute-start.16) | collective-permute-done | bytes 3104 | tf_op jit(solution)/shard_map/ppermute | solution.py:398
  68.7 3.3 %collective-permute-done.15 = f32[768]{0:T(1024)S(1)} collective-permute-done((f32[768]{0:T(1024)S(1)}, f32[768]{0:T(1024)S(1)}, u32[]{:S(2)}, u32[]{:S(2)}) %collective-permute-start.15) | collective-permute-done | bytes 3104 | tf_op jit(solution)/shard_map/ppermute | solution.py:398
  72.8 0.9 %total.1 = f32[512,256]{1,0:T(8,128)} custom-call(f32[512,256]{1,0:T(8,128)S(1)} %get-tuple-element.56.kept, f32[520,256]{1,0:T(8,128)S(1)} %collective-permute-done.18.crossed, f32[528,256]{1,0:T(8,128)S(1)} %convert_element_type.25.refs_0_, f32[528,256]{1,0:T(8,128)S(1)} %convert_element_type.27.refs_1_, f32[528,256]{1,0:T(8,128)S(1)} %convert_element_type.29.refs_2_), custom_call_target="tpu_custom_call" | custom-call | tf_op jit(solution)/shard_map/total/pallas_call | solution.py:23
  (65 shorter events, 6.6 us)
Async XLA Ops:
  0.6 18.4 %copy-start.8 = (f32[256]{0:T(256)S(1)}, f32[256]{0:T(256)}, u32[]{:S(2)}) copy-start(f32[256]{0:T(256)} %param.10) | copy-start | bytes 3076
  0.6 18.4 %copy-start.9 = (f32[256]{0:T(256)S(1)}, f32[256]{0:T(256)}, u32[]{:S(2)}) copy-start(f32[256]{0:T(256)} %param.11) | copy-start | bytes 3076
  0.7 29.4 %copy-start.10 = (s32[256]{0:T(256)S(1)}, s32[256]{0:T(256)}, u32[]{:S(2)}) copy-start(s32[256]{0:T(256)} %param.16) | copy-start | bytes 3076
  5.0 5.8 %collective-permute-start = (f32[4,256]{1,0:T(4,128)S(1)}, f32[4,256]{1,0:T(4,128)S(1)}, u32[]{:S(2)}, u32[]{:S(2)}) collective-permute-start(f32[4,256]{1,0:T(4,128)S(1)} %get-tuple-element.36), channel_id=1, source_target_pairs={{0,4},{4,0},{8,12},{12,8},{16,20},{20,16},{24,28},{28,24},{1,5},{5... | collective-permute-start | bytes 12296 | tf_op jit(solution)/shard_map/ppermute | solution.py:398
  5.5 24.5 %collective-permute-start.4 = (bf16[336,256]{1,0:T(8,128)(2,1)S(1)}, bf16[336,256]{1,0:T(8,128)(2,1)S(1)}, u32[]{:S(2)}, u32[]{:S(2)}) collective-permute-start(bf16[336,256]{1,0:T(8,128)(2,1)S(1)} %get-tuple-element.39), channel_id=1, source_target_pairs={{0,1},{1,0},{2,3},{3,2},{4,5},{5,4},{6,7},{7,6},{8,9},{9,8},{10,11... | collective-permute-start | bytes 516104 | tf_op jit(solution)/shard_map/ppermute | solution.py:398
  8.2 21.8 %collective-permute-start.5 = (bf16[336,256]{1,0:T(8,128)(2,1)S(1)}, bf16[336,256]{1,0:T(8,128)(2,1)S(1)}, u32[]{:S(2)}, u32[]{:S(2)}) collective-permute-start(bf16[336,256]{1,0:T(8,128)(2,1)S(1)} %get-tuple-element.40), channel_id=1, source_target_pairs={{0,2},{1,3},{2,0},{3,1},{4,6},{5,7},{6,4},{7,5},{8,10},{9,11},{10,... | collective-permute-start | bytes 516104 | tf_op jit(solution)/shard_map/ppermute | solution.py:398
  10.7 19.2 %collective-permute-start.6 = (bf16[336,256]{1,0:T(8,128)(2,1)S(1)}, bf16[336,256]{1,0:T(8,128)(2,1)S(1)}, u32[]{:S(2)}, u32[]{:S(2)}) collective-permute-start(bf16[336,256]{1,0:T(8,128)(2,1)S(1)} %get-tuple-element.41), channel_id=1, source_target_pairs={{0,3},{1,2},{2,1},{3,0},{4,7},{5,6},{6,5},{7,4},{8,11},{9,10},{10,... | collective-permute-start | bytes 516104 | tf_op jit(solution)/shard_map/ppermute | solution.py:398
  10.8 4.6 %collective-permute-start.3 = (f32[8,256]{1,0:T(8,128)S(1)}, f32[8,256]{1,0:T(8,128)S(1)}, u32[]{:S(2)}, u32[]{:S(2)}) collective-permute-start(f32[8,256]{1,0:T(8,128)S(1)} %pad_maximum_fusion.refs_0_), channel_id=1, source_target_pairs={{0,24},{4,28},{8,16},{12,20},{16,8},{20,12},{24,0},{28,4},{1,25},{... | collective-permute-start | bytes 24584 | tf_op jit(solution)/shard_map/ppermute | solution.py:398
  13.5 5.5 %collective-permute-start.2 = (f32[8,256]{1,0:T(8,128)S(1)}, f32[8,256]{1,0:T(8,128)S(1)}, u32[]{:S(2)}, u32[]{:S(2)}) collective-permute-start(f32[8,256]{1,0:T(8,128)S(1)} %pad_maximum_fusion.refs_0_), channel_id=1, source_target_pairs={{0,16},{4,20},{8,24},{12,28},{16,0},{20,4},{24,8},{28,12},{1,17},{... | collective-permute-start | bytes 24584 | tf_op jit(solution)/shard_map/ppermute | solution.py:398
  15.4 3.7 %collective-permute-start.1 = (f32[8,256]{1,0:T(8,128)S(1)}, f32[8,256]{1,0:T(8,128)S(1)}, u32[]{:S(2)}, u32[]{:S(2)}) collective-permute-start(f32[8,256]{1,0:T(8,128)S(1)} %pad_maximum_fusion.refs_0_), channel_id=1, source_target_pairs={{0,8},{4,12},{8,0},{12,4},{16,24},{20,28},{24,16},{28,20},{1,9},{5... | collective-permute-start | bytes 24584 | tf_op jit(solution)/shard_map/ppermute | solution.py:398
  18.7 11.4 %copy-start.2 = (f32[2,256,768]{2,1,0:T(8,128)S(1)}, f32[2,256,768]{2,1,0:T(8,128)}, u32[]{:S(2)}) copy-start(f32[2,256,768]{2,1,0:T(8,128)} %uniform.1) | copy-start | bytes 4718596
  18.7 11.4 %copy-start.5 = (f32[256,768]{1,0:T(8,128)S(1)}, f32[256,768]{1,0:T(8,128)}, u32[]{:S(2)}) copy-start(f32[256,768]{1,0:T(8,128)} %gauss.1) | copy-start | bytes 2359300
  19.9 4.4 %collective-permute-start.7 = (f32[22,256]{1,0:T(8,128)S(1)}, f32[22,256]{1,0:T(8,128)S(1)}, u32[]{:S(2)}, u32[]{:S(2)}) collective-permute-start(f32[22,256]{1,0:T(8,128)S(1)} %get-tuple-element.42), channel_id=1, source_target_pairs={{0,1},{1,0},{2,3},{3,2},{4,5},{5,4},{6,7},{7,6},{8,9},{9,8},{10,11... | collective-permute-start | bytes 67592 | tf_op jit(solution)/shard_map/ppermute | solution.py:398
  20.8 7.4 %collective-permute-start.8 = (f32[22,256]{1,0:T(8,128)S(1)}, f32[22,256]{1,0:T(8,128)S(1)}, u32[]{:S(2)}, u32[]{:S(2)}) collective-permute-start(f32[22,256]{1,0:T(8,128)S(1)} %get-tuple-element.43), channel_id=1, source_target_pairs={{0,2},{1,3},{2,0},{3,1},{4,6},{5,7},{6,4},{7,5},{8,10},{9,11},{10,... | collective-permute-start | bytes 67592 | tf_op jit(solution)/shard_map/ppermute | solution.py:398
  24.3 5.6 %collective-permute-start.9 = (f32[22,256]{1,0:T(8,128)S(1)}, f32[22,256]{1,0:T(8,128)S(1)}, u32[]{:S(2)}, u32[]{:S(2)}) collective-permute-start(f32[22,256]{1,0:T(8,128)S(1)} %get-tuple-element.44), channel_id=1, source_target_pairs={{0,3},{1,2},{2,1},{3,0},{4,7},{5,6},{6,5},{7,4},{8,11},{9,10},{10,... | collective-permute-start | bytes 67592 | tf_op jit(solution)/shard_map/ppermute | solution.py:398
  30.0 1.7 %collective-permute-start.10 = (bf16[384,256]{1,0:T(8,128)(2,1)S(1)}, bf16[384,256]{1,0:T(8,128)(2,1)S(1)}, u32[]{:S(2)}, u32[]{:S(2)}) collective-permute-start(bf16[384,256]{1,0:T(8,128)(2,1)S(1)} %halves.1), channel_id=1, source_target_pairs={{0,4},{4,0},{8,12},{12,8},{16,20},{20,16},{24,28},{28,24},{1,5},{5... | collective-permute-start | bytes 589832 | tf_op jit(solution)/shard_map/ppermute | solution.py:398
  31.0 13.3 %copy-start.1 = (bf16[256,4096]{1,0:T(8,128)(2,1)S(1)}, bf16[256,4096]{1,0:T(8,128)(2,1)}, u32[]{:S(2)}) copy-start(bf16[256,4096]{1,0:T(8,128)(2,1)} %templates.3) | copy-start | bytes 6291460
  31.0 13.3 %copy-start.4 = (bf16[256,768]{1,0:T(8,128)(2,1)S(1)}, bf16[256,768]{1,0:T(8,128)(2,1)}, u32[]{:S(2)}) copy-start(bf16[256,768]{1,0:T(8,128)(2,1)} %spectrum.1) | copy-start | bytes 1179652
  33.0 7.5 %collective-permute-start.14 = (bf16[384,128]{1,0:T(8,128)(2,1)S(1)}, bf16[384,128]{1,0:T(8,128)(2,1)S(1)}, u32[]{:S(2)}, u32[]{:S(2)}) collective-permute-start(bf16[384,128]{1,0:T(8,128)(2,1)S(1)} %get-tuple-element.49.own), channel_id=1, source_target_pairs={{0,3},{1,2},{2,1},{3,0},{4,7},{5,6},{6,5},{7,4},{8,11},{9,10},{10,... | collective-permute-start | bytes 294920 | tf_op jit(solution)/shard_map/ppermute | solution.py:398
  36.6 7.7 %collective-permute-start.13 = (bf16[384,128]{1,0:T(8,128)(2,1)S(1)}, bf16[384,128]{1,0:T(8,128)(2,1)S(1)}, u32[]{:S(2)}, u32[]{:S(2)}) collective-permute-start(bf16[384,128]{1,0:T(8,128)(2,1)S(1)} %get-tuple-element.49.own), channel_id=1, source_target_pairs={{0,2},{1,3},{2,0},{3,1},{4,6},{5,7},{6,4},{7,5},{8,10},{9,11},{10,... | collective-permute-start | bytes 294920 | tf_op jit(solution)/shard_map/ppermute | solution.py:398
  36.6 7.7 %collective-permute-start.12 = (bf16[384,128]{1,0:T(8,128)(2,1)S(1)}, bf16[384,128]{1,0:T(8,128)(2,1)S(1)}, u32[]{:S(2)}, u32[]{:S(2)}) collective-permute-start(bf16[384,128]{1,0:T(8,128)(2,1)S(1)} %get-tuple-element.49.own), channel_id=1, source_target_pairs={{0,1},{1,0},{2,3},{3,2},{4,5},{5,4},{6,7},{7,6},{8,9},{9,8},{10,11... | collective-permute-start | bytes 294920 | tf_op jit(solution)/shard_map/ppermute | solution.py:398
  37.4 2.5 %collective-permute-start.11 = (bf16[256,128]{1,0:T(8,128)(2,1)S(1)}, bf16[256,128]{1,0:T(8,128)(2,1)S(1)}, u32[]{:S(2)}, u32[]{:S(2)}) collective-permute-start(bf16[256,128]{1,0:T(8,128)(2,1)S(1)} %get-tuple-element.50), channel_id=1, source_target_pairs={{0,4},{4,8},{8,12},{12,16},{16,20},{20,24},{24,28},{1,5},{5,9},{9,... | collective-permute-start | bytes 196616 | tf_op jit(solution)/shard_map/ppermute | solution.py:515
  51.7 2.6 %collective-permute-start.19 = (f32[520,256]{1,0:T(8,128)S(1)}, f32[520,256]{1,0:T(8,128)S(1)}, u32[]{:S(2)}, u32[]{:S(2)}) collective-permute-start(f32[520,256]{1,0:T(8,128)S(1)} %get-tuple-element.59), channel_id=1, source_target_pairs={{0,4},{4,0},{8,12},{12,8},{16,20},{20,16},{24,28},{28,24},{1,5},{5... | collective-permute-start | bytes 1597448 | tf_op jit(solution)/shard_map/ppermute | solution.py:398
  51.8 4.2 %collective-permute-start.21 = (f32[520,256]{1,0:T(8,128)S(1)}, f32[520,256]{1,0:T(8,128)S(1)}, u32[]{:S(2)}, u32[]{:S(2)}) collective-permute-start(f32[520,256]{1,0:T(8,128)S(1)} %get-tuple-element.61), channel_id=1, source_target_pairs={{0,4},{4,0},{8,12},{12,8},{16,20},{20,16},{24,28},{28,24},{1,5},{5... | collective-permute-start | bytes 1597448 | tf_op jit(solution)/shard_map/ppermute | solution.py:398
  52.3 5.5 %collective-permute-start.23 = (f32[520,256]{1,0:T(8,128)S(1)}, f32[520,256]{1,0:T(8,128)S(1)}, u32[]{:S(2)}, u32[]{:S(2)}) collective-permute-start(f32[520,256]{1,0:T(8,128)S(1)} %get-tuple-element.63), channel_id=1, source_target_pairs={{0,4},{4,0},{8,12},{12,8},{16,20},{20,16},{24,28},{28,24},{1,5},{5... | collective-permute-start | bytes 1597448 | tf_op jit(solution)/shard_map/ppermute | solution.py:398
  52.3 20.4 %collective-permute-start.18 = (f32[520,256]{1,0:T(8,128)S(1)}, f32[520,256]{1,0:T(8,128)S(1)}, u32[]{:S(2)}, u32[]{:S(2)}) collective-permute-start(f32[520,256]{1,0:T(8,128)S(1)} %get-tuple-element.57), channel_id=1, source_target_pairs={{0,4},{4,0},{8,12},{12,8},{16,20},{20,16},{24,28},{28,24},{1,5},{5... | collective-permute-start | bytes 1597448 | tf_op jit(solution)/shard_map/ppermute | solution.py:398
  54.4 18.2 %collective-permute-start.20 = (f16[528,256]{1,0:T(8,128)(2,1)S(1)}, f16[528,256]{1,0:T(8,128)(2,1)S(1)}, u32[]{:S(2)}, u32[]{:S(2)}) collective-permute-start(f16[528,256]{1,0:T(8,128)(2,1)S(1)} %convert_element_type.24), channel_id=1, source_target_pairs={{0,8},{4,12},{8,0},{12,4},{16,24},{20,28},{24,16},{28,20},{1,9},{5... | collective-permute-start | bytes 811016 | tf_op jit(solution)/shard_map/ppermute | solution.py:398
  56.1 16.5 %collective-permute-start.22 = (f16[528,256]{1,0:T(8,128)(2,1)S(1)}, f16[528,256]{1,0:T(8,128)(2,1)S(1)}, u32[]{:S(2)}, u32[]{:S(2)}) collective-permute-start(f16[528,256]{1,0:T(8,128)(2,1)S(1)} %convert_element_type.26), channel_id=1, source_target_pairs={{0,16},{4,20},{8,24},{12,28},{16,0},{20,4},{24,8},{28,12},{1,17},{... | collective-permute-start | bytes 811016 | tf_op jit(solution)/shard_map/ppermute | solution.py:398
  57.8 14.9 %collective-permute-start.24 = (f16[528,256]{1,0:T(8,128)(2,1)S(1)}, f16[528,256]{1,0:T(8,128)(2,1)S(1)}, u32[]{:S(2)}, u32[]{:S(2)}) collective-permute-start(f16[528,256]{1,0:T(8,128)(2,1)S(1)} %convert_element_type.28), channel_id=1, source_target_pairs={{0,24},{4,28},{8,16},{12,20},{16,8},{20,12},{24,0},{28,4},{1,25},{... | collective-permute-start | bytes 811016 | tf_op jit(solution)/shard_map/ppermute | solution.py:398
  58.4 5.5 %collective-permute-start.17 = (f32[768]{0:T(1024)S(1)}, f32[768]{0:T(1024)S(1)}, u32[]{:S(2)}, u32[]{:S(2)}) collective-permute-start(f32[768]{0:T(1024)S(1)} %get-tuple-element.64), channel_id=1, source_target_pairs={{0,3},{1,2},{2,1},{3,0},{4,7},{5,6},{6,5},{7,4},{8,11},{9,10},{10,... | collective-permute-start | bytes 9224 | tf_op jit(solution)/shard_map/ppermute | solution.py:398
  63.9 4.5 %collective-permute-start.16 = (f32[768]{0:T(1024)S(1)}, f32[768]{0:T(1024)S(1)}, u32[]{:S(2)}, u32[]{:S(2)}) collective-permute-start(f32[768]{0:T(1024)S(1)} %get-tuple-element.64), channel_id=1, source_target_pairs={{0,2},{1,3},{2,0},{3,1},{4,6},{5,7},{6,4},{7,5},{8,10},{9,11},{10,... | collective-permute-start | bytes 9224 | tf_op jit(solution)/shard_map/ppermute | solution.py:398
  68.4 3.6 %collective-permute-start.15 = (f32[768]{0:T(1024)S(1)}, f32[768]{0:T(1024)S(1)}, u32[]{:S(2)}, u32[]{:S(2)}) collective-permute-start(f32[768]{0:T(1024)S(1)} %get-tuple-element.64), channel_id=1, source_target_pairs={{0,1},{1,0},{2,3},{3,2},{4,5},{5,4},{6,7},{7,6},{8,9},{9,8},{10,11... | collective-permute-start | bytes 9224 | tf_op jit(solution)/shard_map/ppermute | solution.py:398
  (4 other events, 10.9 us)

commit v3 on v2

--- a/solution.py
+++ b/solution.py
@@ -52,23 +52,32 @@
     return (size - 1 - lax.broadcasted_iota(jnp.int32, (size, 1), 0)).astype(f32)
 
 
-def summary_kernel(nf, place, *refs):
-    sources, messages, (own, gains, states, tm_message, frame_sums), (frames_first, *held, copied) = (
-        refs[:3],
-        refs[3 : nf + 2],
-        refs[nf + 2 : nf + 7],
-        refs[nf + 7 :],
-    )
-    copies = [
-        pltpu.make_async_copy(source, target, copied.at[index])
-        for index, (source, target) in enumerate(zip(sources, held))
-    ]
-    for copy in copies:
-        copy.start()
-    for copy in copies:
-        copy.wait()
-    spectrum, small, encoder = held
-    bins, frames = spectrum.shape
+def pieces_kernel(nf, place, both, *refs):
+    messages, (own, flipped, frame_sums, frames_first) = refs[: nf - 1], refs[nf - 1 :]
+    frames, bins = flipped.shape
+    spectrum, encoder = both.at[:, 0:frames], both.at[:, frames:]
+    piece = frames // nf
+    half = encoder.shape[0] // 2
+    here, core = place[0, 0], place[0, 1] & 1
+    spectral = spectrum[...].astype(f32)
+    turned = jnp.transpose(spectral)
+    frames_first[...] = turned
+    flipped[...] = turned.astype(bf16)
+    for step in range(nf):
+        target = own if step == 0 else messages[step - 1]
+        start = pl.multiple_of((here ^ step) * piece, piece)
+        target[0:piece, :] = frames_first[pl.ds(start, piece), :].astype(bf16)
+        target[piece : piece + TAIL, :] = turned[frames - TAIL :].astype(bf16)
+        if step:
+            low = pl.multiple_of(core * half, half)
+            target[piece + TAIL :, :] = encoder[pl.ds(low, half), :]
+    total = jnp.sum(spectral, axis=0, keepdims=True)
+    for row in range(frames // bins):
+        frame_sums[row : row + 1, :] = total[:, row * bins : (row + 1) * bins]
+
+
+def summary_kernel(nf, place, flipped, small, gains, states, tm_message, all_gains):
+    frames, bins = flipped.shape
     piece = frames // nf
     here = place[0, 0]
     clip_row = small[:, bins:]
@@ -79,14 +88,13 @@
         seen = jnp.max(jnp.where(clip_row == value, 1.0, 0.0), axis=1, keepdims=True)
         counts = (seen > 0.0) & (first < value)
         gain = jnp.where(counts & (clip_col >= value), gain * 0.8, gain)
-    spectral = spectrum[...].astype(f32)
-    frames_first[...] = jnp.transpose(spectral)
-    total = jnp.sum(spectral, axis=0, keepdims=True)
-    for row in range(frames // bins):
-        frame_sums[row : row + 1, :] = total[:, row * bins : (row + 1) * bins]
+    all_gains[...] = gain
+    start = pl.multiple_of(here * piece, piece)
+    gains[0:piece, :] = all_gains[pl.ds(start, piece), :]
+    gains[piece:, :] = gain[frames - TAIL :]
     rate = small[:, 0:bins]
     keep = log_keep(rate)
-    scaled = frames_first[...] * wide(1.0 / gain, bins) * rate
+    scaled = flipped[...].astype(f32) * wide(1.0 / gain, bins) * rate
     weights = jnp.exp(steps_down(piece) * keep)
     state = jnp.zeros((1, bins), f32)
     states[...] = jnp.zeros_like(states)
@@ -106,22 +114,9 @@
     tm_message[0:1, :] = state
     for row in range(frames // bins):
         tm_message[row + 1 : row + 2, :] = clip_row[:, row * bins : (row + 1) * bins]
-    for step in range(nf):
-        target = own if step == 0 else messages[step - 1]
-        start = pl.multiple_of((here ^ step) * piece, piece)
-        target[0:piece, :] = frames_first[pl.ds(start, piece), :].astype(bf16)
-        target[piece : piece + TAIL, :] = frames_first[frames - TAIL :, :].astype(bf16)
-        if step:
-            half = encoder.shape[0] // 2
-            low = pl.multiple_of((place[0, 1] & 1) * half, half)
-            target[piece + TAIL :, :] = encoder[pl.ds(low, half), :]
-    start = pl.multiple_of(here * piece, piece)
-    frames_first[:, 0:LANES] = gain
-    gains[0:piece, :] = frames_first[pl.ds(start, piece), 0:LANES]
-    gains[piece:, :] = gain[frames - TAIL :]
-
-
-def halves_kernel(rows, *refs):
+
+
+def halves_kernel(rows, _, *refs):
     messages = refs[len(refs) // 2 : -1]
     half = messages[0].shape[0] - rows
     for index, message in enumerate(messages):
@@ -137,6 +132,7 @@
 
 
 def entry_kernel(nt, nf, place, decay, init, states, stats, *refs):
+    refs = refs[nf - 2 :]
     pairs, messages, (own, clips_wide), (blocks, gains) = (
         refs[: nt // 2],
         refs[nt // 2 : nt // 2 + nf - 1],
@@ -364,10 +360,12 @@
     sums[1:2, :] = jnp.sum(spectral * jnp.log(rebuilt), axis=0, keepdims=True)
 
 
-def product_kernel(side, steps, place, stacked, ratio, bound, *targets):
+def product_kernel(side, routed, place, stacked, ratio, bound, *targets):
     height = targets[0].shape[0] - 8 * side
     lap = place[0, 1]
-    for step, target in zip(steps, targets):
+    hop = 1 + ((lap ^ side) & 1)
+    order = (3, hop, 3 ^ hop, 0) if routed else (*range(1, len(targets)), 0)
+    for step, target in zip(order, targets):
         at = pl.multiple_of((lap ^ (2 * step + side)) * height, height)
         target[0:height, :] = jnp.dot(
             stacked[pl.ds(at, height), :], ratio[...], preferred_element_type=f32
@@ -376,11 +374,17 @@
             target[height:, :] = bound[...]
 
 
-def message_kernel(bound, kept, crossed, message):
+def message_kernel(bound, kept, crossed, *refs):
+    parts, message = refs[:-1], refs[-1]
     height = kept.shape[0]
-    limit = (bound[0:1, :] + crossed[height : height + 1, :]) * (1.02 / 32768.0)
-    unit = jnp.maximum(limit, 2.0**-14).astype(bf16).astype(f32)
-    message[0:height, :] = (kept[...] + crossed[0:height, :]) * (1.0 / unit)
+    limit = bound[0:1, :] + crossed[height : height + 1, :]
+    value = kept[...] + crossed[0:height, :]
+    for part in parts:
+        carried = part[height : height + 1, :]
+        limit = limit + carried * 32768.0
+        value = value + part[0:height, :] * carried
+    unit = jnp.maximum(limit * (1.02 / 32768.0), 2.0**-14).astype(bf16).astype(f32)
+    message[0:height, :] = value * (1.0 / unit)
     message[height:, :] = jnp.broadcast_to(unit, (16, kept.shape[1]))
 
 
@@ -421,30 +425,27 @@
     state_rows = -(-(nf + 1) // 8) * 8
     height = 1 + frames // bins
 
+    *messages, own, flipped, frame_sums = call(
+        functools.partial(pieces_kernel, nf),
+        "pieces",
+        [((rows + topics // 2, bins), bf16)] * (nf - 1)
+        + [((rows, bins), bf16), ((frames, bins), bf16), ((frames // bins, bins), f32)],
+        [((frames, bins), f32)],
+        place,
+        jnp.concatenate([spectrum, encoder], axis=1),
+        scalars=1,
+    )
     small = jnp.pad(decay_rate, (0, frames)) + jnp.pad(clip_ids, (bins, 0)).astype(f32)
-    small = small[None]
-    *messages, own, gains, states, tm_message, frame_sums = pl.pallas_call(
+    gains, states, tm_message = call(
         functools.partial(summary_kernel, nf),
-        name="summary",
-        out_shape=[jax.ShapeDtypeStruct((rows + topics // 2, bins), bf16)] * (nf - 1)
-        + [
-            jax.ShapeDtypeStruct((rows, bins), bf16),
-            jax.ShapeDtypeStruct((rows, LANES), f32),
-            jax.ShapeDtypeStruct((state_rows, bins), f32),
-            jax.ShapeDtypeStruct((height, bins), f32),
-            jax.ShapeDtypeStruct((frames // bins, bins), f32),
-        ],
-        in_specs=[SMEM] + [pl.BlockSpec(memory_space=pltpu.HBM)] * 3,
-        out_specs=[VMEM] * (nf + 4),
-        scratch_shapes=[
-            pltpu.VMEM((frames, bins), f32),
-            pltpu.VMEM((bins, frames), bf16),
-            pltpu.VMEM((1, bins + frames), f32),
-            pltpu.VMEM((topics, bins), bf16),
-            pltpu.SemaphoreType.DMA((3,)),
-        ],
-        compiler_params=pltpu.CompilerParams(vmem_limit_bytes=12 << 20),
-    )(place, spectrum, small, encoder)
+        "summary",
+        [((rows, LANES), f32), ((state_rows, bins), f32), ((height, bins), f32)],
+        [((frames, LANES), f32)],
+        place,
+        flipped,
+        small[None],
+        scalars=1,
+    )
     messages = [exchanged(messages[step - 1], "freq", step) for step in range(1, nf)]
     pair = jnp.concatenate([tm_message, exchanged(tm_message, "tm", 1)], axis=0)
     pairs = [pair] + [exchanged(pair, "tm", step) for step in range(2, nt, 2)]
@@ -463,19 +464,11 @@
         init_state[None],
         states,
         stats,
+        *messages[: nf - 2],
         *pairs,
         scalars=1,
     )
     arrivals = [exchanged(arrivals[step - 1], "freq", step) for step in range(1, nf)]
-    (halves,) = call(
-        functools.partial(halves_kernel, rows),
-        "halves",
-        [(((nf - 1) * topics // 2, bins), bf16)],
-        [],
-        *arrivals,
-        *messages,
-    )
-    halves = exchanged(halves, "tm", 1)
     noises = call(
         functools.partial(noise_kernel, nf),
         "noise",
@@ -487,6 +480,16 @@
         boost_count[None],
         scalars=1,
     )
+    (halves,) = call(
+        functools.partial(halves_kernel, rows),
+        "halves",
+        [(((nf - 1) * topics // 2, bins), bf16)],
+        [],
+        noises[0],
+        *arrivals,
+        *messages,
+    )
+    halves = exchanged(halves, "tm", 1)
     (normed,) = call(
         functools.partial(normed_kernel, nf),
         "normed",
@@ -530,12 +533,14 @@
         scalars=1,
     )
     height = columns // nt
-    order = list(range(1, nt // 2)) + [0]
+    routed = nt == 8
+    steps = [1 << power for power in range(nf.bit_length() - 1)]
+    log_sum = sums[1:2] + exchanged(sums[1:2], "freq", steps[0])
     away, kept = (
         call(
-            functools.partial(product_kernel, side, order),
+            functools.partial(product_kernel, side, routed),
             name,
-            [((height + 8 * side, bins), f32)] * len(order),
+            [((height + 8 * side, bins), f32)] * (nt // 2),
             [],
             place,
             stacked,
@@ -545,27 +550,38 @@
         )
         for side, name in ((1, "away"), (0, "kept"))
     )
-    kept = dict(zip(order, kept))
-    crossed = {step: exchanged(block, "tm", 1) for step, block in zip(order, away)}
-    parts = []
-    for step in order[:-1]:
+    crossed = [exchanged(block, "tm", 1) for block in away]
+
+    def sent(index, pairs, *extra):
         (message,) = call(
             message_kernel,
             "message",
             [((height + 16, bins), f32)],
             [],
             bound,
-            kept[step],
-            crossed[step],
+            kept[index],
+            crossed[index],
+            *extra,
         )
-        part = exchanged(message.astype(jnp.float16), "tm", 2 * step)
-        parts.append(part.astype(f32))
+        return lax.ppermute(message.astype(jnp.float16), "tm", pairs).astype(f32)
+
+    if routed:
+        first = [(lap, lap ^ (2 << (lap & 1))) for lap in range(nt)]
+        second = [(lap, lap ^ (4 >> (lap & 1))) for lap in range(nt)]
+        carried = sent(0, first)
+        carried, log_sum = lax.optimization_barrier((carried, log_sum))
+        parts = [sent(1, first), sent(2, second, carried)]
+    else:
+        parts = [
+            sent(step - 1, [(lap, lap ^ (2 * step)) for lap in range(nt)])
+            for step in range(1, nt // 2)
+        ]
     (result,) = call(
-        total_kernel, "total", [((height, bins), f32)], [], kept[0], crossed[0], *parts
-    )
-    log_part = sums[1]
-    log_sum = log_part + sum(exchanged(log_part, "freq", step) for step in range(1, nf))
-    frame_loss = jnp.log(sums[0]) - log_sum / sums[2]
+        total_kernel, "total", [((height, bins), f32)], [], kept[-1], crossed[-1], *parts
+    )
+    for step in steps[1:]:
+        log_sum = log_sum + exchanged(log_sum, "freq", step)
+    frame_loss = jnp.log(sums[0]) - log_sum[0] / sums[2]
     return (frame_loss, result)
 
 

time: 74 us -> 69 us (0.932)
  waiting for transfers between devices: 19.5 us -> 16.4 us
  local copies, waits for them, and re-layouts: 3.56 us -> 1.63 us
  starting transfers between devices: 32.4 us -> 31 us
  other arithmetic: 1.63 us -> 2.88 us
    ppermute x24 -> x20, starting transfers between devices: 30.8 us -> 25.1 us  [exchanged(): lax.ppermute(value, axis, [(index, index ^ step) for index in range(size)])]
    ppermute x24 -> x20, waiting for transfers between devices: 18.6 us -> 13 us  [exchanged(): lax.ppermute(value, axis, [(index, index ^ step) for index in range(size)])]
    ppermute x0 -> x3, starting transfers between devices: none -> 4.7 us  [sent(): return lax.ppermute(message.astype(jnp.float16), 'tm', pairs).astype(f32)]
    ppermute x0 -> x3, waiting for transfers between devices: none -> 2.44 us  [sent(): return lax.ppermute(message.astype(jnp.float16), 'tm', pairs).astype(f32)]
    unnamed x22 -> x18, local copies, waits for them, and re-layouts: 3.53 us -> 1.63 us
    pallas_call x13 -> x15, Pallas kernels: 14.1 us -> 15.9 us  [call(): pl.pallas_call(kernel, name=name, out_shape=[jax.ShapeDtypeStruct(shape,...]
    pallas_call x1 -> x0, Pallas kernels: 1.63 us -> none  [on_device(): pl.pallas_call(functools.partial(summary_kernel, nf), name='summary', out...]
    concatenate x0 -> x1, other arithmetic: none -> 1.24 us  [on_device(): jnp.concatenate([spectrum, encoder], axis=1)]
  transfers between devices with their start and end apart: 25 -> 24, of which waited for: 9 -> 11; matrix products, arithmetic and copies ran while one was open for 1% -> 2% of each run, Pallas kernels for 6% -> 8%
where the time goes in v3:
time: 69 us; the launch traced here: 68.8 us
  starting transfers between devices  31 us (45%)
  waiting for transfers between devices  16.4 us (24%)
  Pallas kernels  15.9 us (23%)
  other arithmetic  2.88 us (4%)
  local copies, waits for them, and re-layouts  1.63 us (2%)
  between operations  0.93 us (1%)
    ppermute x20, starting transfers between devices, exchanged(): lax.ppermute(value, axis, [(index, index ^ step) for index in range(size)])  25.1 us
    pallas_call x15, Pallas kernels, call(): pl.pallas_call(kernel, name=name, out_shape=[jax.ShapeDtypeStruct(shape,...  15.9 us
    ppermute x20, waiting for transfers between devices, exchanged(): lax.ppermute(value, axis, [(index, index ^ step) for index in range(size)])  13 us
    ppermute x3, starting transfers between devices, sent(): return lax.ppermute(message.astype(jnp.float16), 'tm', pairs).astype(f32)  4.7 us
    ppermute x3, waiting for transfers between devices, sent(): return lax.ppermute(message.astype(jnp.float16), 'tm', pairs).astype(f32)  2.44 us
    unnamed x18, local copies, waits for them, and re-layouts  1.63 us
  transfers between devices with their start and end apart: 24, of which 11 were waited for; matrix products, arithmetic and copies ran while one was open for 2% of the time, Pallas kernels for 8%

profile of v3, /device:TPU:0, one launch (start us, length us, event | category | flops | bytes accessed | tf_op | source)
XLA Modules:
  0.0 68.8 jit_solution(5125975450987394832)
XLA Ops:
  0.7 1.2 %pad_maximum_fusion.both = bf16[256,1024]{1,0:T(8,128)(2,1)S(1)} fusion(bf16[256,256]{1,0:T(8,128)(2,1)} %encoder.1, bf16[256,768]{1,0:T(8,128)(2,1)} %spectrum.1), kind=kLoop, calls=%fused_computation | loop fusion | flops 1048576 | bytes 1048576 | tf_op jit(solution)/shard_map/concatenate | solution.py:435
  2.8 3.1 %collective-permute-start = (bf16[336,256]{1,0:T(8,128)(2,1)S(1)}, bf16[336,256]{1,0:T(8,128)(2,1)S(1)}, u32[]{:S(2)}, u32[]{:S(2)}) collective-permute-start(bf16[336,256]{1,0:T(8,128)(2,1)S(1)} %get-tuple-element.40), channel_id=1, source_target_pairs={{0,1},{1,0},{2,3},{3,2},{4,5},{5,4},{6,7},{7,6},{8,9},{9,8},{10,11... | collective-permute-start | bytes 516104 | tf_op jit(solution)/shard_map/ppermute | solution.py:402
  5.9 2.6 %collective-permute-start.1 = (bf16[336,256]{1,0:T(8,128)(2,1)S(1)}, bf16[336,256]{1,0:T(8,128)(2,1)S(1)}, u32[]{:S(2)}, u32[]{:S(2)}) collective-permute-start(bf16[336,256]{1,0:T(8,128)(2,1)S(1)} %get-tuple-element.41), channel_id=1, source_target_pairs={{0,2},{1,3},{2,0},{3,1},{4,6},{5,7},{6,4},{7,5},{8,10},{9,11},{10,... | collective-permute-start | bytes 516104 | tf_op jit(solution)/shard_map/ppermute | solution.py:402
  9.1 1.1 %summary.1 = (f32[208,128]{1,0:T(8,128)S(1)}, f32[8,256]{1,0:T(8,128)S(1)}, f32[4,256]{1,0:T(4,128)S(1)}) custom-call(s32[1,2]{1,0:T(1,128)S(1)} %add_bitcast_fusion.place, bf16[768,256]{1,0:T(8,128)(2,1)S(1)} %get-tuple-element.37.flipped, f32[1,1024]{1,0:T(1,128)S(1)} %bitcast.8), custom_call_target="tpu_custom_call" | custom-call | tf_op jit(solution)/shard_map/summary/pallas_call | solution.py:23
  10.3 1.2 %collective-permute-done.2 = f32[4,256]{1,0:T(4,128)S(1)} collective-permute-done((f32[4,256]{1,0:T(4,128)S(1)}, f32[4,256]{1,0:T(4,128)S(1)}, u32[]{:S(2)}, u32[]{:S(2)}) %collective-permute-start.2) | collective-permute-done | bytes 4128 | tf_op jit(solution)/shard_map/ppermute | solution.py:402
  11.5 1.7 %collective-permute-start.3 = (f32[8,256]{1,0:T(8,128)S(1)}, f32[8,256]{1,0:T(8,128)S(1)}, u32[]{:S(2)}, u32[]{:S(2)}) collective-permute-start(f32[8,256]{1,0:T(8,128)S(1)} %pad_maximum_fusion.1.refs_2_), channel_id=1, source_target_pairs={{0,8},{4,12},{8,0},{12,4},{16,24},{20,28},{24,16},{28,20},{1,9},{5... | collective-permute-start | bytes 24584 | tf_op jit(solution)/shard_map/ppermute | solution.py:402
  13.2 1.5 %collective-permute-start.4 = (f32[8,256]{1,0:T(8,128)S(1)}, f32[8,256]{1,0:T(8,128)S(1)}, u32[]{:S(2)}, u32[]{:S(2)}) collective-permute-start(f32[8,256]{1,0:T(8,128)S(1)} %pad_maximum_fusion.1.refs_2_), channel_id=1, source_target_pairs={{0,16},{4,20},{8,24},{12,28},{16,0},{20,4},{24,8},{28,12},{1,17},{... | collective-permute-start | bytes 24584 | tf_op jit(solution)/shard_map/ppermute | solution.py:402
  15.1 2.7 %collective-permute-start.5 = (f32[8,256]{1,0:T(8,128)S(1)}, f32[8,256]{1,0:T(8,128)S(1)}, u32[]{:S(2)}, u32[]{:S(2)}) collective-permute-start(f32[8,256]{1,0:T(8,128)S(1)} %pad_maximum_fusion.1.refs_2_), channel_id=1, source_target_pairs={{0,24},{4,28},{8,16},{12,20},{16,8},{20,12},{24,0},{28,4},{1,25},{... | collective-permute-start | bytes 24584 | tf_op jit(solution)/shard_map/ppermute | solution.py:402
  17.8 1.6 %copy-done = bf16[256,4096]{1,0:T(8,128)(2,1)S(1)} copy-done((bf16[256,4096]{1,0:T(8,128)(2,1)S(1)}, bf16[256,4096]{1,0:T(8,128)(2,1)}, u32[]{:S(2)}) %copy-start) | copy-done | bytes 2097176
  19.7 1.7 %collective-permute-done.1.refs_1_.refs_4_ = bf16[336,256]{1,0:T(8,128)(2,1)S(1)} collective-permute-done((bf16[336,256]{1,0:T(8,128)(2,1)S(1)}, bf16[336,256]{1,0:T(8,128)(2,1)S(1)}, u32[]{:S(2)}, u32[]{:S(2)}) %collective-permute-start.1) | collective-permute-done | bytes 172064 | tf_op jit(solution)/shard_map/ppermute | solution.py:402
  22.4 2.9 %collective-permute-start.8 = (f32[22,256]{1,0:T(8,128)S(1)}, f32[22,256]{1,0:T(8,128)S(1)}, u32[]{:S(2)}, u32[]{:S(2)}) collective-permute-start(f32[22,256]{1,0:T(8,128)S(1)} %get-tuple-element.47), channel_id=1, source_target_pairs={{0,2},{1,3},{2,0},{3,1},{4,6},{5,7},{6,4},{7,5},{8,10},{9,11},{10,... | collective-permute-start | bytes 67592 | tf_op jit(solution)/shard_map/ppermute | solution.py:402
  25.3 1.4 %collective-permute-start.9 = (f32[22,256]{1,0:T(8,128)S(1)}, f32[22,256]{1,0:T(8,128)S(1)}, u32[]{:S(2)}, u32[]{:S(2)}) collective-permute-start(f32[22,256]{1,0:T(8,128)S(1)} %get-tuple-element.48), channel_id=1, source_target_pairs={{0,3},{1,2},{2,1},{3,0},{4,7},{5,6},{6,5},{7,4},{8,11},{9,10},{10,... | collective-permute-start | bytes 67592 | tf_op jit(solution)/shard_map/ppermute | solution.py:402
  26.7 0.9 %noise.1 = (f32[256,256]{1,0:T(8,128)S(1)}, f32[256,256]{1,0:T(8,128)S(1)}, f32[256,256]{1,0:T(8,128)S(1)}, f32[256,256]{1,0:T(8,128)S(1)}) custom-call(s32[1,2]{1,0:T(1,128)S(1)} %add_bitcast_fusion.place, f32[256,768]{1,0:T(8,128)S(1)} %copy-done.4, f32[2,256,768]{2,1,0:T(8,128)S(1)} %copy-done.2, s32[1,256]{1,0:T(1,128)S(1)} %bitcast.11), custom_call_target="tpu_custom_call" | custom-call | tf_op jit(solution)/shard_map/noise/pallas_call | solution.py:23
  27.7 3.3 %collective-permute-done.9.refs_5_.refs_2_ = f32[22,256]{1,0:T(8,128)S(1)} collective-permute-done((f32[22,256]{1,0:T(8,128)S(1)}, f32[22,256]{1,0:T(8,128)S(1)}, u32[]{:S(2)}, u32[]{:S(2)}) %collective-permute-start.9) | collective-permute-done | bytes 22560 | tf_op jit(solution)/shard_map/ppermute | solution.py:402
  32.5 1.3 %sampler.1 = (bf16[384,128]{1,0:T(8,128)(2,1)S(1)}, bf16[256,128]{1,0:T(8,128)(2,1)S(1)}) custom-call(s32[1,2]{1,0:T(1,128)S(1)} %add_bitcast_fusion.place, bf16[4,256,256]{2,1,0:T(8,128)(2,1)S(1)} %normed.1, bf16[256,256]{1,0:T(8,128)(2,1)S(1)} %copy-done.5, bf16[384,256]{1,0:T(8,128)(2,1)S(1)} %collective-permute-done.10.halves, ...), custom_call_target="tpu_custom_call" | custom-call | tf_op jit(solution)/shard_map/sampler/pallas_call | solution.py:23
  33.8 2.0 %collective-permute-start.13 = (bf16[384,128]{1,0:T(8,128)(2,1)S(1)}, bf16[384,128]{1,0:T(8,128)(2,1)S(1)}, u32[]{:S(2)}, u32[]{:S(2)}) collective-permute-start(bf16[384,128]{1,0:T(8,128)(2,1)S(1)} %get-tuple-element.53.own), channel_id=1, source_target_pairs={{0,2},{1,3},{2,0},{3,1},{4,6},{5,7},{6,4},{7,5},{8,10},{9,11},{10,... | collective-permute-start | bytes 294920 | tf_op jit(solution)/shard_map/ppermute | solution.py:402
  35.8 2.4 %collective-permute-start.14 = (bf16[384,128]{1,0:T(8,128)(2,1)S(1)}, bf16[384,128]{1,0:T(8,128)(2,1)S(1)}, u32[]{:S(2)}, u32[]{:S(2)}) collective-permute-start(bf16[384,128]{1,0:T(8,128)(2,1)S(1)} %get-tuple-element.53.own), channel_id=1, source_target_pairs={{0,3},{1,2},{2,1},{3,0},{4,7},{5,6},{6,5},{7,4},{8,11},{9,10},{10,... | collective-permute-start | bytes 294920 | tf_op jit(solution)/shard_map/ppermute | solution.py:402
  38.2 1.3 %collective-permute-start.11 = (bf16[256,128]{1,0:T(8,128)(2,1)S(1)}, bf16[256,128]{1,0:T(8,128)(2,1)S(1)}, u32[]{:S(2)}, u32[]{:S(2)}) collective-permute-start(bf16[256,128]{1,0:T(8,128)(2,1)S(1)} %get-tuple-element.54), channel_id=1, source_target_pairs={{0,4},{4,8},{8,12},{12,16},{16,20},{20,24},{24,28},{1,5},{5,9},{9,... | collective-permute-start | bytes 196616 | tf_op jit(solution)/shard_map/ppermute | solution.py:518
  39.5 0.9 %collective-permute-done.11.rim = bf16[256,128]{1,0:T(8,128)(2,1)S(1)} collective-permute-done((bf16[256,128]{1,0:T(8,128)(2,1)S(1)}, bf16[256,128]{1,0:T(8,128)(2,1)S(1)}, u32[]{:S(2)}, u32[]{:S(2)}) %collective-permute-start.11) | collective-permute-done | bytes 65568 | tf_op jit(solution)/shard_map/ppermute | solution.py:518
  40.4 4.3 %collective-permute-done.13.refs_1_ = bf16[384,128]{1,0:T(8,128)(2,1)S(1)} collective-permute-done((bf16[384,128]{1,0:T(8,128)(2,1)S(1)}, bf16[384,128]{1,0:T(8,128)(2,1)S(1)}, u32[]{:S(2)}, u32[]{:S(2)}) %collective-permute-start.13) | collective-permute-done | bytes 98336 | tf_op jit(solution)/shard_map/ppermute | solution.py:402
  44.7 5.9 %rebuild.1 = (bf16[4096,768]{1,0:T(8,128)(2,1)S(1)}, bf16[768,256]{1,0:T(8,128)(2,1)S(1)}, f32[8,768]{1,0:T(8,128)S(1)}, f32[8,256]{1,0:T(8,128)S(1)}) custom-call(s32[1,2]{1,0:T(1,128)S(1)} %add_bitcast_fusion.place, bf16[384,128]{1,0:T(8,128)(2,1)S(1)} %get-tuple-element.53.own, bf16[256,128]{1,0:T(8,128)(2,1)S(1)} %collective-permute-done.11.rim, ...), custom_call_target="tpu_custom_call" | custom-call | tf_op jit(solution)/shard_map/rebuild/pallas_call | solution.py:23
  50.6 1.5 %away.1 = (f32[520,256]{1,0:T(8,128)S(1)}, f32[520,256]{1,0:T(8,128)S(1)}, f32[520,256]{1,0:T(8,128)S(1)}, f32[520,256]{1,0:T(8,128)S(1)}) custom-call(s32[1,2]{1,0:T(1,128)S(1)} %add_bitcast_fusion.place, bf16[4096,768]{1,0:T(8,128)(2,1)S(1)} %get-tuple-element.58.stacked, bf16[768,256]{1,0:T(8,128)(2,1)S(1)} %get-tuple-element.59.ratio, ...), custom_call_target="tpu_custom_call" | custom-call | tf_op jit(solution)/shard_map/away/pallas_call | solution.py:23
  52.8 1.5 %kept.1 = (f32[512,256]{1,0:T(8,128)S(1)}, f32[512,256]{1,0:T(8,128)S(1)}, f32[512,256]{1,0:T(8,128)S(1)}, f32[512,256]{1,0:T(8,128)S(1)}) custom-call(s32[1,2]{1,0:T(1,128)S(1)} %add_bitcast_fusion.place, bf16[4096,768]{1,0:T(8,128)(2,1)S(1)} %get-tuple-element.58.stacked, bf16[768,256]{1,0:T(8,128)(2,1)S(1)} %get-tuple-element.59.ratio, ...), custom_call_target="tpu_custom_call" | custom-call | tf_op jit(solution)/shard_map/kept/pallas_call | solution.py:23
  54.4 1.6 %collective-permute-start.16 = (f16[528,256]{1,0:T(8,128)(2,1)S(1)}, f16[528,256]{1,0:T(8,128)(2,1)S(1)}, u32[]{:S(2)}, u32[]{:S(2)}) collective-permute-start(f16[528,256]{1,0:T(8,128)(2,1)S(1)} %convert_element_type.24), channel_id=1, source_target_pairs={{0,8},{4,20},{8,0},{12,28},{16,24},{20,4},{24,16},{28,12},{1,9},{5... | collective-permute-start | bytes 811016 | tf_op jit(solution)/shard_map/ppermute | solution.py:566
  56.1 1.8 %collective-permute-start.17 = (f32[1,768]{1,0:T(1,128)S(1)}, f32[1,768]{1,0:T(1,128)S(1)}, u32[]{:S(2)}, u32[]{:S(2)}) collective-permute-start(f32[1,768]{1,0:T(1,128)S(1)} %slice.11), channel_id=1, source_target_pairs={{0,1},{1,0},{2,3},{3,2},{4,5},{5,4},{6,7},{7,6},{8,9},{9,8},{10,11... | collective-permute-start | bytes 9224 | tf_op jit(solution)/shard_map/ppermute | solution.py:402
  58.1 1.6 %collective-permute-start.21 = (f16[528,256]{1,0:T(8,128)(2,1)S(1)}, f16[528,256]{1,0:T(8,128)(2,1)S(1)}, u32[]{:S(2)}, u32[]{:S(2)}) collective-permute-start(f16[528,256]{1,0:T(8,128)(2,1)S(1)} %convert_element_type.26), channel_id=1, source_target_pairs={{0,8},{4,20},{8,0},{12,28},{16,24},{20,4},{24,16},{28,12},{1,9},{5... | collective-permute-start | bytes 811016 | tf_op jit(solution)/shard_map/ppermute | solution.py:566
  59.8 1.2 %collective-permute-done.16 = f16[528,256]{1,0:T(8,128)(2,1)S(1)} collective-permute-done((f16[528,256]{1,0:T(8,128)(2,1)S(1)}, f16[528,256]{1,0:T(8,128)(2,1)S(1)}, u32[]{:S(2)}, u32[]{:S(2)}) %collective-permute-start.16) | collective-permute-done | bytes 270368 | tf_op jit(solution)/shard_map/ppermute | solution.py:566
  61.1 1.6 %collective-permute-start.23 = (f16[528,256]{1,0:T(8,128)(2,1)S(1)}, f16[528,256]{1,0:T(8,128)(2,1)S(1)}, u32[]{:S(2)}, u32[]{:S(2)}) collective-permute-start(f16[528,256]{1,0:T(8,128)(2,1)S(1)} %convert_element_type.28), channel_id=1, source_target_pairs={{0,16},{4,12},{8,24},{12,4},{16,0},{20,28},{24,8},{28,20},{1,17},{... | collective-permute-start | bytes 811016 | tf_op jit(solution)/shard_map/ppermute | solution.py:566
  62.7 1.8 %collective-permute-start.18 = (f32[1,768]{1,0:T(1,128)S(1)}, f32[1,768]{1,0:T(1,128)S(1)}, u32[]{:S(2)}, u32[]{:S(2)}) collective-permute-start(f32[1,768]{1,0:T(1,128)S(1)} %slice_add_fusion), channel_id=1, source_target_pairs={{0,2},{1,3},{2,0},{3,1},{4,6},{5,7},{6,4},{7,5},{8,10},{9,11},{10,... | collective-permute-start | bytes 9224 | tf_op jit(solution)/shard_map/ppermute | solution.py:402
  64.5 1.3 %collective-permute-done.21 = f16[528,256]{1,0:T(8,128)(2,1)S(1)} collective-permute-done((f16[528,256]{1,0:T(8,128)(2,1)S(1)}, f16[528,256]{1,0:T(8,128)(2,1)S(1)}, u32[]{:S(2)}, u32[]{:S(2)}) %collective-permute-start.21) | collective-permute-done | bytes 270368 | tf_op jit(solution)/shard_map/ppermute | solution.py:566
  65.9 1.4 %collective-permute-done.18 = f32[1,768]{1,0:T(1,128)S(1)} collective-permute-done((f32[1,768]{1,0:T(1,128)S(1)}, f32[1,768]{1,0:T(1,128)S(1)}, u32[]{:S(2)}, u32[]{:S(2)}) %collective-permute-start.18) | collective-permute-done | bytes 3104 | tf_op jit(solution)/shard_map/ppermute | solution.py:402
  67.9 0.9 %total.1 = f32[512,256]{1,0:T(8,128)} custom-call(f32[512,256]{1,0:T(8,128)S(1)} %get-tuple-element.63.kept, f32[520,256]{1,0:T(8,128)S(1)} %collective-permute-done.19.crossed, f32[528,256]{1,0:T(8,128)S(1)} %convert_element_type.27.refs_0_, f32[528,256]{1,0:T(8,128)S(1)} %convert_element_type.29.refs_1_), custom_call_target="tpu_custom_call" | custom-call | tf_op jit(solution)/shard_map/total/pallas_call | solution.py:23
  (62 shorter events, 7.0 us)
Async XLA Ops:
  0.6 20.8 %copy-start.6 = (f32[256]{0:T(256)S(1)}, f32[256]{0:T(256)}, u32[]{:S(2)}) copy-start(f32[256]{0:T(256)} %param.10) | copy-start | bytes 3076
  0.6 20.8 %copy-start.7 = (f32[256]{0:T(256)S(1)}, f32[256]{0:T(256)}, u32[]{:S(2)}) copy-start(f32[256]{0:T(256)} %param.11) | copy-start | bytes 3076
  0.7 26.0 %copy-start.2 = (f32[2,256,768]{2,1,0:T(8,128)S(1)}, f32[2,256,768]{2,1,0:T(8,128)}, u32[]{:S(2)}) copy-start(f32[2,256,768]{2,1,0:T(8,128)} %uniform.1) | copy-start | bytes 4718596
  0.7 26.0 %copy-start.8 = (s32[256]{0:T(256)S(1)}, s32[256]{0:T(256)}, u32[]{:S(2)}) copy-start(s32[256]{0:T(256)} %param.16) | copy-start | bytes 3076
  2.8 17.0 %collective-permute-start = (bf16[336,256]{1,0:T(8,128)(2,1)S(1)}, bf16[336,256]{1,0:T(8,128)(2,1)S(1)}, u32[]{:S(2)}, u32[]{:S(2)}) collective-permute-start(bf16[336,256]{1,0:T(8,128)(2,1)S(1)} %get-tuple-element.40), channel_id=1, source_target_pairs={{0,1},{1,0},{2,3},{3,2},{4,5},{5,4},{6,7},{7,6},{8,9},{9,8},{10,11... | collective-permute-start | bytes 516104 | tf_op jit(solution)/shard_map/ppermute | solution.py:402
  5.9 15.6 %collective-permute-start.1 = (bf16[336,256]{1,0:T(8,128)(2,1)S(1)}, bf16[336,256]{1,0:T(8,128)(2,1)S(1)}, u32[]{:S(2)}, u32[]{:S(2)}) collective-permute-start(bf16[336,256]{1,0:T(8,128)(2,1)S(1)} %get-tuple-element.41), channel_id=1, source_target_pairs={{0,2},{1,3},{2,0},{3,1},{4,6},{5,7},{6,4},{7,5},{8,10},{9,11},{10,... | collective-permute-start | bytes 516104 | tf_op jit(solution)/shard_map/ppermute | solution.py:402
  8.4 19.2 %collective-permute-start.6 = (bf16[336,256]{1,0:T(8,128)(2,1)S(1)}, bf16[336,256]{1,0:T(8,128)(2,1)S(1)}, u32[]{:S(2)}, u32[]{:S(2)}) collective-permute-start(bf16[336,256]{1,0:T(8,128)(2,1)S(1)} %get-tuple-element.45), channel_id=1, source_target_pairs={{0,3},{1,2},{2,1},{3,0},{4,7},{5,6},{6,5},{7,4},{8,11},{9,10},{10,... | collective-permute-start | bytes 516104 | tf_op jit(solution)/shard_map/ppermute | solution.py:402
  10.2 1.2 %collective-permute-start.2 = (f32[4,256]{1,0:T(4,128)S(1)}, f32[4,256]{1,0:T(4,128)S(1)}, u32[]{:S(2)}, u32[]{:S(2)}) collective-permute-start(f32[4,256]{1,0:T(4,128)S(1)} %get-tuple-element.42), channel_id=1, source_target_pairs={{0,4},{4,0},{8,12},{12,8},{16,20},{20,16},{24,28},{28,24},{1,5},{5... | collective-permute-start | bytes 12296 | tf_op jit(solution)/shard_map/ppermute | solution.py:402
  11.5 3.7 %collective-permute-start.3 = (f32[8,256]{1,0:T(8,128)S(1)}, f32[8,256]{1,0:T(8,128)S(1)}, u32[]{:S(2)}, u32[]{:S(2)}) collective-permute-start(f32[8,256]{1,0:T(8,128)S(1)} %pad_maximum_fusion.1.refs_2_), channel_id=1, source_target_pairs={{0,8},{4,12},{8,0},{12,4},{16,24},{20,28},{24,16},{28,20},{1,9},{5... | collective-permute-start | bytes 24584 | tf_op jit(solution)/shard_map/ppermute | solution.py:402
  13.2 6.5 %collective-permute-start.4 = (f32[8,256]{1,0:T(8,128)S(1)}, f32[8,256]{1,0:T(8,128)S(1)}, u32[]{:S(2)}, u32[]{:S(2)}) collective-permute-start(f32[8,256]{1,0:T(8,128)S(1)} %pad_maximum_fusion.1.refs_2_), channel_id=1, source_target_pairs={{0,16},{4,20},{8,24},{12,28},{16,0},{20,4},{24,8},{28,12},{1,17},{... | collective-permute-start | bytes 24584 | tf_op jit(solution)/shard_map/ppermute | solution.py:402
  15.1 4.6 %collective-permute-start.5 = (f32[8,256]{1,0:T(8,128)S(1)}, f32[8,256]{1,0:T(8,128)S(1)}, u32[]{:S(2)}, u32[]{:S(2)}) collective-permute-start(f32[8,256]{1,0:T(8,128)S(1)} %pad_maximum_fusion.1.refs_2_), channel_id=1, source_target_pairs={{0,24},{4,28},{8,16},{12,20},{16,8},{20,12},{24,0},{28,4},{1,25},{... | collective-permute-start | bytes 24584 | tf_op jit(solution)/shard_map/ppermute | solution.py:402
  19.4 7.4 %copy-start.4 = (f32[256,768]{1,0:T(8,128)S(1)}, f32[256,768]{1,0:T(8,128)}, u32[]{:S(2)}) copy-start(f32[256,768]{1,0:T(8,128)} %gauss.1) | copy-start | bytes 2359300
  22.3 5.4 %collective-permute-start.7 = (f32[22,256]{1,0:T(8,128)S(1)}, f32[22,256]{1,0:T(8,128)S(1)}, u32[]{:S(2)}, u32[]{:S(2)}) collective-permute-start(f32[22,256]{1,0:T(8,128)S(1)} %get-tuple-element.46), channel_id=1, source_target_pairs={{0,1},{1,0},{2,3},{3,2},{4,5},{5,4},{6,7},{7,6},{8,9},{9,8},{10,11... | collective-permute-start | bytes 67592 | tf_op jit(solution)/shard_map/ppermute | solution.py:402
  22.4 5.3 %collective-permute-start.8 = (f32[22,256]{1,0:T(8,128)S(1)}, f32[22,256]{1,0:T(8,128)S(1)}, u32[]{:S(2)}, u32[]{:S(2)}) collective-permute-start(f32[22,256]{1,0:T(8,128)S(1)} %get-tuple-element.47), channel_id=1, source_target_pairs={{0,2},{1,3},{2,0},{3,1},{4,6},{5,7},{6,4},{7,5},{8,10},{9,11},{10,... | collective-permute-start | bytes 67592 | tf_op jit(solution)/shard_map/ppermute | solution.py:402
  25.3 5.6 %collective-permute-start.9 = (f32[22,256]{1,0:T(8,128)S(1)}, f32[22,256]{1,0:T(8,128)S(1)}, u32[]{:S(2)}, u32[]{:S(2)}) collective-permute-start(f32[22,256]{1,0:T(8,128)S(1)} %get-tuple-element.48), channel_id=1, source_target_pairs={{0,3},{1,2},{2,1},{3,0},{4,7},{5,6},{6,5},{7,4},{8,11},{9,10},{10,... | collective-permute-start | bytes 67592 | tf_op jit(solution)/shard_map/ppermute | solution.py:402
  26.7 5.7 %copy-start.5 = (bf16[256,256]{1,0:T(8,128)(2,1)S(1)}, bf16[256,256]{1,0:T(8,128)(2,1)}, u32[]{:S(2)}) copy-start(bf16[256,256]{1,0:T(8,128)(2,1)} %encoder.1) | copy-start | bytes 393220
  30.9 13.7 %copy-start.1 = (bf16[256,4096]{1,0:T(8,128)(2,1)S(1)}, bf16[256,4096]{1,0:T(8,128)(2,1)}, u32[]{:S(2)}) copy-start(bf16[256,4096]{1,0:T(8,128)(2,1)} %templates.3) | copy-start | bytes 6291460
  30.9 13.7 %copy-start.3 = (bf16[256,768]{1,0:T(8,128)(2,1)S(1)}, bf16[256,768]{1,0:T(8,128)(2,1)}, u32[]{:S(2)}) copy-start(bf16[256,768]{1,0:T(8,128)(2,1)} %spectrum.1) | copy-start | bytes 1179652
  31.0 1.5 %collective-permute-start.10 = (bf16[384,256]{1,0:T(8,128)(2,1)S(1)}, bf16[384,256]{1,0:T(8,128)(2,1)S(1)}, u32[]{:S(2)}, u32[]{:S(2)}) collective-permute-start(bf16[384,256]{1,0:T(8,128)(2,1)S(1)} %halves.1), channel_id=1, source_target_pairs={{0,4},{4,0},{8,12},{12,8},{16,20},{20,16},{24,28},{28,24},{1,5},{5... | collective-permute-start | bytes 589832 | tf_op jit(solution)/shard_map/ppermute | solution.py:402
  33.7 6.6 %collective-permute-start.12 = (bf16[384,128]{1,0:T(8,128)(2,1)S(1)}, bf16[384,128]{1,0:T(8,128)(2,1)S(1)}, u32[]{:S(2)}, u32[]{:S(2)}) collective-permute-start(bf16[384,128]{1,0:T(8,128)(2,1)S(1)} %get-tuple-element.53.own), channel_id=1, source_target_pairs={{0,1},{1,0},{2,3},{3,2},{4,5},{5,4},{6,7},{7,6},{8,9},{9,8},{10,11... | collective-permute-start | bytes 294920 | tf_op jit(solution)/shard_map/ppermute | solution.py:402
  33.8 10.9 %collective-permute-start.13 = (bf16[384,128]{1,0:T(8,128)(2,1)S(1)}, bf16[384,128]{1,0:T(8,128)(2,1)S(1)}, u32[]{:S(2)}, u32[]{:S(2)}) collective-permute-start(bf16[384,128]{1,0:T(8,128)(2,1)S(1)} %get-tuple-element.53.own), channel_id=1, source_target_pairs={{0,2},{1,3},{2,0},{3,1},{4,6},{5,7},{6,4},{7,5},{8,10},{9,11},{10,... | collective-permute-start | bytes 294920 | tf_op jit(solution)/shard_map/ppermute | solution.py:402
  35.8 8.9 %collective-permute-start.14 = (bf16[384,128]{1,0:T(8,128)(2,1)S(1)}, bf16[384,128]{1,0:T(8,128)(2,1)S(1)}, u32[]{:S(2)}, u32[]{:S(2)}) collective-permute-start(bf16[384,128]{1,0:T(8,128)(2,1)S(1)} %get-tuple-element.53.own), channel_id=1, source_target_pairs={{0,3},{1,2},{2,1},{3,0},{4,7},{5,6},{6,5},{7,4},{8,11},{9,10},{10,... | collective-permute-start | bytes 294920 | tf_op jit(solution)/shard_map/ppermute | solution.py:402
  38.2 2.2 %collective-permute-start.11 = (bf16[256,128]{1,0:T(8,128)(2,1)S(1)}, bf16[256,128]{1,0:T(8,128)(2,1)S(1)}, u32[]{:S(2)}, u32[]{:S(2)}) collective-permute-start(bf16[256,128]{1,0:T(8,128)(2,1)S(1)} %get-tuple-element.54), channel_id=1, source_target_pairs={{0,4},{4,8},{8,12},{12,16},{16,20},{20,24},{24,28},{1,5},{5,9},{9,... | collective-permute-start | bytes 196616 | tf_op jit(solution)/shard_map/ppermute | solution.py:518
  52.1 2.2 %collective-permute-start.15 = (f32[520,256]{1,0:T(8,128)S(1)}, f32[520,256]{1,0:T(8,128)S(1)}, u32[]{:S(2)}, u32[]{:S(2)}) collective-permute-start(f32[520,256]{1,0:T(8,128)S(1)} %get-tuple-element.61), channel_id=1, source_target_pairs={{0,4},{4,0},{8,12},{12,8},{16,20},{20,16},{24,28},{28,24},{1,5},{5... | collective-permute-start | bytes 1597448 | tf_op jit(solution)/shard_map/ppermute | solution.py:402
  52.2 5.8 %collective-permute-start.20 = (f32[520,256]{1,0:T(8,128)S(1)}, f32[520,256]{1,0:T(8,128)S(1)}, u32[]{:S(2)}, u32[]{:S(2)}) collective-permute-start(f32[520,256]{1,0:T(8,128)S(1)} %get-tuple-element.66), channel_id=1, source_target_pairs={{0,4},{4,0},{8,12},{12,8},{16,20},{20,16},{24,28},{28,24},{1,5},{5... | collective-permute-start | bytes 1597448 | tf_op jit(solution)/shard_map/ppermute | solution.py:402
  52.7 8.3 %collective-permute-start.22 = (f32[520,256]{1,0:T(8,128)S(1)}, f32[520,256]{1,0:T(8,128)S(1)}, u32[]{:S(2)}, u32[]{:S(2)}) collective-permute-start(f32[520,256]{1,0:T(8,128)S(1)} %get-tuple-element.68), channel_id=1, source_target_pairs={{0,4},{4,0},{8,12},{12,8},{16,20},{20,16},{24,28},{28,24},{1,5},{5... | collective-permute-start | bytes 1597448 | tf_op jit(solution)/shard_map/ppermute | solution.py:402
  54.4 6.5 %collective-permute-start.16 = (f16[528,256]{1,0:T(8,128)(2,1)S(1)}, f16[528,256]{1,0:T(8,128)(2,1)S(1)}, u32[]{:S(2)}, u32[]{:S(2)}) collective-permute-start(f16[528,256]{1,0:T(8,128)(2,1)S(1)} %convert_element_type.24), channel_id=1, source_target_pairs={{0,8},{4,20},{8,0},{12,28},{16,24},{20,4},{24,16},{28,12},{1,9},{5... | collective-permute-start | bytes 811016 | tf_op jit(solution)/shard_map/ppermute | solution.py:566
  56.0 11.9 %collective-permute-start.19 = (f32[520,256]{1,0:T(8,128)S(1)}, f32[520,256]{1,0:T(8,128)S(1)}, u32[]{:S(2)}, u32[]{:S(2)}) collective-permute-start(f32[520,256]{1,0:T(8,128)S(1)} %get-tuple-element.64), channel_id=1, source_target_pairs={{0,4},{4,0},{8,12},{12,8},{16,20},{20,16},{24,28},{28,24},{1,5},{5... | collective-permute-start | bytes 1597448 | tf_op jit(solution)/shard_map/ppermute | solution.py:402
  56.1 3.6 %collective-permute-start.17 = (f32[1,768]{1,0:T(1,128)S(1)}, f32[1,768]{1,0:T(1,128)S(1)}, u32[]{:S(2)}, u32[]{:S(2)}) collective-permute-start(f32[1,768]{1,0:T(1,128)S(1)} %slice.11), channel_id=1, source_target_pairs={{0,1},{1,0},{2,3},{3,2},{4,5},{5,4},{6,7},{7,6},{8,9},{9,8},{10,11... | collective-permute-start | bytes 9224 | tf_op jit(solution)/shard_map/ppermute | solution.py:402
  58.1 7.7 %collective-permute-start.21 = (f16[528,256]{1,0:T(8,128)(2,1)S(1)}, f16[528,256]{1,0:T(8,128)(2,1)S(1)}, u32[]{:S(2)}, u32[]{:S(2)}) collective-permute-start(f16[528,256]{1,0:T(8,128)(2,1)S(1)} %convert_element_type.26), channel_id=1, source_target_pairs={{0,8},{4,20},{8,0},{12,28},{16,24},{20,4},{24,16},{28,12},{1,9},{5... | collective-permute-start | bytes 811016 | tf_op jit(solution)/shard_map/ppermute | solution.py:566
  61.1 6.7 %collective-permute-start.23 = (f16[528,256]{1,0:T(8,128)(2,1)S(1)}, f16[528,256]{1,0:T(8,128)(2,1)S(1)}, u32[]{:S(2)}, u32[]{:S(2)}) collective-permute-start(f16[528,256]{1,0:T(8,128)(2,1)S(1)} %convert_element_type.28), channel_id=1, source_target_pairs={{0,16},{4,12},{8,24},{12,4},{16,0},{20,28},{24,8},{28,20},{1,17},{... | collective-permute-start | bytes 811016 | tf_op jit(solution)/shard_map/ppermute | solution.py:566
  62.7 4.5 %collective-permute-start.18 = (f32[1,768]{1,0:T(1,128)S(1)}, f32[1,768]{1,0:T(1,128)S(1)}, u32[]{:S(2)}, u32[]{:S(2)}) collective-permute-start(f32[1,768]{1,0:T(1,128)S(1)} %slice_add_fusion), channel_id=1, source_target_pairs={{0,2},{1,3},{2,0},{3,1},{4,6},{5,7},{6,4},{7,5},{8,10},{9,11},{10,... | collective-permute-start | bytes 9224 | tf_op jit(solution)/shard_map/ppermute | solution.py:402
  (1 other events, 1.6 us)

commit v4 on v3

--- a/solution.py
+++ b/solution.py
@@ -64,7 +64,7 @@
     frames_first[...] = turned
     flipped[...] = turned.astype(bf16)
     for step in range(nf):
-        target = own if step == 0 else messages[step - 1]
+        target = own if step == 0 else messages[-step]
         start = pl.multiple_of((here ^ step) * piece, piece)
         target[0:piece, :] = frames_first[pl.ds(start, piece), :].astype(bf16)
         target[piece : piece + TAIL, :] = turned[frames - TAIL :].astype(bf16)
@@ -132,7 +132,7 @@
 
 
 def entry_kernel(nt, nf, place, decay, init, states, stats, *refs):
-    refs = refs[nf - 2 :]
+    refs = refs[1:]
     pairs, messages, (own, clips_wide), (blocks, gains) = (
         refs[: nt // 2],
         refs[nt // 2 : nt // 2 + nf - 1],
@@ -167,7 +167,7 @@
         state = jnp.where(block < lap, passed, state)
     tail = jnp.exp((frames - TAIL) * keep) * state + states[nf : nf + 1, :]
     for step in range(nf):
-        target = own if step == 0 else messages[step - 1]
+        target = own if step == 0 else messages[-step]
         other = here ^ step
         power = jnp.exp((other * piece).astype(f32) * keep)
         target[0:1, :] = power * state + states[pl.ds(other, 1), :]
@@ -220,8 +220,8 @@
     powers = (1 + lax.broadcasted_iota(jnp.int32, (segment, 1), 0)).astype(f32)
     normed[:, rows:, :] = jnp.zeros_like(normed[:, rows:, :])
     for step in range(nf):
-        state = own_state if step == 0 else arrivals[step - 1]
-        block = own if step == 0 else messages[step - 1]
+        state = own_state if step == 0 else arrivals[-step]
+        block = own if step == 0 else messages[-step]
         for part in range(bins // LANES):
             at = step * (bins // LANES) + part
             lanes = slice(part * LANES, (part + 1) * LANES)
@@ -260,8 +260,8 @@
         if step == 0:
             weights = encoder[...]
         else:
-            mine = messages[step - 1][rows:, :]
-            other = halves[(step - 1) * half : step * half, :]
+            mine = messages[-step][rows:, :]
+            other = halves[(nf - 1 - step) * half : (nf - step) * half, :]
             lower = jnp.where(core == 0, mine, other)
             upper = jnp.where(core == 0, other, mine)
             weights = jnp.concatenate([lower, upper], axis=0)
@@ -287,11 +287,10 @@
 
 
 def rebuild_kernel(nt, nf, place, own, rim, clips, templates, spectrum, stats, *refs):
-    messages, arrivals, (stacked, ratio, sums, bound), (extended, heads, recon) = (
+    messages, arrivals, (stacked, ratio, sums, bound, *away, extended, heads, recon) = (
         refs[: nf - 1],
         refs[nf - 1 : 2 * nf - 2],
-        refs[2 * nf - 2 : 2 * nf + 2],
-        refs[2 * nf + 2 :],
+        refs[2 * nf - 2 :],
     )
     bins, frames = spectrum.shape
     here = place[0, 0]
@@ -300,7 +299,7 @@
     full, rest = piece // LANES, piece % LANES
     extended[:, 0:LANES] = rim[...].astype(f32)
     for step in range(nf):
-        source = own if step == 0 else messages[step - 1]
+        source = own if step == 0 else messages[-step]
         for index in range(nf):
 
             @pl.when((here ^ step) == index)
@@ -333,13 +332,13 @@
         sums[2:3, row * bins : (row + 1) * bins] = total[at : at + 1, :]
     ids = jnp.broadcast_to(clips[...], (L, LANES + frames))
     shifted = pltpu.roll(ids, 0, 1, stride=1, stride_axis=0)
-    valid = jnp.where(shifted == ids, 1.0, 0.0)[:, LANES:]
+    valid = jnp.where(shifted == ids, 1.0, 0.0)[:, LANES:].astype(bf16)
     group = 32
     for low in range(0, topics, group):
         for topic in range(low, low + group):
             row = jnp.broadcast_to(extended[topic : topic + 1, :], (L, LANES + frames))
             lagged = pltpu.roll(row, 0, 1, stride=1, stride_axis=0)[:, LANES:]
-            stacked[topic * L : (topic + 1) * L, :] = (lagged * valid).astype(bf16)
+            stacked[topic * L : (topic + 1) * L, :] = lagged.astype(bf16) * valid
         part = slice(low * L, (low + group) * L)
         left = jnp.concatenate([templates[:, part], heads[:, part]], axis=0)
         product = jnp.dot(left, stacked[part, :], preferred_element_type=f32)
@@ -358,20 +357,25 @@
     bound[...] = jnp.broadcast_to(jnp.max(reach, axis=1, keepdims=True), bound.shape)
     sums[0:1, :] = recon_sum
     sums[1:2, :] = jnp.sum(spectral * jnp.log(rebuilt), axis=0, keepdims=True)
-
-
-def product_kernel(side, routed, place, stacked, ratio, bound, *targets):
-    height = targets[0].shape[0] - 8 * side
+    products(1, nt, place, stacked, ratio, away)
+    for target in away:
+        target[target.shape[0] - 8 :, :] = bound[...]
+
+
+def products(side, nt, place, stacked, ratio, targets):
+    height = stacked.shape[0] // nt
     lap = place[0, 1]
     hop = 1 + ((lap ^ side) & 1)
-    order = (3, hop, 3 ^ hop, 0) if routed else (*range(1, len(targets)), 0)
+    order = (3, hop, 3 ^ hop, 0) if nt == 8 else (*range(1, len(targets)), 0)
     for step, target in zip(order, targets):
         at = pl.multiple_of((lap ^ (2 * step + side)) * height, height)
         target[0:height, :] = jnp.dot(
             stacked[pl.ds(at, height), :], ratio[...], preferred_element_type=f32
         )
-        if side:
-            target[height:, :] = bound[...]
+
+
+def kept_kernel(nt, place, stacked, ratio, *targets):
+    products(0, nt, place, stacked, ratio, targets)
 
 
 def message_kernel(bound, kept, crossed, *refs):
@@ -420,6 +424,7 @@
     piece = frames // nf
     rows = piece + TAIL
     width = -(-rows // LANES) * LANES
+    far_first = range(nf - 1, 0, -1)
     place = jnp.stack([lax.axis_index("freq"), lax.axis_index("tm")]).astype(jnp.int32)[None]
     decay = decay_rate[None]
     state_rows = -(-(nf + 1) // 8) * 8
@@ -446,7 +451,7 @@
         small[None],
         scalars=1,
     )
-    messages = [exchanged(messages[step - 1], "freq", step) for step in range(1, nf)]
+    messages = [exchanged(messages[-step], "freq", step) for step in far_first]
     pair = jnp.concatenate([tm_message, exchanged(tm_message, "tm", 1)], axis=0)
     pairs = [pair] + [exchanged(pair, "tm", step) for step in range(2, nt, 2)]
     stat_rows = columns // bins + frames // bins
@@ -464,11 +469,11 @@
         init_state[None],
         states,
         stats,
-        *messages[: nf - 2],
+        messages[0],
         *pairs,
         scalars=1,
     )
-    arrivals = [exchanged(arrivals[step - 1], "freq", step) for step in range(1, nf)]
+    arrivals = [exchanged(arrivals[-step], "freq", step) for step in far_first]
     noises = call(
         functools.partial(noise_kernel, nf),
         "noise",
@@ -514,12 +519,14 @@
         *messages,
         scalars=1,
     )
-    shares = [exchanged(packed, "freq", step) for step in range(1, nf)]
+    shares = [exchanged(packed, "freq", step) for step in far_first]
     rim = lax.ppermute(tail, "tm", [(index, index + 1) for index in range(nt - 1)])
-    stacked, ratio, sums, bound = call(
+    height = columns // nt
+    stacked, ratio, sums, bound, *away = call(
         functools.partial(rebuild_kernel, nt, nf),
         "rebuild",
-        [((columns, frames), bf16), ((frames, bins), bf16), ((8, frames), f32), ((8, bins), f32)],
+        [((columns, frames), bf16), ((frames, bins), bf16), ((8, frames), f32), ((8, bins), f32)]
+        + [((height + 8, bins), f32)] * (nt // 2),
         [((topics, LANES + frames), f32), ((16, columns), bf16), ((bins + 16, frames), f32)],
         place,
         packed,
@@ -532,23 +539,17 @@
         *arrivals,
         scalars=1,
     )
-    height = columns // nt
-    routed = nt == 8
     steps = [1 << power for power in range(nf.bit_length() - 1)]
     log_sum = sums[1:2] + exchanged(sums[1:2], "freq", steps[0])
-    away, kept = (
-        call(
-            functools.partial(product_kernel, side, routed),
-            name,
-            [((height + 8 * side, bins), f32)] * (nt // 2),
-            [],
-            place,
-            stacked,
-            ratio,
-            bound,
-            scalars=1,
-        )
-        for side, name in ((1, "away"), (0, "kept"))
+    kept = call(
+        functools.partial(kept_kernel, nt),
+        "kept",
+        [((height, bins), f32)] * (nt // 2),
+        [],
+        place,
+        stacked,
+        ratio,
+        scalars=1,
     )
     crossed = [exchanged(block, "tm", 1) for block in away]
 
@@ -565,7 +566,7 @@
         )
         return lax.ppermute(message.astype(jnp.float16), "tm", pairs).astype(f32)
 
-    if routed:
+    if nt == 8:
         first = [(lap, lap ^ (2 << (lap & 1))) for lap in range(nt)]
         second = [(lap, lap ^ (4 >> (lap & 1))) for lap in range(nt)]
         carried = sent(0, first)

time: 69 us -> 66.1 us (0.958)
  waiting for transfers between devices: 16.4 us -> 14.1 us
  Pallas kernels: 15.9 us -> 14.3 us
  starting transfers between devices: 31 us -> 32.1 us
    pallas_call x15 -> x14, Pallas kernels: 15.9 us -> 14.3 us  [call(): pl.pallas_call(kernel, name=name, out_shape=[jax.ShapeDtypeStruct(shape,...]
    ppermute x3, waiting for transfers between devices: 2.44 us -> 0.9 us  [sent(): return lax.ppermute(message.astype(jnp.float16), 'tm', pairs).astype(f32)]
    ppermute x20, starting transfers between devices: 25.1 us -> 25.9 us  [exchanged(): lax.ppermute(value, axis, [(index, index ^ step) for index in range(size)])]
    ppermute x20, waiting for transfers between devices: 13 us -> 12.3 us  [exchanged(): lax.ppermute(value, axis, [(index, index ^ step) for index in range(size)])]
  transfers between devices with their start and end apart: 24 -> 24, of which waited for: 11 -> 12; matrix products, arithmetic and copies ran while one was open for 2% -> 2% of each run, Pallas kernels for 8% -> 8%
where the time goes in v4:
time: 66.1 us; the launch traced here: 65.9 us
  starting transfers between devices  32.1 us (49%)
  Pallas kernels  14.3 us (22%)
  waiting for transfers between devices  14.1 us (21%)
  other arithmetic  2.88 us (4%)
  local copies, waits for them, and re-layouts  1.63 us (2%)
  between operations  0.9 us (1%)
    ppermute x20, starting transfers between devices, exchanged(): lax.ppermute(value, axis, [(index, index ^ step) for index in range(size)])  25.9 us
    pallas_call x14, Pallas kernels, call(): pl.pallas_call(kernel, name=name, out_shape=[jax.ShapeDtypeStruct(shape,...  14.3 us
    ppermute x20, waiting for transfers between devices, exchanged(): lax.ppermute(value, axis, [(index, index ^ step) for index in range(size)])  12.3 us
    ppermute x3, starting transfers between devices, sent(): return lax.ppermute(message.astype(jnp.float16), 'tm', pairs).astype(f32)  4.99 us
    unnamed x18, local copies, waits for them, and re-layouts  1.63 us
  transfers between devices with their start and end apart: 24, of which 12 were waited for; matrix products, arithmetic and copies ran while one was open for 2% of the time, Pallas kernels for 8%

profile of v4, /device:TPU:0, one launch (start us, length us, event | category | flops | bytes accessed | tf_op | source)
XLA Modules:
  0.0 65.9 jit_solution(4861895044889964291)
XLA Ops:
  0.7 1.2 %pad_maximum_fusion.both = bf16[256,1024]{1,0:T(8,128)(2,1)S(1)} fusion(bf16[256,256]{1,0:T(8,128)(2,1)} %encoder.1, bf16[256,768]{1,0:T(8,128)(2,1)} %spectrum.1), kind=kLoop, calls=%fused_computation | loop fusion | flops 1048576 | bytes 1048576 | tf_op jit(solution)/shard_map/concatenate | solution.py:440
  2.0 0.8 %pieces.1 = (bf16[336,256]{1,0:T(8,128)(2,1)S(1)}, bf16[336,256]{1,0:T(8,128)(2,1)S(1)}, bf16[336,256]{1,0:T(8,128)(2,1)S(1)}, bf16[208,256]{1,0:T(8,128)(2,1)S(...) custom-call(s32[1,2]{1,0:T(1,128)S(1)} %add_bitcast_fusion.place, bf16[256,1024]{1,0:T(8,128)(2,1)S(1)} %pad_maximum_fusion.both), custom_call_target="tpu_custom_call" | custom-call | tf_op jit(solution)/shard_map/pieces/pallas_call | solution.py:23
  2.8 5.1 %collective-permute-start = (bf16[336,256]{1,0:T(8,128)(2,1)S(1)}, bf16[336,256]{1,0:T(8,128)(2,1)S(1)}, u32[]{:S(2)}, u32[]{:S(2)}) collective-permute-start(bf16[336,256]{1,0:T(8,128)(2,1)S(1)} %get-tuple-element.40), channel_id=1, source_target_pairs={{0,3},{1,2},{2,1},{3,0},{4,7},{5,6},{6,5},{7,4},{8,11},{9,10},{10,... | collective-permute-start | bytes 516104 | tf_op jit(solution)/shard_map/ppermute | solution.py:406
  8.5 0.7 %convert_add_fusion = f32[1024]{0:T(1024)S(1)} fusion(s32[768]{0:T(1024)} %param.12, f32[256]{0:T(256)} %param.10), kind=kLoop, calls=%fused_computation.2 | loop fusion | flops 2048 | bytes 8192 | tf_op jit(solution)/shard_map/add | solution.py:443
  9.2 1.1 %summary.1 = (f32[208,128]{1,0:T(8,128)S(1)}, f32[8,256]{1,0:T(8,128)S(1)}, f32[4,256]{1,0:T(4,128)S(1)}) custom-call(s32[1,2]{1,0:T(1,128)S(1)} %add_bitcast_fusion.place, bf16[768,256]{1,0:T(8,128)(2,1)S(1)} %get-tuple-element.37.flipped, f32[1,1024]{1,0:T(1,128)S(1)} %bitcast.8), custom_call_target="tpu_custom_call" | custom-call | tf_op jit(solution)/shard_map/summary/pallas_call | solution.py:23
  10.4 1.2 %collective-permute-done.1 = f32[4,256]{1,0:T(4,128)S(1)} collective-permute-done((f32[4,256]{1,0:T(4,128)S(1)}, f32[4,256]{1,0:T(4,128)S(1)}, u32[]{:S(2)}, u32[]{:S(2)}) %collective-permute-start.1) | collective-permute-done | bytes 4128 | tf_op jit(solution)/shard_map/ppermute | solution.py:406
  11.5 2.6 %collective-permute-start.4 = (f32[8,256]{1,0:T(8,128)S(1)}, f32[8,256]{1,0:T(8,128)S(1)}, u32[]{:S(2)}, u32[]{:S(2)}) collective-permute-start(f32[8,256]{1,0:T(8,128)S(1)} %pad_maximum_fusion.1.refs_1_), channel_id=1, source_target_pairs={{0,24},{4,28},{8,16},{12,20},{16,8},{20,12},{24,0},{28,4},{1,25},{... | collective-permute-start | bytes 24584 | tf_op jit(solution)/shard_map/ppermute | solution.py:406
  14.6 1.5 %collective-permute-done.4.refs_4_ = f32[8,256]{1,0:T(8,128)S(1)} collective-permute-done((f32[8,256]{1,0:T(8,128)S(1)}, f32[8,256]{1,0:T(8,128)S(1)}, u32[]{:S(2)}, u32[]{:S(2)}) %collective-permute-start.4) | collective-permute-done | bytes 8224 | tf_op jit(solution)/shard_map/ppermute | solution.py:406
  16.1 1.6 %collective-permute-start.2 = (f32[8,256]{1,0:T(8,128)S(1)}, f32[8,256]{1,0:T(8,128)S(1)}, u32[]{:S(2)}, u32[]{:S(2)}) collective-permute-start(f32[8,256]{1,0:T(8,128)S(1)} %pad_maximum_fusion.1.refs_1_), channel_id=1, source_target_pairs={{0,8},{4,12},{8,0},{12,4},{16,24},{20,28},{24,16},{28,20},{1,9},{5... | collective-permute-start | bytes 24584 | tf_op jit(solution)/shard_map/ppermute | solution.py:406
  17.7 1.6 %copy-done = bf16[256,4096]{1,0:T(8,128)(2,1)S(1)} copy-done((bf16[256,4096]{1,0:T(8,128)(2,1)S(1)}, bf16[256,4096]{1,0:T(8,128)(2,1)}, u32[]{:S(2)}) %copy-start) | copy-done | bytes 2097176
  19.8 0.8 %entry.1 = (f32[22,256]{1,0:T(8,128)S(1)}, f32[22,256]{1,0:T(8,128)S(1)}, f32[22,256]{1,0:T(8,128)S(1)}, f32[3,256]{1,0:T(4,128)S(1)}, f32[1,896]{1,0:T(1,128)S(1)}) custom-call(s32[1,2]{1,0:T(1,128)S(1)} %add_bitcast_fusion.place, f32[1,256]{1,0:T(1,128)S(1)} %bitcast.9, f32[1,256]{1,0:T(1,128)S(1)} %bitcast.10, f32[8,256]{1,0:T(8,128)S(1)} %get-tuple-element.38.states, ...), custom_call_target="tpu_custom_call" | custom-call | tf_op jit(solution)/shard_map/entry/pallas_call | solution.py:23
  20.6 3.8 %collective-permute-start.7 = (f32[22,256]{1,0:T(8,128)S(1)}, f32[22,256]{1,0:T(8,128)S(1)}, u32[]{:S(2)}, u32[]{:S(2)}) collective-permute-start(f32[22,256]{1,0:T(8,128)S(1)} %get-tuple-element.46), channel_id=1, source_target_pairs={{0,3},{1,2},{2,1},{3,0},{4,7},{5,6},{6,5},{7,4},{8,11},{9,10},{10,... | collective-permute-start | bytes 67592 | tf_op jit(solution)/shard_map/ppermute | solution.py:406
  25.1 0.9 %noise.1 = (f32[256,256]{1,0:T(8,128)S(1)}, f32[256,256]{1,0:T(8,128)S(1)}, f32[256,256]{1,0:T(8,128)S(1)}, f32[256,256]{1,0:T(8,128)S(1)}) custom-call(s32[1,2]{1,0:T(1,128)S(1)} %add_bitcast_fusion.place, f32[256,768]{1,0:T(8,128)S(1)} %copy-done.4, f32[2,256,768]{2,1,0:T(8,128)S(1)} %copy-done.2, s32[1,256]{1,0:T(1,128)S(1)} %bitcast.11), custom_call_target="tpu_custom_call" | custom-call | tf_op jit(solution)/shard_map/noise/pallas_call | solution.py:23
  26.3 2.8 %collective-permute-done.8.refs_4_.refs_1_ = f32[22,256]{1,0:T(8,128)S(1)} collective-permute-done((f32[22,256]{1,0:T(8,128)S(1)}, f32[22,256]{1,0:T(8,128)S(1)}, u32[]{:S(2)}, u32[]{:S(2)}) %collective-permute-start.8) | collective-permute-done | bytes 22560 | tf_op jit(solution)/shard_map/ppermute | solution.py:406
  29.3 0.7 %normed.1 = bf16[4,256,256]{2,1,0:T(8,128)(2,1)S(1)} custom-call(bf16[208,256]{1,0:T(8,128)(2,1)S(1)} %get-tuple-element.36.own, f32[3,256]{1,0:T(4,128)S(1)} %get-tuple-element.42.own_state, f32[208,128]{1,0:T(8,128)S(1)} %get-tuple-element.43.gains, bf16[336,256]{1,0:T(8,128)(2,1)S(1)} %collective-permute-done.refs_0_.refs_3_, ...), custom_call_target="tpu_custom_call" | custom-call | tf_op jit(solution)/shard_map/normed/pallas_call | solution.py:23
  30.0 0.7 %collective-permute-done.10.halves = bf16[384,256]{1,0:T(8,128)(2,1)S(1)} collective-permute-done((bf16[384,256]{1,0:T(8,128)(2,1)S(1)}, bf16[384,256]{1,0:T(8,128)(2,1)S(1)}, u32[]{:S(2)}, u32[]{:S(2)}) %collective-permute-start.10) | collective-permute-done | bytes 196640 | tf_op jit(solution)/shard_map/ppermute | solution.py:406
  30.7 1.3 %sampler.1 = (bf16[384,128]{1,0:T(8,128)(2,1)S(1)}, bf16[256,128]{1,0:T(8,128)(2,1)S(1)}) custom-call(s32[1,2]{1,0:T(1,128)S(1)} %add_bitcast_fusion.place, bf16[4,256,256]{2,1,0:T(8,128)(2,1)S(1)} %normed.1, bf16[256,256]{1,0:T(8,128)(2,1)S(1)} %copy-done.5, bf16[384,256]{1,0:T(8,128)(2,1)S(1)} %collective-permute-done.10.halves, ...), custom_call_target="tpu_custom_call" | custom-call | tf_op jit(solution)/shard_map/sampler/pallas_call | solution.py:23
  32.0 2.1 %collective-permute-start.13 = (bf16[384,128]{1,0:T(8,128)(2,1)S(1)}, bf16[384,128]{1,0:T(8,128)(2,1)S(1)}, u32[]{:S(2)}, u32[]{:S(2)}) collective-permute-start(bf16[384,128]{1,0:T(8,128)(2,1)S(1)} %get-tuple-element.53.own), channel_id=1, source_target_pairs={{0,2},{1,3},{2,0},{3,1},{4,6},{5,7},{6,4},{7,5},{8,10},{9,11},{10,... | collective-permute-start | bytes 294920 | tf_op jit(solution)/shard_map/ppermute | solution.py:406
  34.1 2.3 %collective-permute-start.12 = (bf16[384,128]{1,0:T(8,128)(2,1)S(1)}, bf16[384,128]{1,0:T(8,128)(2,1)S(1)}, u32[]{:S(2)}, u32[]{:S(2)}) collective-permute-start(bf16[384,128]{1,0:T(8,128)(2,1)S(1)} %get-tuple-element.53.own), channel_id=1, source_target_pairs={{0,3},{1,2},{2,1},{3,0},{4,7},{5,6},{6,5},{7,4},{8,11},{9,10},{10,... | collective-permute-start | bytes 294920 | tf_op jit(solution)/shard_map/ppermute | solution.py:406
  36.4 1.3 %collective-permute-start.11 = (bf16[256,128]{1,0:T(8,128)(2,1)S(1)}, bf16[256,128]{1,0:T(8,128)(2,1)S(1)}, u32[]{:S(2)}, u32[]{:S(2)}) collective-permute-start(bf16[256,128]{1,0:T(8,128)(2,1)S(1)} %get-tuple-element.54), channel_id=1, source_target_pairs={{0,4},{4,8},{8,12},{12,16},{16,20},{20,24},{24,28},{1,5},{5,9},{9,... | collective-permute-start | bytes 196616 | tf_op jit(solution)/shard_map/ppermute | solution.py:523
  37.7 0.9 %collective-permute-done.11.rim = bf16[256,128]{1,0:T(8,128)(2,1)S(1)} collective-permute-done((bf16[256,128]{1,0:T(8,128)(2,1)S(1)}, bf16[256,128]{1,0:T(8,128)(2,1)S(1)}, u32[]{:S(2)}, u32[]{:S(2)}) %collective-permute-start.11) | collective-permute-done | bytes 65568 | tf_op jit(solution)/shard_map/ppermute | solution.py:523
  39.0 3.7 %collective-permute-done.12.refs_0_ = bf16[384,128]{1,0:T(8,128)(2,1)S(1)} collective-permute-done((bf16[384,128]{1,0:T(8,128)(2,1)S(1)}, bf16[384,128]{1,0:T(8,128)(2,1)S(1)}, u32[]{:S(2)}, u32[]{:S(2)}) %collective-permute-start.12) | collective-permute-done | bytes 98336 | tf_op jit(solution)/shard_map/ppermute | solution.py:406
  42.6 5.8 %rebuild.1 = (bf16[4096,768]{1,0:T(8,128)(2,1)S(1)}, bf16[768,256]{1,0:T(8,128)(2,1)S(1)}, f32[8,768]{1,0:T(8,128)S(1)}, f32[8,256]{1,0:T(8,128)S(1)}, f32[520,2...) custom-call(s32[1,2]{1,0:T(1,128)S(1)} %add_bitcast_fusion.place, ...), custom_call_target="tpu_custom_call" | custom-call | tf_op jit(solution)/shard_map/rebuild/pallas_call | solution.py:23
  49.1 1.5 %kept.1 = (f32[512,256]{1,0:T(8,128)S(1)}, f32[512,256]{1,0:T(8,128)S(1)}, f32[512,256]{1,0:T(8,128)S(1)}, f32[512,256]{1,0:T(8,128)S(1)}) custom-call(s32[1,2]{1,0:T(1,128)S(1)} %add_bitcast_fusion.place, bf16[4096,768]{1,0:T(8,128)(2,1)S(1)} %get-tuple-element.58.stacked, bf16[768,256]{1,0:T(8,128)(2,1)S(1)} %get-tuple-element.59.ratio), custom_call_target="tpu_custom_call" | custom-call | tf_op jit(solution)/shard_map/kept/pallas_call | solution.py:23
  50.8 1.6 %collective-permute-start.16 = (f16[528,256]{1,0:T(8,128)(2,1)S(1)}, f16[528,256]{1,0:T(8,128)(2,1)S(1)}, u32[]{:S(2)}, u32[]{:S(2)}) collective-permute-start(f16[528,256]{1,0:T(8,128)(2,1)S(1)} %convert_element_type.24), channel_id=1, source_target_pairs={{0,8},{4,20},{8,0},{12,28},{16,24},{20,4},{24,16},{28,12},{1,9},{5... | collective-permute-start | bytes 811016 | tf_op jit(solution)/shard_map/ppermute | solution.py:567
  52.8 1.9 %collective-permute-start.17 = (f32[1,768]{1,0:T(1,128)S(1)}, f32[1,768]{1,0:T(1,128)S(1)}, u32[]{:S(2)}, u32[]{:S(2)}) collective-permute-start(f32[1,768]{1,0:T(1,128)S(1)} %slice.11), channel_id=1, source_target_pairs={{0,1},{1,0},{2,3},{3,2},{4,5},{5,4},{6,7},{7,6},{8,9},{9,8},{10,11... | collective-permute-start | bytes 9224 | tf_op jit(solution)/shard_map/ppermute | solution.py:406
  54.8 1.6 %collective-permute-start.21 = (f16[528,256]{1,0:T(8,128)(2,1)S(1)}, f16[528,256]{1,0:T(8,128)(2,1)S(1)}, u32[]{:S(2)}, u32[]{:S(2)}) collective-permute-start(f16[528,256]{1,0:T(8,128)(2,1)S(1)} %convert_element_type.26), channel_id=1, source_target_pairs={{0,8},{4,20},{8,0},{12,28},{16,24},{20,4},{24,16},{28,12},{1,9},{5... | collective-permute-start | bytes 811016 | tf_op jit(solution)/shard_map/ppermute | solution.py:567
  56.4 0.9 %collective-permute-done.16 = f16[528,256]{1,0:T(8,128)(2,1)S(1)} collective-permute-done((f16[528,256]{1,0:T(8,128)(2,1)S(1)}, f16[528,256]{1,0:T(8,128)(2,1)S(1)}, u32[]{:S(2)}, u32[]{:S(2)}) %collective-permute-start.16) | collective-permute-done | bytes 270368 | tf_op jit(solution)/shard_map/ppermute | solution.py:567
  57.5 1.9 %collective-permute-start.23 = (f16[528,256]{1,0:T(8,128)(2,1)S(1)}, f16[528,256]{1,0:T(8,128)(2,1)S(1)}, u32[]{:S(2)}, u32[]{:S(2)}) collective-permute-start(f16[528,256]{1,0:T(8,128)(2,1)S(1)} %convert_element_type.28), channel_id=1, source_target_pairs={{0,16},{4,12},{8,24},{12,4},{16,0},{20,28},{24,8},{28,20},{1,17},{... | collective-permute-start | bytes 811016 | tf_op jit(solution)/shard_map/ppermute | solution.py:567
  59.4 3.4 %collective-permute-start.18 = (f32[1,768]{1,0:T(1,128)S(1)}, f32[1,768]{1,0:T(1,128)S(1)}, u32[]{:S(2)}, u32[]{:S(2)}) collective-permute-start(f32[1,768]{1,0:T(1,128)S(1)} %slice_add_fusion), channel_id=1, source_target_pairs={{0,2},{1,3},{2,0},{3,1},{4,6},{5,7},{6,4},{7,5},{8,10},{9,11},{10,... | collective-permute-start | bytes 9224 | tf_op jit(solution)/shard_map/ppermute | solution.py:406
  62.8 1.5 %collective-permute-done.18 = f32[1,768]{1,0:T(1,128)S(1)} collective-permute-done((f32[1,768]{1,0:T(1,128)S(1)}, f32[1,768]{1,0:T(1,128)S(1)}, u32[]{:S(2)}, u32[]{:S(2)}) %collective-permute-start.18) | collective-permute-done | bytes 3104 | tf_op jit(solution)/shard_map/ppermute | solution.py:406
  65.0 0.9 %total.1 = f32[512,256]{1,0:T(8,128)} custom-call(f32[512,256]{1,0:T(8,128)S(1)} %get-tuple-element.63.kept, f32[520,256]{1,0:T(8,128)S(1)} %collective-permute-done.19.crossed, f32[528,256]{1,0:T(8,128)S(1)} %convert_element_type.27.refs_0_, f32[528,256]{1,0:T(8,128)S(1)} %convert_element_type.29.refs_1_), custom_call_target="tpu_custom_call" | custom-call | tf_op jit(solution)/shard_map/total/pallas_call | solution.py:23
  (61 shorter events, 5.6 us)
Async XLA Ops:
  0.6 19.1 %copy-start.6 = (f32[256]{0:T(256)S(1)}, f32[256]{0:T(256)}, u32[]{:S(2)}) copy-start(f32[256]{0:T(256)} %param.10) | copy-start | bytes 3076
  0.6 19.1 %copy-start.7 = (f32[256]{0:T(256)S(1)}, f32[256]{0:T(256)}, u32[]{:S(2)}) copy-start(f32[256]{0:T(256)} %param.11) | copy-start | bytes 3076
  0.7 24.3 %copy-start.2 = (f32[2,256,768]{2,1,0:T(8,128)S(1)}, f32[2,256,768]{2,1,0:T(8,128)}, u32[]{:S(2)}) copy-start(f32[2,256,768]{2,1,0:T(8,128)} %uniform.1) | copy-start | bytes 4718596
  0.7 24.3 %copy-start.8 = (s32[256]{0:T(256)S(1)}, s32[256]{0:T(256)}, u32[]{:S(2)}) copy-start(s32[256]{0:T(256)} %param.16) | copy-start | bytes 3076
  2.8 17.0 %collective-permute-start = (bf16[336,256]{1,0:T(8,128)(2,1)S(1)}, bf16[336,256]{1,0:T(8,128)(2,1)S(1)}, u32[]{:S(2)}, u32[]{:S(2)}) collective-permute-start(bf16[336,256]{1,0:T(8,128)(2,1)S(1)} %get-tuple-element.40), channel_id=1, source_target_pairs={{0,3},{1,2},{2,1},{3,0},{4,7},{5,6},{6,5},{7,4},{8,11},{9,10},{10,... | collective-permute-start | bytes 516104 | tf_op jit(solution)/shard_map/ppermute | solution.py:406
  7.9 18.1 %collective-permute-start.5 = (bf16[336,256]{1,0:T(8,128)(2,1)S(1)}, bf16[336,256]{1,0:T(8,128)(2,1)S(1)}, u32[]{:S(2)}, u32[]{:S(2)}) collective-permute-start(bf16[336,256]{1,0:T(8,128)(2,1)S(1)} %get-tuple-element.44), channel_id=1, source_target_pairs={{0,2},{1,3},{2,0},{3,1},{4,6},{5,7},{6,4},{7,5},{8,10},{9,11},{10,... | collective-permute-start | bytes 516104 | tf_op jit(solution)/shard_map/ppermute | solution.py:406
  7.9 18.1 %collective-permute-start.6 = (bf16[336,256]{1,0:T(8,128)(2,1)S(1)}, bf16[336,256]{1,0:T(8,128)(2,1)S(1)}, u32[]{:S(2)}, u32[]{:S(2)}) collective-permute-start(bf16[336,256]{1,0:T(8,128)(2,1)S(1)} %get-tuple-element.45), channel_id=1, source_target_pairs={{0,1},{1,0},{2,3},{3,2},{4,5},{5,4},{6,7},{7,6},{8,9},{9,8},{10,11... | collective-permute-start | bytes 516104 | tf_op jit(solution)/shard_map/ppermute | solution.py:406
  10.3 1.2 %collective-permute-start.1 = (f32[4,256]{1,0:T(4,128)S(1)}, f32[4,256]{1,0:T(4,128)S(1)}, u32[]{:S(2)}, u32[]{:S(2)}) collective-permute-start(f32[4,256]{1,0:T(4,128)S(1)} %get-tuple-element.41), channel_id=1, source_target_pairs={{0,4},{4,0},{8,12},{12,8},{16,20},{20,16},{24,28},{28,24},{1,5},{5... | collective-permute-start | bytes 12296 | tf_op jit(solution)/shard_map/ppermute | solution.py:406
  11.5 4.5 %collective-permute-start.4 = (f32[8,256]{1,0:T(8,128)S(1)}, f32[8,256]{1,0:T(8,128)S(1)}, u32[]{:S(2)}, u32[]{:S(2)}) collective-permute-start(f32[8,256]{1,0:T(8,128)S(1)} %pad_maximum_fusion.1.refs_1_), channel_id=1, source_target_pairs={{0,24},{4,28},{8,16},{12,20},{16,8},{20,12},{24,0},{28,4},{1,25},{... | collective-permute-start | bytes 24584 | tf_op jit(solution)/shard_map/ppermute | solution.py:406
  14.1 5.5 %collective-permute-start.3 = (f32[8,256]{1,0:T(8,128)S(1)}, f32[8,256]{1,0:T(8,128)S(1)}, u32[]{:S(2)}, u32[]{:S(2)}) collective-permute-start(f32[8,256]{1,0:T(8,128)S(1)} %pad_maximum_fusion.1.refs_1_), channel_id=1, source_target_pairs={{0,16},{4,20},{8,24},{12,28},{16,0},{20,4},{24,8},{28,12},{1,17},{... | collective-permute-start | bytes 24584 | tf_op jit(solution)/shard_map/ppermute | solution.py:406
  16.1 3.7 %collective-permute-start.2 = (f32[8,256]{1,0:T(8,128)S(1)}, f32[8,256]{1,0:T(8,128)S(1)}, u32[]{:S(2)}, u32[]{:S(2)}) collective-permute-start(f32[8,256]{1,0:T(8,128)S(1)} %pad_maximum_fusion.1.refs_1_), channel_id=1, source_target_pairs={{0,8},{4,12},{8,0},{12,4},{16,24},{20,28},{24,16},{28,20},{1,9},{5... | collective-permute-start | bytes 24584 | tf_op jit(solution)/shard_map/ppermute | solution.py:406
  19.3 5.7 %copy-start.4 = (f32[256,768]{1,0:T(8,128)S(1)}, f32[256,768]{1,0:T(8,128)}, u32[]{:S(2)}) copy-start(f32[256,768]{1,0:T(8,128)} %gauss.1) | copy-start | bytes 2359300
  20.6 5.7 %collective-permute-start.7 = (f32[22,256]{1,0:T(8,128)S(1)}, f32[22,256]{1,0:T(8,128)S(1)}, u32[]{:S(2)}, u32[]{:S(2)}) collective-permute-start(f32[22,256]{1,0:T(8,128)S(1)} %get-tuple-element.46), channel_id=1, source_target_pairs={{0,3},{1,2},{2,1},{3,0},{4,7},{5,6},{6,5},{7,4},{8,11},{9,10},{10,... | collective-permute-start | bytes 67592 | tf_op jit(solution)/shard_map/ppermute | solution.py:406
  24.4 4.7 %collective-permute-start.8 = (f32[22,256]{1,0:T(8,128)S(1)}, f32[22,256]{1,0:T(8,128)S(1)}, u32[]{:S(2)}, u32[]{:S(2)}) collective-permute-start(f32[22,256]{1,0:T(8,128)S(1)} %get-tuple-element.47), channel_id=1, source_target_pairs={{0,2},{1,3},{2,0},{3,1},{4,6},{5,7},{6,4},{7,5},{8,10},{9,11},{10,... | collective-permute-start | bytes 67592 | tf_op jit(solution)/shard_map/ppermute | solution.py:406
  24.4 4.7 %collective-permute-start.9 = (f32[22,256]{1,0:T(8,128)S(1)}, f32[22,256]{1,0:T(8,128)S(1)}, u32[]{:S(2)}, u32[]{:S(2)}) collective-permute-start(f32[22,256]{1,0:T(8,128)S(1)} %get-tuple-element.48), channel_id=1, source_target_pairs={{0,1},{1,0},{2,3},{3,2},{4,5},{5,4},{6,7},{7,6},{8,9},{9,8},{10,11... | collective-permute-start | bytes 67592 | tf_op jit(solution)/shard_map/ppermute | solution.py:406
  25.1 5.6 %copy-start.5 = (bf16[256,256]{1,0:T(8,128)(2,1)S(1)}, bf16[256,256]{1,0:T(8,128)(2,1)}, u32[]{:S(2)}) copy-start(bf16[256,256]{1,0:T(8,128)(2,1)} %encoder.1) | copy-start | bytes 393220
  29.2 13.5 %copy-start.1 = (bf16[256,4096]{1,0:T(8,128)(2,1)S(1)}, bf16[256,4096]{1,0:T(8,128)(2,1)}, u32[]{:S(2)}) copy-start(bf16[256,4096]{1,0:T(8,128)(2,1)} %templates.3) | copy-start | bytes 6291460
  29.2 13.5 %copy-start.3 = (bf16[256,768]{1,0:T(8,128)(2,1)S(1)}, bf16[256,768]{1,0:T(8,128)(2,1)}, u32[]{:S(2)}) copy-start(bf16[256,768]{1,0:T(8,128)(2,1)} %spectrum.1) | copy-start | bytes 1179652
  29.2 1.5 %collective-permute-start.10 = (bf16[384,256]{1,0:T(8,128)(2,1)S(1)}, bf16[384,256]{1,0:T(8,128)(2,1)S(1)}, u32[]{:S(2)}, u32[]{:S(2)}) collective-permute-start(bf16[384,256]{1,0:T(8,128)(2,1)S(1)} %halves.1), channel_id=1, source_target_pairs={{0,4},{4,0},{8,12},{12,8},{16,20},{20,16},{24,28},{28,24},{1,5},{5... | collective-permute-start | bytes 589832 | tf_op jit(solution)/shard_map/ppermute | solution.py:406
  32.0 7.0 %collective-permute-start.14 = (bf16[384,128]{1,0:T(8,128)(2,1)S(1)}, bf16[384,128]{1,0:T(8,128)(2,1)S(1)}, u32[]{:S(2)}, u32[]{:S(2)}) collective-permute-start(bf16[384,128]{1,0:T(8,128)(2,1)S(1)} %get-tuple-element.53.own), channel_id=1, source_target_pairs={{0,1},{1,0},{2,3},{3,2},{4,5},{5,4},{6,7},{7,6},{8,9},{9,8},{10,11... | collective-permute-start | bytes 294920 | tf_op jit(solution)/shard_map/ppermute | solution.py:406
  32.0 6.9 %collective-permute-start.13 = (bf16[384,128]{1,0:T(8,128)(2,1)S(1)}, bf16[384,128]{1,0:T(8,128)(2,1)S(1)}, u32[]{:S(2)}, u32[]{:S(2)}) collective-permute-start(bf16[384,128]{1,0:T(8,128)(2,1)S(1)} %get-tuple-element.53.own), channel_id=1, source_target_pairs={{0,2},{1,3},{2,0},{3,1},{4,6},{5,7},{6,4},{7,5},{8,10},{9,11},{10,... | collective-permute-start | bytes 294920 | tf_op jit(solution)/shard_map/ppermute | solution.py:406
  34.1 8.5 %collective-permute-start.12 = (bf16[384,128]{1,0:T(8,128)(2,1)S(1)}, bf16[384,128]{1,0:T(8,128)(2,1)S(1)}, u32[]{:S(2)}, u32[]{:S(2)}) collective-permute-start(bf16[384,128]{1,0:T(8,128)(2,1)S(1)} %get-tuple-element.53.own), channel_id=1, source_target_pairs={{0,3},{1,2},{2,1},{3,0},{4,7},{5,6},{6,5},{7,4},{8,11},{9,10},{10,... | collective-permute-start | bytes 294920 | tf_op jit(solution)/shard_map/ppermute | solution.py:406
  36.4 2.2 %collective-permute-start.11 = (bf16[256,128]{1,0:T(8,128)(2,1)S(1)}, bf16[256,128]{1,0:T(8,128)(2,1)S(1)}, u32[]{:S(2)}, u32[]{:S(2)}) collective-permute-start(bf16[256,128]{1,0:T(8,128)(2,1)S(1)} %get-tuple-element.54), channel_id=1, source_target_pairs={{0,4},{4,8},{8,12},{12,16},{16,20},{20,24},{24,28},{1,5},{5,9},{9,... | collective-permute-start | bytes 196616 | tf_op jit(solution)/shard_map/ppermute | solution.py:523
  48.4 2.2 %collective-permute-start.15 = (f32[520,256]{1,0:T(8,128)S(1)}, f32[520,256]{1,0:T(8,128)S(1)}, u32[]{:S(2)}, u32[]{:S(2)}) collective-permute-start(f32[520,256]{1,0:T(8,128)S(1)} %get-tuple-element.61), channel_id=1, source_target_pairs={{0,4},{4,0},{8,12},{12,8},{16,20},{20,16},{24,28},{28,24},{1,5},{5... | collective-permute-start | bytes 1597448 | tf_op jit(solution)/shard_map/ppermute | solution.py:406
  48.5 6.1 %collective-permute-start.20 = (f32[520,256]{1,0:T(8,128)S(1)}, f32[520,256]{1,0:T(8,128)S(1)}, u32[]{:S(2)}, u32[]{:S(2)}) collective-permute-start(f32[520,256]{1,0:T(8,128)S(1)} %get-tuple-element.66), channel_id=1, source_target_pairs={{0,4},{4,0},{8,12},{12,8},{16,20},{20,16},{24,28},{28,24},{1,5},{5... | collective-permute-start | bytes 1597448 | tf_op jit(solution)/shard_map/ppermute | solution.py:406
  49.0 8.3 %collective-permute-start.22 = (f32[520,256]{1,0:T(8,128)S(1)}, f32[520,256]{1,0:T(8,128)S(1)}, u32[]{:S(2)}, u32[]{:S(2)}) collective-permute-start(f32[520,256]{1,0:T(8,128)S(1)} %get-tuple-element.68), channel_id=1, source_target_pairs={{0,4},{4,0},{8,12},{12,8},{16,20},{20,16},{24,28},{28,24},{1,5},{5... | collective-permute-start | bytes 1597448 | tf_op jit(solution)/shard_map/ppermute | solution.py:406
  50.8 6.5 %collective-permute-start.16 = (f16[528,256]{1,0:T(8,128)(2,1)S(1)}, f16[528,256]{1,0:T(8,128)(2,1)S(1)}, u32[]{:S(2)}, u32[]{:S(2)}) collective-permute-start(f16[528,256]{1,0:T(8,128)(2,1)S(1)} %convert_element_type.24), channel_id=1, source_target_pairs={{0,8},{4,20},{8,0},{12,28},{16,24},{20,4},{24,16},{28,12},{1,9},{5... | collective-permute-start | bytes 811016 | tf_op jit(solution)/shard_map/ppermute | solution.py:567
  52.3 12.6 %collective-permute-start.19 = (f32[520,256]{1,0:T(8,128)S(1)}, f32[520,256]{1,0:T(8,128)S(1)}, u32[]{:S(2)}, u32[]{:S(2)}) collective-permute-start(f32[520,256]{1,0:T(8,128)S(1)} %get-tuple-element.64), channel_id=1, source_target_pairs={{0,4},{4,0},{8,12},{12,8},{16,20},{20,16},{24,28},{28,24},{1,5},{5... | collective-permute-start | bytes 1597448 | tf_op jit(solution)/shard_map/ppermute | solution.py:406
  52.8 3.6 %collective-permute-start.17 = (f32[1,768]{1,0:T(1,128)S(1)}, f32[1,768]{1,0:T(1,128)S(1)}, u32[]{:S(2)}, u32[]{:S(2)}) collective-permute-start(f32[1,768]{1,0:T(1,128)S(1)} %slice.11), channel_id=1, source_target_pairs={{0,1},{1,0},{2,3},{3,2},{4,5},{5,4},{6,7},{7,6},{8,9},{9,8},{10,11... | collective-permute-start | bytes 9224 | tf_op jit(solution)/shard_map/ppermute | solution.py:406
  54.8 8.0 %collective-permute-start.21 = (f16[528,256]{1,0:T(8,128)(2,1)S(1)}, f16[528,256]{1,0:T(8,128)(2,1)S(1)}, u32[]{:S(2)}, u32[]{:S(2)}) collective-permute-start(f16[528,256]{1,0:T(8,128)(2,1)S(1)} %convert_element_type.26), channel_id=1, source_target_pairs={{0,8},{4,20},{8,0},{12,28},{16,24},{20,4},{24,16},{28,12},{1,9},{5... | collective-permute-start | bytes 811016 | tf_op jit(solution)/shard_map/ppermute | solution.py:567
  57.5 7.4 %collective-permute-start.23 = (f16[528,256]{1,0:T(8,128)(2,1)S(1)}, f16[528,256]{1,0:T(8,128)(2,1)S(1)}, u32[]{:S(2)}, u32[]{:S(2)}) collective-permute-start(f16[528,256]{1,0:T(8,128)(2,1)S(1)} %convert_element_type.28), channel_id=1, source_target_pairs={{0,16},{4,12},{8,24},{12,4},{16,0},{20,28},{24,8},{28,20},{1,17},{... | collective-permute-start | bytes 811016 | tf_op jit(solution)/shard_map/ppermute | solution.py:567
  59.4 5.0 %collective-permute-start.18 = (f32[1,768]{1,0:T(1,128)S(1)}, f32[1,768]{1,0:T(1,128)S(1)}, u32[]{:S(2)}, u32[]{:S(2)}) collective-permute-start(f32[1,768]{1,0:T(1,128)S(1)} %slice_add_fusion), channel_id=1, source_target_pairs={{0,2},{1,3},{2,0},{3,1},{4,6},{5,7},{6,4},{7,5},{8,10},{9,11},{10,... | collective-permute-start | bytes 9224 | tf_op jit(solution)/shard_map/ppermute | solution.py:406
  (1 other events, 1.6 us)

commit v5 on v4

--- a/solution.py
+++ b/solution.py
@@ -540,7 +540,6 @@
         scalars=1,
     )
     steps = [1 << power for power in range(nf.bit_length() - 1)]
-    log_sum = sums[1:2] + exchanged(sums[1:2], "freq", steps[0])
     kept = call(
         functools.partial(kept_kernel, nt),
         "kept",
@@ -553,7 +552,7 @@
     )
     crossed = [exchanged(block, "tm", 1) for block in away]
 
-    def sent(index, pairs, *extra):
+    def message_of(index, *extra):
         (message,) = call(
             message_kernel,
             "message",
@@ -564,17 +563,25 @@
             crossed[index],
             *extra,
         )
-        return lax.ppermute(message.astype(jnp.float16), "tm", pairs).astype(f32)
-
+        return message.astype(jnp.float16)
+
+    def sent(message, pairs):
+        return lax.ppermute(message, "tm", pairs).astype(f32)
+
+    log_sum = sums[1:2]
     if nt == 8:
         first = [(lap, lap ^ (2 << (lap & 1))) for lap in range(nt)]
         second = [(lap, lap ^ (4 >> (lap & 1))) for lap in range(nt)]
-        carried = sent(0, first)
+        carried = sent(message_of(0), first)
+        direct, log_sum = lax.optimization_barrier((message_of(1), log_sum))
+        parts = [sent(direct, first)]
+        log_sum = log_sum + exchanged(log_sum, "freq", steps[0])
         carried, log_sum = lax.optimization_barrier((carried, log_sum))
-        parts = [sent(1, first), sent(2, second, carried)]
+        parts.append(sent(message_of(2, carried), second))
     else:
+        log_sum = log_sum + exchanged(log_sum, "freq", steps[0])
         parts = [
-            sent(step - 1, [(lap, lap ^ (2 * step)) for lap in range(nt)])
+            sent(message_of(step - 1), [(lap, lap ^ (2 * step)) for lap in range(nt)])
             for step in range(1, nt // 2)
         ]
     (result,) = call(

time: 66.1 us -> 66.1 us (level)
    ppermute x20, waiting for transfers between devices: 12.3 us -> 13.8 us  [exchanged(): lax.ppermute(value, axis, [(index, index ^ step) for index in range(size)])]
    ppermute x3, starting transfers between devices: 4.99 us -> 4.09 us  [sent(): return lax.ppermute(message, 'tm', pairs).astype(f32)]
    ppermute x3, waiting for transfers between devices: 0.9 us -> 0.01 us  [sent(): return lax.ppermute(message, 'tm', pairs).astype(f32)]
  transfers between devices with their start and end apart: 24 -> 24, of which waited for: 12 -> 11; matrix products, arithmetic and copies ran while one was open for 2% -> 2% of each run, Pallas kernels for 8% -> 8%
where the time goes in v5:
time: 66.1 us; the launch traced here: 65.9 us
  starting transfers between devices  31.5 us (48%)
  waiting for transfers between devices  14.7 us (22%)
  Pallas kernels  14.3 us (22%)
  other arithmetic  2.88 us (4%)
  local copies, waits for them, and re-layouts  1.63 us (2%)
  between operations  0.91 us (1%)
    ppermute x20, starting transfers between devices, exchanged(): lax.ppermute(value, axis, [(index, index ^ step) for index in range(size)])  26.1 us
    pallas_call x14, Pallas kernels, call(): pl.pallas_call(kernel, name=name, out_shape=[jax.ShapeDtypeStruct(shape,...  14.3 us
    ppermute x20, waiting for transfers between devices, exchanged(): lax.ppermute(value, axis, [(index, index ^ step) for index in range(size)])  13.8 us
    ppermute x3, starting transfers between devices, sent(): return lax.ppermute(message, 'tm', pairs).astype(f32)  4.09 us
    unnamed x18, local copies, waits for them, and re-layouts  1.63 us
  transfers between devices with their start and end apart: 24, of which 11 were waited for; matrix products, arithmetic and copies ran while one was open for 2% of the time, Pallas kernels for 8%

profile of v5, /device:TPU:0, one launch (start us, length us, event | category | flops | bytes accessed | tf_op | source)
XLA Modules:
  0.0 65.9 jit_solution(14703539385904565642)
XLA Ops:
  0.7 1.2 %pad_maximum_fusion.both = bf16[256,1024]{1,0:T(8,128)(2,1)S(1)} fusion(bf16[256,256]{1,0:T(8,128)(2,1)} %encoder.1, bf16[256,768]{1,0:T(8,128)(2,1)} %spectrum.1), kind=kLoop, calls=%fused_computation | loop fusion | flops 1048576 | bytes 1048576 | tf_op jit(solution)/shard_map/concatenate | solution.py:440
  2.0 0.8 %pieces.1 = (bf16[336,256]{1,0:T(8,128)(2,1)S(1)}, bf16[336,256]{1,0:T(8,128)(2,1)S(1)}, bf16[336,256]{1,0:T(8,128)(2,1)S(1)}, bf16[208,256]{1,0:T(8,128)(2,1)S(...) custom-call(s32[1,2]{1,0:T(1,128)S(1)} %add_bitcast_fusion.place, bf16[256,1024]{1,0:T(8,128)(2,1)S(1)} %pad_maximum_fusion.both), custom_call_target="tpu_custom_call" | custom-call | tf_op jit(solution)/shard_map/pieces/pallas_call | solution.py:23
  2.8 5.1 %collective-permute-start = (bf16[336,256]{1,0:T(8,128)(2,1)S(1)}, bf16[336,256]{1,0:T(8,128)(2,1)S(1)}, u32[]{:S(2)}, u32[]{:S(2)}) collective-permute-start(bf16[336,256]{1,0:T(8,128)(2,1)S(1)} %get-tuple-element.42), channel_id=1, source_target_pairs={{0,3},{1,2},{2,1},{3,0},{4,7},{5,6},{6,5},{7,4},{8,11},{9,10},{10,... | collective-permute-start | bytes 516104 | tf_op jit(solution)/shard_map/ppermute | solution.py:406
  8.5 0.7 %convert_add_fusion = f32[1024]{0:T(1024)S(1)} fusion(s32[768]{0:T(1024)} %param.12, f32[256]{0:T(256)} %param.10), kind=kLoop, calls=%fused_computation.2 | loop fusion | flops 2048 | bytes 8192 | tf_op jit(solution)/shard_map/add | solution.py:443
  9.2 1.1 %summary.1 = (f32[208,128]{1,0:T(8,128)S(1)}, f32[8,256]{1,0:T(8,128)S(1)}, f32[4,256]{1,0:T(4,128)S(1)}) custom-call(s32[1,2]{1,0:T(1,128)S(1)} %add_bitcast_fusion.place, bf16[768,256]{1,0:T(8,128)(2,1)S(1)} %get-tuple-element.39.flipped, f32[1,1024]{1,0:T(1,128)S(1)} %bitcast.8), custom_call_target="tpu_custom_call" | custom-call | tf_op jit(solution)/shard_map/summary/pallas_call | solution.py:23
  10.4 1.2 %collective-permute-done.1 = f32[4,256]{1,0:T(4,128)S(1)} collective-permute-done((f32[4,256]{1,0:T(4,128)S(1)}, f32[4,256]{1,0:T(4,128)S(1)}, u32[]{:S(2)}, u32[]{:S(2)}) %collective-permute-start.1) | collective-permute-done | bytes 4128 | tf_op jit(solution)/shard_map/ppermute | solution.py:406
  11.5 2.6 %collective-permute-start.4 = (f32[8,256]{1,0:T(8,128)S(1)}, f32[8,256]{1,0:T(8,128)S(1)}, u32[]{:S(2)}, u32[]{:S(2)}) collective-permute-start(f32[8,256]{1,0:T(8,128)S(1)} %pad_maximum_fusion.1.refs_1_), channel_id=1, source_target_pairs={{0,24},{4,28},{8,16},{12,20},{16,8},{20,12},{24,0},{28,4},{1,25},{... | collective-permute-start | bytes 24584 | tf_op jit(solution)/shard_map/ppermute | solution.py:406
  14.6 1.5 %collective-permute-done.4.refs_4_ = f32[8,256]{1,0:T(8,128)S(1)} collective-permute-done((f32[8,256]{1,0:T(8,128)S(1)}, f32[8,256]{1,0:T(8,128)S(1)}, u32[]{:S(2)}, u32[]{:S(2)}) %collective-permute-start.4) | collective-permute-done | bytes 8224 | tf_op jit(solution)/shard_map/ppermute | solution.py:406
  16.1 1.6 %collective-permute-start.2 = (f32[8,256]{1,0:T(8,128)S(1)}, f32[8,256]{1,0:T(8,128)S(1)}, u32[]{:S(2)}, u32[]{:S(2)}) collective-permute-start(f32[8,256]{1,0:T(8,128)S(1)} %pad_maximum_fusion.1.refs_1_), channel_id=1, source_target_pairs={{0,8},{4,12},{8,0},{12,4},{16,24},{20,28},{24,16},{28,20},{1,9},{5... | collective-permute-start | bytes 24584 | tf_op jit(solution)/shard_map/ppermute | solution.py:406
  17.7 1.6 %copy-done = bf16[256,4096]{1,0:T(8,128)(2,1)S(1)} copy-done((bf16[256,4096]{1,0:T(8,128)(2,1)S(1)}, bf16[256,4096]{1,0:T(8,128)(2,1)}, u32[]{:S(2)}) %copy-start) | copy-done | bytes 2097176
  19.8 0.8 %entry.1 = (f32[22,256]{1,0:T(8,128)S(1)}, f32[22,256]{1,0:T(8,128)S(1)}, f32[22,256]{1,0:T(8,128)S(1)}, f32[3,256]{1,0:T(4,128)S(1)}, f32[1,896]{1,0:T(1,128)S(1)}) custom-call(s32[1,2]{1,0:T(1,128)S(1)} %add_bitcast_fusion.place, f32[1,256]{1,0:T(1,128)S(1)} %bitcast.9, f32[1,256]{1,0:T(1,128)S(1)} %bitcast.10, f32[8,256]{1,0:T(8,128)S(1)} %get-tuple-element.40.states, ...), custom_call_target="tpu_custom_call" | custom-call | tf_op jit(solution)/shard_map/entry/pallas_call | solution.py:23
  20.6 3.8 %collective-permute-start.7 = (f32[22,256]{1,0:T(8,128)S(1)}, f32[22,256]{1,0:T(8,128)S(1)}, u32[]{:S(2)}, u32[]{:S(2)}) collective-permute-start(f32[22,256]{1,0:T(8,128)S(1)} %get-tuple-element.48), channel_id=1, source_target_pairs={{0,3},{1,2},{2,1},{3,0},{4,7},{5,6},{6,5},{7,4},{8,11},{9,10},{10,... | collective-permute-start | bytes 67592 | tf_op jit(solution)/shard_map/ppermute | solution.py:406
  25.1 0.9 %noise.1 = (f32[256,256]{1,0:T(8,128)S(1)}, f32[256,256]{1,0:T(8,128)S(1)}, f32[256,256]{1,0:T(8,128)S(1)}, f32[256,256]{1,0:T(8,128)S(1)}) custom-call(s32[1,2]{1,0:T(1,128)S(1)} %add_bitcast_fusion.place, f32[256,768]{1,0:T(8,128)S(1)} %copy-done.4, f32[2,256,768]{2,1,0:T(8,128)S(1)} %copy-done.2, s32[1,256]{1,0:T(1,128)S(1)} %bitcast.11), custom_call_target="tpu_custom_call" | custom-call | tf_op jit(solution)/shard_map/noise/pallas_call | solution.py:23
  26.3 2.8 %collective-permute-done.8.refs_4_.refs_1_ = f32[22,256]{1,0:T(8,128)S(1)} collective-permute-done((f32[22,256]{1,0:T(8,128)S(1)}, f32[22,256]{1,0:T(8,128)S(1)}, u32[]{:S(2)}, u32[]{:S(2)}) %collective-permute-start.8) | collective-permute-done | bytes 22560 | tf_op jit(solution)/shard_map/ppermute | solution.py:406
  29.3 0.7 %normed.1 = bf16[4,256,256]{2,1,0:T(8,128)(2,1)S(1)} custom-call(bf16[208,256]{1,0:T(8,128)(2,1)S(1)} %get-tuple-element.38.own, f32[3,256]{1,0:T(4,128)S(1)} %get-tuple-element.44.own_state, f32[208,128]{1,0:T(8,128)S(1)} %get-tuple-element.45.gains, bf16[336,256]{1,0:T(8,128)(2,1)S(1)} %collective-permute-done.refs_0_.refs_3_, ...), custom_call_target="tpu_custom_call" | custom-call | tf_op jit(solution)/shard_map/normed/pallas_call | solution.py:23
  30.0 0.7 %collective-permute-done.10.halves = bf16[384,256]{1,0:T(8,128)(2,1)S(1)} collective-permute-done((bf16[384,256]{1,0:T(8,128)(2,1)S(1)}, bf16[384,256]{1,0:T(8,128)(2,1)S(1)}, u32[]{:S(2)}, u32[]{:S(2)}) %collective-permute-start.10) | collective-permute-done | bytes 196640 | tf_op jit(solution)/shard_map/ppermute | solution.py:406
  30.7 1.3 %sampler.1 = (bf16[384,128]{1,0:T(8,128)(2,1)S(1)}, bf16[256,128]{1,0:T(8,128)(2,1)S(1)}) custom-call(s32[1,2]{1,0:T(1,128)S(1)} %add_bitcast_fusion.place, bf16[4,256,256]{2,1,0:T(8,128)(2,1)S(1)} %normed.1, bf16[256,256]{1,0:T(8,128)(2,1)S(1)} %copy-done.5, bf16[384,256]{1,0:T(8,128)(2,1)S(1)} %collective-permute-done.10.halves, ...), custom_call_target="tpu_custom_call" | custom-call | tf_op jit(solution)/shard_map/sampler/pallas_call | solution.py:23
  32.0 2.1 %collective-permute-start.13 = (bf16[384,128]{1,0:T(8,128)(2,1)S(1)}, bf16[384,128]{1,0:T(8,128)(2,1)S(1)}, u32[]{:S(2)}, u32[]{:S(2)}) collective-permute-start(bf16[384,128]{1,0:T(8,128)(2,1)S(1)} %get-tuple-element.55.own), channel_id=1, source_target_pairs={{0,2},{1,3},{2,0},{3,1},{4,6},{5,7},{6,4},{7,5},{8,10},{9,11},{10,... | collective-permute-start | bytes 294920 | tf_op jit(solution)/shard_map/ppermute | solution.py:406
  34.1 2.3 %collective-permute-start.12 = (bf16[384,128]{1,0:T(8,128)(2,1)S(1)}, bf16[384,128]{1,0:T(8,128)(2,1)S(1)}, u32[]{:S(2)}, u32[]{:S(2)}) collective-permute-start(bf16[384,128]{1,0:T(8,128)(2,1)S(1)} %get-tuple-element.55.own), channel_id=1, source_target_pairs={{0,3},{1,2},{2,1},{3,0},{4,7},{5,6},{6,5},{7,4},{8,11},{9,10},{10,... | collective-permute-start | bytes 294920 | tf_op jit(solution)/shard_map/ppermute | solution.py:406
  36.4 1.3 %collective-permute-start.11 = (bf16[256,128]{1,0:T(8,128)(2,1)S(1)}, bf16[256,128]{1,0:T(8,128)(2,1)S(1)}, u32[]{:S(2)}, u32[]{:S(2)}) collective-permute-start(bf16[256,128]{1,0:T(8,128)(2,1)S(1)} %get-tuple-element.56), channel_id=1, source_target_pairs={{0,4},{4,8},{8,12},{12,16},{16,20},{20,24},{24,28},{1,5},{5,9},{9,... | collective-permute-start | bytes 196616 | tf_op jit(solution)/shard_map/ppermute | solution.py:523
  37.7 0.9 %collective-permute-done.11.rim = bf16[256,128]{1,0:T(8,128)(2,1)S(1)} collective-permute-done((bf16[256,128]{1,0:T(8,128)(2,1)S(1)}, bf16[256,128]{1,0:T(8,128)(2,1)S(1)}, u32[]{:S(2)}, u32[]{:S(2)}) %collective-permute-start.11) | collective-permute-done | bytes 65568 | tf_op jit(solution)/shard_map/ppermute | solution.py:523
  39.0 3.7 %collective-permute-done.12.refs_0_ = bf16[384,128]{1,0:T(8,128)(2,1)S(1)} collective-permute-done((bf16[384,128]{1,0:T(8,128)(2,1)S(1)}, bf16[384,128]{1,0:T(8,128)(2,1)S(1)}, u32[]{:S(2)}, u32[]{:S(2)}) %collective-permute-start.12) | collective-permute-done | bytes 98336 | tf_op jit(solution)/shard_map/ppermute | solution.py:406
  42.6 5.8 %rebuild.1 = (bf16[4096,768]{1,0:T(8,128)(2,1)S(1)}, bf16[768,256]{1,0:T(8,128)(2,1)S(1)}, f32[8,768]{1,0:T(8,128)S(1)}, f32[8,256]{1,0:T(8,128)S(1)}, f32[520,2...) custom-call(s32[1,2]{1,0:T(1,128)S(1)} %add_bitcast_fusion.place, ...), custom_call_target="tpu_custom_call" | custom-call | tf_op jit(solution)/shard_map/rebuild/pallas_call | solution.py:23
  49.1 1.5 %kept.1 = (f32[512,256]{1,0:T(8,128)S(1)}, f32[512,256]{1,0:T(8,128)S(1)}, f32[512,256]{1,0:T(8,128)S(1)}, f32[512,256]{1,0:T(8,128)S(1)}) custom-call(s32[1,2]{1,0:T(1,128)S(1)} %add_bitcast_fusion.place, bf16[4096,768]{1,0:T(8,128)(2,1)S(1)} %get-tuple-element.60.stacked, bf16[768,256]{1,0:T(8,128)(2,1)S(1)} %get-tuple-element.61.ratio), custom_call_target="tpu_custom_call" | custom-call | tf_op jit(solution)/shard_map/kept/pallas_call | solution.py:23
  50.8 1.6 %collective-permute-start.16 = (f16[528,256]{1,0:T(8,128)(2,1)S(1)}, f16[528,256]{1,0:T(8,128)(2,1)S(1)}, u32[]{:S(2)}, u32[]{:S(2)}) collective-permute-start(f16[528,256]{1,0:T(8,128)(2,1)S(1)} %convert_element_type.24), channel_id=1, source_target_pairs={{0,8},{4,20},{8,0},{12,28},{16,24},{20,4},{24,16},{28,12},{1,9},{5... | collective-permute-start | bytes 811016 | tf_op jit(solution)/shard_map/ppermute | solution.py:569
  52.9 1.3 %collective-permute-start.21 = (f16[528,256]{1,0:T(8,128)(2,1)S(1)}, f16[528,256]{1,0:T(8,128)(2,1)S(1)}, u32[]{:S(2)}, u32[]{:S(2)}) collective-permute-start(f16[528,256]{1,0:T(8,128)(2,1)S(1)} %convert_element_type.26), channel_id=1, source_target_pairs={{0,8},{4,20},{8,0},{12,28},{16,24},{20,4},{24,16},{28,12},{1,9},{5... | collective-permute-start | bytes 811016 | tf_op jit(solution)/shard_map/ppermute | solution.py:569
  54.2 2.1 %collective-permute-start.18 = (f32[1,768]{1,0:T(1,128)S(1)}, f32[1,768]{1,0:T(1,128)S(1)}, u32[]{:S(2)}, u32[]{:S(2)}) collective-permute-start(f32[1,768]{1,0:T(1,128)S(1)} %slice.10), channel_id=1, source_target_pairs={{0,1},{1,0},{2,3},{3,2},{4,5},{5,4},{6,7},{7,6},{8,9},{9,8},{10,11... | collective-permute-start | bytes 9224 | tf_op jit(solution)/shard_map/ppermute | solution.py:406
  56.3 1.6 %collective-permute-done.18 = f32[1,768]{1,0:T(1,128)S(1)} collective-permute-done((f32[1,768]{1,0:T(1,128)S(1)}, f32[1,768]{1,0:T(1,128)S(1)}, u32[]{:S(2)}, u32[]{:S(2)}) %collective-permute-start.18) | collective-permute-done | bytes 3104 | tf_op jit(solution)/shard_map/ppermute | solution.py:406
  58.1 1.2 %collective-permute-start.23 = (f16[528,256]{1,0:T(8,128)(2,1)S(1)}, f16[528,256]{1,0:T(8,128)(2,1)S(1)}, u32[]{:S(2)}, u32[]{:S(2)}) collective-permute-start(f16[528,256]{1,0:T(8,128)(2,1)S(1)} %convert_element_type.28), channel_id=1, source_target_pairs={{0,16},{4,12},{8,24},{12,4},{16,0},{20,28},{24,8},{28,20},{1,17},{... | collective-permute-start | bytes 811016 | tf_op jit(solution)/shard_map/ppermute | solution.py:569
  59.4 3.4 %collective-permute-start.19 = (f32[1,768]{1,0:T(1,128)S(1)}, f32[1,768]{1,0:T(1,128)S(1)}, u32[]{:S(2)}, u32[]{:S(2)}) collective-permute-start(f32[1,768]{1,0:T(1,128)S(1)} %add.14), channel_id=1, source_target_pairs={{0,2},{1,3},{2,0},{3,1},{4,6},{5,7},{6,4},{7,5},{8,10},{9,11},{10,... | collective-permute-start | bytes 9224 | tf_op jit(solution)/shard_map/ppermute | solution.py:406
  62.8 1.5 %collective-permute-done.19 = f32[1,768]{1,0:T(1,128)S(1)} collective-permute-done((f32[1,768]{1,0:T(1,128)S(1)}, f32[1,768]{1,0:T(1,128)S(1)}, u32[]{:S(2)}, u32[]{:S(2)}) %collective-permute-start.19) | collective-permute-done | bytes 3104 | tf_op jit(solution)/shard_map/ppermute | solution.py:406
  65.0 0.9 %total.1 = f32[512,256]{1,0:T(8,128)} custom-call(f32[512,256]{1,0:T(8,128)S(1)} %get-tuple-element.68.kept, f32[520,256]{1,0:T(8,128)S(1)} %collective-permute-done.20.crossed, f32[528,256]{1,0:T(8,128)S(1)} %convert_element_type.27.refs_0_, f32[528,256]{1,0:T(8,128)S(1)} %convert_element_type.29.refs_1_), custom_call_target="tpu_custom_call" | custom-call | tf_op jit(solution)/shard_map/total/pallas_call | solution.py:23
  (61 shorter events, 5.5 us)
Async XLA Ops:
  0.6 19.1 %copy-start.6 = (f32[256]{0:T(256)S(1)}, f32[256]{0:T(256)}, u32[]{:S(2)}) copy-start(f32[256]{0:T(256)} %param.10) | copy-start | bytes 3076
  0.6 19.1 %copy-start.7 = (f32[256]{0:T(256)S(1)}, f32[256]{0:T(256)}, u32[]{:S(2)}) copy-start(f32[256]{0:T(256)} %param.11) | copy-start | bytes 3076
  0.7 24.3 %copy-start.2 = (f32[2,256,768]{2,1,0:T(8,128)S(1)}, f32[2,256,768]{2,1,0:T(8,128)}, u32[]{:S(2)}) copy-start(f32[2,256,768]{2,1,0:T(8,128)} %uniform.1) | copy-start | bytes 4718596
  0.7 24.3 %copy-start.8 = (s32[256]{0:T(256)S(1)}, s32[256]{0:T(256)}, u32[]{:S(2)}) copy-start(s32[256]{0:T(256)} %param.16) | copy-start | bytes 3076
  2.8 17.0 %collective-permute-start = (bf16[336,256]{1,0:T(8,128)(2,1)S(1)}, bf16[336,256]{1,0:T(8,128)(2,1)S(1)}, u32[]{:S(2)}, u32[]{:S(2)}) collective-permute-start(bf16[336,256]{1,0:T(8,128)(2,1)S(1)} %get-tuple-element.42), channel_id=1, source_target_pairs={{0,3},{1,2},{2,1},{3,0},{4,7},{5,6},{6,5},{7,4},{8,11},{9,10},{10,... | collective-permute-start | bytes 516104 | tf_op jit(solution)/shard_map/ppermute | solution.py:406
  7.9 18.1 %collective-permute-start.5 = (bf16[336,256]{1,0:T(8,128)(2,1)S(1)}, bf16[336,256]{1,0:T(8,128)(2,1)S(1)}, u32[]{:S(2)}, u32[]{:S(2)}) collective-permute-start(bf16[336,256]{1,0:T(8,128)(2,1)S(1)} %get-tuple-element.46), channel_id=1, source_target_pairs={{0,2},{1,3},{2,0},{3,1},{4,6},{5,7},{6,4},{7,5},{8,10},{9,11},{10,... | collective-permute-start | bytes 516104 | tf_op jit(solution)/shard_map/ppermute | solution.py:406
  7.9 18.1 %collective-permute-start.6 = (bf16[336,256]{1,0:T(8,128)(2,1)S(1)}, bf16[336,256]{1,0:T(8,128)(2,1)S(1)}, u32[]{:S(2)}, u32[]{:S(2)}) collective-permute-start(bf16[336,256]{1,0:T(8,128)(2,1)S(1)} %get-tuple-element.47), channel_id=1, source_target_pairs={{0,1},{1,0},{2,3},{3,2},{4,5},{5,4},{6,7},{7,6},{8,9},{9,8},{10,11... | collective-permute-start | bytes 516104 | tf_op jit(solution)/shard_map/ppermute | solution.py:406
  10.3 1.2 %collective-permute-start.1 = (f32[4,256]{1,0:T(4,128)S(1)}, f32[4,256]{1,0:T(4,128)S(1)}, u32[]{:S(2)}, u32[]{:S(2)}) collective-permute-start(f32[4,256]{1,0:T(4,128)S(1)} %get-tuple-element.43), channel_id=1, source_target_pairs={{0,4},{4,0},{8,12},{12,8},{16,20},{20,16},{24,28},{28,24},{1,5},{5... | collective-permute-start | bytes 12296 | tf_op jit(solution)/shard_map/ppermute | solution.py:406
  11.5 4.5 %collective-permute-start.4 = (f32[8,256]{1,0:T(8,128)S(1)}, f32[8,256]{1,0:T(8,128)S(1)}, u32[]{:S(2)}, u32[]{:S(2)}) collective-permute-start(f32[8,256]{1,0:T(8,128)S(1)} %pad_maximum_fusion.1.refs_1_), channel_id=1, source_target_pairs={{0,24},{4,28},{8,16},{12,20},{16,8},{20,12},{24,0},{28,4},{1,25},{... | collective-permute-start | bytes 24584 | tf_op jit(solution)/shard_map/ppermute | solution.py:406
  14.1 5.5 %collective-permute-start.3 = (f32[8,256]{1,0:T(8,128)S(1)}, f32[8,256]{1,0:T(8,128)S(1)}, u32[]{:S(2)}, u32[]{:S(2)}) collective-permute-start(f32[8,256]{1,0:T(8,128)S(1)} %pad_maximum_fusion.1.refs_1_), channel_id=1, source_target_pairs={{0,16},{4,20},{8,24},{12,28},{16,0},{20,4},{24,8},{28,12},{1,17},{... | collective-permute-start | bytes 24584 | tf_op jit(solution)/shard_map/ppermute | solution.py:406
  16.1 3.7 %collective-permute-start.2 = (f32[8,256]{1,0:T(8,128)S(1)}, f32[8,256]{1,0:T(8,128)S(1)}, u32[]{:S(2)}, u32[]{:S(2)}) collective-permute-start(f32[8,256]{1,0:T(8,128)S(1)} %pad_maximum_fusion.1.refs_1_), channel_id=1, source_target_pairs={{0,8},{4,12},{8,0},{12,4},{16,24},{20,28},{24,16},{28,20},{1,9},{5... | collective-permute-start | bytes 24584 | tf_op jit(solution)/shard_map/ppermute | solution.py:406
  19.3 5.7 %copy-start.4 = (f32[256,768]{1,0:T(8,128)S(1)}, f32[256,768]{1,0:T(8,128)}, u32[]{:S(2)}) copy-start(f32[256,768]{1,0:T(8,128)} %gauss.1) | copy-start | bytes 2359300
  20.6 5.7 %collective-permute-start.7 = (f32[22,256]{1,0:T(8,128)S(1)}, f32[22,256]{1,0:T(8,128)S(1)}, u32[]{:S(2)}, u32[]{:S(2)}) collective-permute-start(f32[22,256]{1,0:T(8,128)S(1)} %get-tuple-element.48), channel_id=1, source_target_pairs={{0,3},{1,2},{2,1},{3,0},{4,7},{5,6},{6,5},{7,4},{8,11},{9,10},{10,... | collective-permute-start | bytes 67592 | tf_op jit(solution)/shard_map/ppermute | solution.py:406
  24.4 4.7 %collective-permute-start.8 = (f32[22,256]{1,0:T(8,128)S(1)}, f32[22,256]{1,0:T(8,128)S(1)}, u32[]{:S(2)}, u32[]{:S(2)}) collective-permute-start(f32[22,256]{1,0:T(8,128)S(1)} %get-tuple-element.49), channel_id=1, source_target_pairs={{0,2},{1,3},{2,0},{3,1},{4,6},{5,7},{6,4},{7,5},{8,10},{9,11},{10,... | collective-permute-start | bytes 67592 | tf_op jit(solution)/shard_map/ppermute | solution.py:406
  24.4 4.7 %collective-permute-start.9 = (f32[22,256]{1,0:T(8,128)S(1)}, f32[22,256]{1,0:T(8,128)S(1)}, u32[]{:S(2)}, u32[]{:S(2)}) collective-permute-start(f32[22,256]{1,0:T(8,128)S(1)} %get-tuple-element.50), channel_id=1, source_target_pairs={{0,1},{1,0},{2,3},{3,2},{4,5},{5,4},{6,7},{7,6},{8,9},{9,8},{10,11... | collective-permute-start | bytes 67592 | tf_op jit(solution)/shard_map/ppermute | solution.py:406
  25.1 5.6 %copy-start.5 = (bf16[256,256]{1,0:T(8,128)(2,1)S(1)}, bf16[256,256]{1,0:T(8,128)(2,1)}, u32[]{:S(2)}) copy-start(bf16[256,256]{1,0:T(8,128)(2,1)} %encoder.1) | copy-start | bytes 393220
  29.2 13.5 %copy-start.1 = (bf16[256,4096]{1,0:T(8,128)(2,1)S(1)}, bf16[256,4096]{1,0:T(8,128)(2,1)}, u32[]{:S(2)}) copy-start(bf16[256,4096]{1,0:T(8,128)(2,1)} %templates.3) | copy-start | bytes 6291460
  29.2 13.5 %copy-start.3 = (bf16[256,768]{1,0:T(8,128)(2,1)S(1)}, bf16[256,768]{1,0:T(8,128)(2,1)}, u32[]{:S(2)}) copy-start(bf16[256,768]{1,0:T(8,128)(2,1)} %spectrum.1) | copy-start | bytes 1179652
  29.2 1.5 %collective-permute-start.10 = (bf16[384,256]{1,0:T(8,128)(2,1)S(1)}, bf16[384,256]{1,0:T(8,128)(2,1)S(1)}, u32[]{:S(2)}, u32[]{:S(2)}) collective-permute-start(bf16[384,256]{1,0:T(8,128)(2,1)S(1)} %halves.1), channel_id=1, source_target_pairs={{0,4},{4,0},{8,12},{12,8},{16,20},{20,16},{24,28},{28,24},{1,5},{5... | collective-permute-start | bytes 589832 | tf_op jit(solution)/shard_map/ppermute | solution.py:406
  32.0 7.0 %collective-permute-start.14 = (bf16[384,128]{1,0:T(8,128)(2,1)S(1)}, bf16[384,128]{1,0:T(8,128)(2,1)S(1)}, u32[]{:S(2)}, u32[]{:S(2)}) collective-permute-start(bf16[384,128]{1,0:T(8,128)(2,1)S(1)} %get-tuple-element.55.own), channel_id=1, source_target_pairs={{0,1},{1,0},{2,3},{3,2},{4,5},{5,4},{6,7},{7,6},{8,9},{9,8},{10,11... | collective-permute-start | bytes 294920 | tf_op jit(solution)/shard_map/ppermute | solution.py:406
  32.0 6.9 %collective-permute-start.13 = (bf16[384,128]{1,0:T(8,128)(2,1)S(1)}, bf16[384,128]{1,0:T(8,128)(2,1)S(1)}, u32[]{:S(2)}, u32[]{:S(2)}) collective-permute-start(bf16[384,128]{1,0:T(8,128)(2,1)S(1)} %get-tuple-element.55.own), channel_id=1, source_target_pairs={{0,2},{1,3},{2,0},{3,1},{4,6},{5,7},{6,4},{7,5},{8,10},{9,11},{10,... | collective-permute-start | bytes 294920 | tf_op jit(solution)/shard_map/ppermute | solution.py:406
  34.1 8.5 %collective-permute-start.12 = (bf16[384,128]{1,0:T(8,128)(2,1)S(1)}, bf16[384,128]{1,0:T(8,128)(2,1)S(1)}, u32[]{:S(2)}, u32[]{:S(2)}) collective-permute-start(bf16[384,128]{1,0:T(8,128)(2,1)S(1)} %get-tuple-element.55.own), channel_id=1, source_target_pairs={{0,3},{1,2},{2,1},{3,0},{4,7},{5,6},{6,5},{7,4},{8,11},{9,10},{10,... | collective-permute-start | bytes 294920 | tf_op jit(solution)/shard_map/ppermute | solution.py:406
  36.4 2.2 %collective-permute-start.11 = (bf16[256,128]{1,0:T(8,128)(2,1)S(1)}, bf16[256,128]{1,0:T(8,128)(2,1)S(1)}, u32[]{:S(2)}, u32[]{:S(2)}) collective-permute-start(bf16[256,128]{1,0:T(8,128)(2,1)S(1)} %get-tuple-element.56), channel_id=1, source_target_pairs={{0,4},{4,8},{8,12},{12,16},{16,20},{20,24},{24,28},{1,5},{5,9},{9,... | collective-permute-start | bytes 196616 | tf_op jit(solution)/shard_map/ppermute | solution.py:523
  48.4 2.2 %collective-permute-start.15 = (f32[520,256]{1,0:T(8,128)S(1)}, f32[520,256]{1,0:T(8,128)S(1)}, u32[]{:S(2)}, u32[]{:S(2)}) collective-permute-start(f32[520,256]{1,0:T(8,128)S(1)} %get-tuple-element.63), channel_id=1, source_target_pairs={{0,4},{4,0},{8,12},{12,8},{16,20},{20,16},{24,28},{28,24},{1,5},{5... | collective-permute-start | bytes 1597448 | tf_op jit(solution)/shard_map/ppermute | solution.py:406
  48.5 4.3 %collective-permute-start.17 = (f32[520,256]{1,0:T(8,128)S(1)}, f32[520,256]{1,0:T(8,128)S(1)}, u32[]{:S(2)}, u32[]{:S(2)}) collective-permute-start(f32[520,256]{1,0:T(8,128)S(1)} %get-tuple-element.65), channel_id=1, source_target_pairs={{0,4},{4,0},{8,12},{12,8},{16,20},{20,16},{24,28},{28,24},{1,5},{5... | collective-permute-start | bytes 1597448 | tf_op jit(solution)/shard_map/ppermute | solution.py:406
  49.0 8.9 %collective-permute-start.22 = (f32[520,256]{1,0:T(8,128)S(1)}, f32[520,256]{1,0:T(8,128)S(1)}, u32[]{:S(2)}, u32[]{:S(2)}) collective-permute-start(f32[520,256]{1,0:T(8,128)S(1)} %get-tuple-element.72), channel_id=1, source_target_pairs={{0,4},{4,0},{8,12},{12,8},{16,20},{20,16},{24,28},{28,24},{1,5},{5... | collective-permute-start | bytes 1597448 | tf_op jit(solution)/shard_map/ppermute | solution.py:406
  50.8 7.1 %collective-permute-start.16 = (f16[528,256]{1,0:T(8,128)(2,1)S(1)}, f16[528,256]{1,0:T(8,128)(2,1)S(1)}, u32[]{:S(2)}, u32[]{:S(2)}) collective-permute-start(f16[528,256]{1,0:T(8,128)(2,1)S(1)} %convert_element_type.24), channel_id=1, source_target_pairs={{0,8},{4,20},{8,0},{12,28},{16,24},{20,4},{24,16},{28,12},{1,9},{5... | collective-permute-start | bytes 811016 | tf_op jit(solution)/shard_map/ppermute | solution.py:569
  52.3 12.6 %collective-permute-start.20 = (f32[520,256]{1,0:T(8,128)S(1)}, f32[520,256]{1,0:T(8,128)S(1)}, u32[]{:S(2)}, u32[]{:S(2)}) collective-permute-start(f32[520,256]{1,0:T(8,128)S(1)} %get-tuple-element.69), channel_id=1, source_target_pairs={{0,4},{4,0},{8,12},{12,8},{16,20},{20,16},{24,28},{28,24},{1,5},{5... | collective-permute-start | bytes 1597448 | tf_op jit(solution)/shard_map/ppermute | solution.py:406
  52.9 9.8 %collective-permute-start.21 = (f16[528,256]{1,0:T(8,128)(2,1)S(1)}, f16[528,256]{1,0:T(8,128)(2,1)S(1)}, u32[]{:S(2)}, u32[]{:S(2)}) collective-permute-start(f16[528,256]{1,0:T(8,128)(2,1)S(1)} %convert_element_type.26), channel_id=1, source_target_pairs={{0,8},{4,20},{8,0},{12,28},{16,24},{20,4},{24,16},{28,12},{1,9},{5... | collective-permute-start | bytes 811016 | tf_op jit(solution)/shard_map/ppermute | solution.py:569
  54.2 3.7 %collective-permute-start.18 = (f32[1,768]{1,0:T(1,128)S(1)}, f32[1,768]{1,0:T(1,128)S(1)}, u32[]{:S(2)}, u32[]{:S(2)}) collective-permute-start(f32[1,768]{1,0:T(1,128)S(1)} %slice.10), channel_id=1, source_target_pairs={{0,1},{1,0},{2,3},{3,2},{4,5},{5,4},{6,7},{7,6},{8,9},{9,8},{10,11... | collective-permute-start | bytes 9224 | tf_op jit(solution)/shard_map/ppermute | solution.py:406
  58.1 6.8 %collective-permute-start.23 = (f16[528,256]{1,0:T(8,128)(2,1)S(1)}, f16[528,256]{1,0:T(8,128)(2,1)S(1)}, u32[]{:S(2)}, u32[]{:S(2)}) collective-permute-start(f16[528,256]{1,0:T(8,128)(2,1)S(1)} %convert_element_type.28), channel_id=1, source_target_pairs={{0,16},{4,12},{8,24},{12,4},{16,0},{20,28},{24,8},{28,20},{1,17},{... | collective-permute-start | bytes 811016 | tf_op jit(solution)/shard_map/ppermute | solution.py:569
  59.4 5.0 %collective-permute-start.19 = (f32[1,768]{1,0:T(1,128)S(1)}, f32[1,768]{1,0:T(1,128)S(1)}, u32[]{:S(2)}, u32[]{:S(2)}) collective-permute-start(f32[1,768]{1,0:T(1,128)S(1)} %add.14), channel_id=1, source_target_pairs={{0,2},{1,3},{2,0},{3,1},{4,6},{5,7},{6,4},{7,5},{8,10},{9,11},{10,... | collective-permute-start | bytes 9224 | tf_op jit(solution)/shard_map/ppermute | solution.py:406
  (1 other events, 1.6 us)

commit v6 on v5

--- a/solution.py
+++ b/solution.py
@@ -451,9 +451,14 @@
         small[None],
         scalars=1,
     )
-    messages = [exchanged(messages[-step], "freq", step) for step in far_first]
+    *messages, nearest = [
+        exchanged(messages[-step], "freq", step) if step > 1 else messages[-1]
+        for step in far_first
+    ]
     pair = jnp.concatenate([tm_message, exchanged(tm_message, "tm", 1)], axis=0)
     pairs = [pair] + [exchanged(pair, "tm", step) for step in range(2, nt, 2)]
+    nearest, pairs[-1] = lax.optimization_barrier((nearest, pairs[-1]))
+    messages.append(exchanged(nearest, "freq", 1))
     stat_rows = columns // bins + frames // bins
     (stats,) = call(
         totals_kernel, "totals", [((stat_rows, bins), f32)], [], templates, frame_sums

time: 66.1 us -> 65.9 us (level)
  starting transfers between devices: 31.5 us -> 30.1 us
  waiting for transfers between devices: 14.7 us -> 15.8 us
    ppermute x20, starting transfers between devices: 26.1 us -> 24.7 us  [exchanged(): lax.ppermute(value, axis, [(index, index ^ step) for index in range(size)])]
    ppermute x20, waiting for transfers between devices: 13.8 us -> 14.6 us  [exchanged(): lax.ppermute(value, axis, [(index, index ^ step) for index in range(size)])]
  transfers between devices with their start and end apart: 24 -> 24, of which waited for: 11 -> 11; matrix products, arithmetic and copies ran while one was open for 2% -> 1% of each run, Pallas kernels for 8% -> 7%
where the time goes in v6:
time: 65.9 us; the launch traced here: 65.7 us
  starting transfers between devices  30.1 us (46%)
  waiting for transfers between devices  15.8 us (24%)
  Pallas kernels  14.3 us (22%)
  other arithmetic  2.88 us (4%)
  local copies, waits for them, and re-layouts  1.63 us (2%)
  between operations  0.9 us (1%)
    ppermute x20, starting transfers between devices, exchanged(): lax.ppermute(value, axis, [(index, index ^ step) for index in range(size)])  24.7 us
    ppermute x20, waiting for transfers between devices, exchanged(): lax.ppermute(value, axis, [(index, index ^ step) for index in range(size)])  14.6 us
    pallas_call x14, Pallas kernels, call(): pl.pallas_call(kernel, name=name, out_shape=[jax.ShapeDtypeStruct(shape,...  14.3 us
    ppermute x3, starting transfers between devices, sent(): return lax.ppermute(message, 'tm', pairs).astype(f32)  4.19 us
    unnamed x18, local copies, waits for them, and re-layouts  1.63 us
  transfers between devices with their start and end apart: 24, of which 11 were waited for; matrix products, arithmetic and copies ran while one was open for 1% of the time, Pallas kernels for 7%

profile of v6, /device:TPU:0, one launch (start us, length us, event | category | flops | bytes accessed | tf_op | source)
XLA Modules:
  0.0 65.7 jit_solution(3835060076401471151)
XLA Ops:
  1.4 1.2 %pad_maximum_fusion.both = bf16[256,1024]{1,0:T(8,128)(2,1)S(1)} fusion(bf16[256,256]{1,0:T(8,128)(2,1)} %encoder.1, bf16[256,768]{1,0:T(8,128)(2,1)} %spectrum.1), kind=kLoop, calls=%fused_computation | loop fusion | flops 1048576 | bytes 1048576 | tf_op jit(solution)/shard_map/concatenate | solution.py:440
  2.7 0.8 %pieces.1 = (bf16[336,256]{1,0:T(8,128)(2,1)S(1)}, bf16[336,256]{1,0:T(8,128)(2,1)S(1)}, bf16[336,256]{1,0:T(8,128)(2,1)S(1)}, bf16[208,256]{1,0:T(8,128)(2,1)S(...) custom-call(s32[1,2]{1,0:T(1,128)S(1)} %add_bitcast_fusion.place, bf16[256,1024]{1,0:T(8,128)(2,1)S(1)} %pad_maximum_fusion.both), custom_call_target="tpu_custom_call" | custom-call | tf_op jit(solution)/shard_map/pieces/pallas_call | solution.py:23
  3.5 1.1 %summary.1 = (f32[208,128]{1,0:T(8,128)S(1)}, f32[8,256]{1,0:T(8,128)S(1)}, f32[4,256]{1,0:T(4,128)S(1)}) custom-call(s32[1,2]{1,0:T(1,128)S(1)} %add_bitcast_fusion.place, bf16[768,256]{1,0:T(8,128)(2,1)S(1)} %get-tuple-element.41.flipped, f32[1,1024]{1,0:T(1,128)S(1)} %bitcast.8), custom_call_target="tpu_custom_call" | custom-call | tf_op jit(solution)/shard_map/summary/pallas_call | solution.py:23
  5.1 4.7 %collective-permute-start = (bf16[336,256]{1,0:T(8,128)(2,1)S(1)}, bf16[336,256]{1,0:T(8,128)(2,1)S(1)}, u32[]{:S(2)}, u32[]{:S(2)}) collective-permute-start(bf16[336,256]{1,0:T(8,128)(2,1)S(1)} %get-tuple-element.44), channel_id=1, source_target_pairs={{0,3},{1,2},{2,1},{3,0},{4,7},{5,6},{6,5},{7,4},{8,11},{9,10},{10,... | collective-permute-start | bytes 516104 | tf_op jit(solution)/shard_map/ppermute | solution.py:406
  9.8 2.5 %collective-permute-start.4 = (f32[8,256]{1,0:T(8,128)S(1)}, f32[8,256]{1,0:T(8,128)S(1)}, u32[]{:S(2)}, u32[]{:S(2)}) collective-permute-start(f32[8,256]{1,0:T(8,128)S(1)} %pad_maximum_fusion.1.refs_1_), channel_id=1, source_target_pairs={{0,24},{4,28},{8,16},{12,20},{16,8},{20,12},{24,0},{28,4},{1,25},{... | collective-permute-start | bytes 24584 | tf_op jit(solution)/shard_map/ppermute | solution.py:406
  12.3 2.1 %collective-permute-done.4.refs_4_ = f32[8,256]{1,0:T(8,128)S(1)} collective-permute-done((f32[8,256]{1,0:T(8,128)S(1)}, f32[8,256]{1,0:T(8,128)S(1)}, u32[]{:S(2)}, u32[]{:S(2)}) %collective-permute-start.4) | collective-permute-done | bytes 8224 | tf_op jit(solution)/shard_map/ppermute | solution.py:406
  14.4 1.5 %collective-permute-start.3 = (f32[8,256]{1,0:T(8,128)S(1)}, f32[8,256]{1,0:T(8,128)S(1)}, u32[]{:S(2)}, u32[]{:S(2)}) collective-permute-start(f32[8,256]{1,0:T(8,128)S(1)} %pad_maximum_fusion.1.refs_1_), channel_id=1, source_target_pairs={{0,16},{4,20},{8,24},{12,28},{16,0},{20,4},{24,8},{28,12},{1,17},{... | collective-permute-start | bytes 24584 | tf_op jit(solution)/shard_map/ppermute | solution.py:406
  15.9 1.5 %collective-permute-start.2 = (f32[8,256]{1,0:T(8,128)S(1)}, f32[8,256]{1,0:T(8,128)S(1)}, u32[]{:S(2)}, u32[]{:S(2)}) collective-permute-start(f32[8,256]{1,0:T(8,128)S(1)} %pad_maximum_fusion.1.refs_1_), channel_id=1, source_target_pairs={{0,8},{4,12},{8,0},{12,4},{16,24},{20,28},{24,16},{28,20},{1,9},{5... | collective-permute-start | bytes 24584 | tf_op jit(solution)/shard_map/ppermute | solution.py:406
  17.4 1.6 %copy-done = bf16[256,4096]{1,0:T(8,128)(2,1)S(1)} copy-done((bf16[256,4096]{1,0:T(8,128)(2,1)S(1)}, bf16[256,4096]{1,0:T(8,128)(2,1)}, u32[]{:S(2)}) %copy-start) | copy-done | bytes 2097176
  19.6 0.8 %entry.1 = (f32[22,256]{1,0:T(8,128)S(1)}, f32[22,256]{1,0:T(8,128)S(1)}, f32[22,256]{1,0:T(8,128)S(1)}, f32[3,256]{1,0:T(4,128)S(1)}, f32[1,896]{1,0:T(1,128)S(1)}) custom-call(s32[1,2]{1,0:T(1,128)S(1)} %add_bitcast_fusion.place, f32[1,256]{1,0:T(1,128)S(1)} %bitcast.9, f32[1,256]{1,0:T(1,128)S(1)} %bitcast.10, f32[8,256]{1,0:T(8,128)S(1)} %get-tuple-element.42.states, ...), custom_call_target="tpu_custom_call" | custom-call | tf_op jit(solution)/shard_map/entry/pallas_call | solution.py:23
  20.4 1.5 %collective-permute-start.7 = (f32[22,256]{1,0:T(8,128)S(1)}, f32[22,256]{1,0:T(8,128)S(1)}, u32[]{:S(2)}, u32[]{:S(2)}) collective-permute-start(f32[22,256]{1,0:T(8,128)S(1)} %get-tuple-element.52), channel_id=1, source_target_pairs={{0,3},{1,2},{2,1},{3,0},{4,7},{5,6},{6,5},{7,4},{8,11},{9,10},{10,... | collective-permute-start | bytes 67592 | tf_op jit(solution)/shard_map/ppermute | solution.py:406
  21.9 2.7 %collective-permute-start.8 = (f32[22,256]{1,0:T(8,128)S(1)}, f32[22,256]{1,0:T(8,128)S(1)}, u32[]{:S(2)}, u32[]{:S(2)}) collective-permute-start(f32[22,256]{1,0:T(8,128)S(1)} %get-tuple-element.53), channel_id=1, source_target_pairs={{0,2},{1,3},{2,0},{3,1},{4,6},{5,7},{6,4},{7,5},{8,10},{9,11},{10,... | collective-permute-start | bytes 67592 | tf_op jit(solution)/shard_map/ppermute | solution.py:406
  24.9 0.9 %noise.1 = (f32[256,256]{1,0:T(8,128)S(1)}, f32[256,256]{1,0:T(8,128)S(1)}, f32[256,256]{1,0:T(8,128)S(1)}, f32[256,256]{1,0:T(8,128)S(1)}) custom-call(s32[1,2]{1,0:T(1,128)S(1)} %add_bitcast_fusion.place, f32[256,768]{1,0:T(8,128)S(1)} %copy-done.4, f32[2,256,768]{2,1,0:T(8,128)S(1)} %copy-done.2, s32[1,256]{1,0:T(1,128)S(1)} %bitcast.11), custom_call_target="tpu_custom_call" | custom-call | tf_op jit(solution)/shard_map/noise/pallas_call | solution.py:23
  26.7 1.8 %collective-permute-done.9.refs_5_.refs_2_ = f32[22,256]{1,0:T(8,128)S(1)} collective-permute-done((f32[22,256]{1,0:T(8,128)S(1)}, f32[22,256]{1,0:T(8,128)S(1)}, u32[]{:S(2)}, u32[]{:S(2)}) %collective-permute-start.9) | collective-permute-done | bytes 22560 | tf_op jit(solution)/shard_map/ppermute | solution.py:406
  29.3 0.7 %collective-permute-done.10.halves = bf16[384,256]{1,0:T(8,128)(2,1)S(1)} collective-permute-done((bf16[384,256]{1,0:T(8,128)(2,1)S(1)}, bf16[384,256]{1,0:T(8,128)(2,1)S(1)}, u32[]{:S(2)}, u32[]{:S(2)}) %collective-permute-start.10) | collective-permute-done | bytes 196640 | tf_op jit(solution)/shard_map/ppermute | solution.py:406
  30.0 1.3 %sampler.1 = (bf16[384,128]{1,0:T(8,128)(2,1)S(1)}, bf16[256,128]{1,0:T(8,128)(2,1)S(1)}) custom-call(s32[1,2]{1,0:T(1,128)S(1)} %add_bitcast_fusion.place, bf16[4,256,256]{2,1,0:T(8,128)(2,1)S(1)} %normed.1, bf16[256,256]{1,0:T(8,128)(2,1)S(1)} %copy-done.5, bf16[384,256]{1,0:T(8,128)(2,1)S(1)} %collective-permute-done.10.halves, ...), custom_call_target="tpu_custom_call" | custom-call | tf_op jit(solution)/shard_map/sampler/pallas_call | solution.py:23
  31.3 1.1 %collective-permute-start.14 = (bf16[384,128]{1,0:T(8,128)(2,1)S(1)}, bf16[384,128]{1,0:T(8,128)(2,1)S(1)}, u32[]{:S(2)}, u32[]{:S(2)}) collective-permute-start(bf16[384,128]{1,0:T(8,128)(2,1)S(1)} %get-tuple-element.59.own), channel_id=1, source_target_pairs={{0,1},{1,0},{2,3},{3,2},{4,5},{5,4},{6,7},{7,6},{8,9},{9,8},{10,11... | collective-permute-start | bytes 294920 | tf_op jit(solution)/shard_map/ppermute | solution.py:406
  32.4 2.0 %collective-permute-start.13 = (bf16[384,128]{1,0:T(8,128)(2,1)S(1)}, bf16[384,128]{1,0:T(8,128)(2,1)S(1)}, u32[]{:S(2)}, u32[]{:S(2)}) collective-permute-start(bf16[384,128]{1,0:T(8,128)(2,1)S(1)} %get-tuple-element.59.own), channel_id=1, source_target_pairs={{0,2},{1,3},{2,0},{3,1},{4,6},{5,7},{6,4},{7,5},{8,10},{9,11},{10,... | collective-permute-start | bytes 294920 | tf_op jit(solution)/shard_map/ppermute | solution.py:406
  34.4 1.3 %collective-permute-start.12 = (bf16[384,128]{1,0:T(8,128)(2,1)S(1)}, bf16[384,128]{1,0:T(8,128)(2,1)S(1)}, u32[]{:S(2)}, u32[]{:S(2)}) collective-permute-start(bf16[384,128]{1,0:T(8,128)(2,1)S(1)} %get-tuple-element.59.own), channel_id=1, source_target_pairs={{0,3},{1,2},{2,1},{3,0},{4,7},{5,6},{6,5},{7,4},{8,11},{9,10},{10,... | collective-permute-start | bytes 294920 | tf_op jit(solution)/shard_map/ppermute | solution.py:406
  35.7 1.3 %collective-permute-start.11 = (bf16[256,128]{1,0:T(8,128)(2,1)S(1)}, bf16[256,128]{1,0:T(8,128)(2,1)S(1)}, u32[]{:S(2)}, u32[]{:S(2)}) collective-permute-start(bf16[256,128]{1,0:T(8,128)(2,1)S(1)} %get-tuple-element.60), channel_id=1, source_target_pairs={{0,4},{4,8},{8,12},{12,16},{16,20},{20,24},{24,28},{1,5},{5,9},{9,... | collective-permute-start | bytes 196616 | tf_op jit(solution)/shard_map/ppermute | solution.py:528
  37.0 0.9 %collective-permute-done.11.rim = bf16[256,128]{1,0:T(8,128)(2,1)S(1)} collective-permute-done((bf16[256,128]{1,0:T(8,128)(2,1)S(1)}, bf16[256,128]{1,0:T(8,128)(2,1)S(1)}, u32[]{:S(2)}, u32[]{:S(2)}) %collective-permute-start.11) | collective-permute-done | bytes 65568 | tf_op jit(solution)/shard_map/ppermute | solution.py:528
  37.9 4.9 %collective-permute-done.13.refs_1_ = bf16[384,128]{1,0:T(8,128)(2,1)S(1)} collective-permute-done((bf16[384,128]{1,0:T(8,128)(2,1)S(1)}, bf16[384,128]{1,0:T(8,128)(2,1)S(1)}, u32[]{:S(2)}, u32[]{:S(2)}) %collective-permute-start.13) | collective-permute-done | bytes 98336 | tf_op jit(solution)/shard_map/ppermute | solution.py:406
  42.8 5.8 %rebuild.1 = (bf16[4096,768]{1,0:T(8,128)(2,1)S(1)}, bf16[768,256]{1,0:T(8,128)(2,1)S(1)}, f32[8,768]{1,0:T(8,128)S(1)}, f32[8,256]{1,0:T(8,128)S(1)}, f32[520,2...) custom-call(s32[1,2]{1,0:T(1,128)S(1)} %add_bitcast_fusion.place, ...), custom_call_target="tpu_custom_call" | custom-call | tf_op jit(solution)/shard_map/rebuild/pallas_call | solution.py:23
  49.3 1.5 %kept.1 = (f32[512,256]{1,0:T(8,128)S(1)}, f32[512,256]{1,0:T(8,128)S(1)}, f32[512,256]{1,0:T(8,128)S(1)}, f32[512,256]{1,0:T(8,128)S(1)}) custom-call(s32[1,2]{1,0:T(1,128)S(1)} %add_bitcast_fusion.place, bf16[4096,768]{1,0:T(8,128)(2,1)S(1)} %get-tuple-element.64.stacked, bf16[768,256]{1,0:T(8,128)(2,1)S(1)} %get-tuple-element.65.ratio), custom_call_target="tpu_custom_call" | custom-call | tf_op jit(solution)/shard_map/kept/pallas_call | solution.py:23
  51.0 1.6 %collective-permute-start.16 = (f16[528,256]{1,0:T(8,128)(2,1)S(1)}, f16[528,256]{1,0:T(8,128)(2,1)S(1)}, u32[]{:S(2)}, u32[]{:S(2)}) collective-permute-start(f16[528,256]{1,0:T(8,128)(2,1)S(1)} %convert_element_type.24), channel_id=1, source_target_pairs={{0,8},{4,20},{8,0},{12,28},{16,24},{20,4},{24,16},{28,12},{1,9},{5... | collective-permute-start | bytes 811016 | tf_op jit(solution)/shard_map/ppermute | solution.py:574
  52.8 1.6 %collective-permute-start.21 = (f16[528,256]{1,0:T(8,128)(2,1)S(1)}, f16[528,256]{1,0:T(8,128)(2,1)S(1)}, u32[]{:S(2)}, u32[]{:S(2)}) collective-permute-start(f16[528,256]{1,0:T(8,128)(2,1)S(1)} %convert_element_type.26), channel_id=1, source_target_pairs={{0,8},{4,20},{8,0},{12,28},{16,24},{20,4},{24,16},{28,12},{1,9},{5... | collective-permute-start | bytes 811016 | tf_op jit(solution)/shard_map/ppermute | solution.py:574
  54.4 1.9 %collective-permute-start.18 = (f32[1,768]{1,0:T(1,128)S(1)}, f32[1,768]{1,0:T(1,128)S(1)}, u32[]{:S(2)}, u32[]{:S(2)}) collective-permute-start(f32[1,768]{1,0:T(1,128)S(1)} %slice.10), channel_id=1, source_target_pairs={{0,1},{1,0},{2,3},{3,2},{4,5},{5,4},{6,7},{7,6},{8,9},{9,8},{10,11... | collective-permute-start | bytes 9224 | tf_op jit(solution)/shard_map/ppermute | solution.py:406
  56.3 1.7 %collective-permute-done.18 = f32[1,768]{1,0:T(1,128)S(1)} collective-permute-done((f32[1,768]{1,0:T(1,128)S(1)}, f32[1,768]{1,0:T(1,128)S(1)}, u32[]{:S(2)}, u32[]{:S(2)}) %collective-permute-start.18) | collective-permute-done | bytes 3104 | tf_op jit(solution)/shard_map/ppermute | solution.py:406
  58.2 1.1 %collective-permute-start.23 = (f16[528,256]{1,0:T(8,128)(2,1)S(1)}, f16[528,256]{1,0:T(8,128)(2,1)S(1)}, u32[]{:S(2)}, u32[]{:S(2)}) collective-permute-start(f16[528,256]{1,0:T(8,128)(2,1)S(1)} %convert_element_type.28), channel_id=1, source_target_pairs={{0,16},{4,12},{8,24},{12,4},{16,0},{20,28},{24,8},{28,20},{1,17},{... | collective-permute-start | bytes 811016 | tf_op jit(solution)/shard_map/ppermute | solution.py:574
  59.3 2.3 %collective-permute-start.19 = (f32[1,768]{1,0:T(1,128)S(1)}, f32[1,768]{1,0:T(1,128)S(1)}, u32[]{:S(2)}, u32[]{:S(2)}) collective-permute-start(f32[1,768]{1,0:T(1,128)S(1)} %add.14), channel_id=1, source_target_pairs={{0,2},{1,3},{2,0},{3,1},{4,6},{5,7},{6,4},{7,5},{8,10},{9,11},{10,... | collective-permute-start | bytes 9224 | tf_op jit(solution)/shard_map/ppermute | solution.py:406
  61.6 2.2 %collective-permute-done.19 = f32[1,768]{1,0:T(1,128)S(1)} collective-permute-done((f32[1,768]{1,0:T(1,128)S(1)}, f32[1,768]{1,0:T(1,128)S(1)}, u32[]{:S(2)}, u32[]{:S(2)}) %collective-permute-start.19) | collective-permute-done | bytes 3104 | tf_op jit(solution)/shard_map/ppermute | solution.py:406
  64.8 0.9 %total.1 = f32[512,256]{1,0:T(8,128)} custom-call(f32[512,256]{1,0:T(8,128)S(1)} %get-tuple-element.72.kept, f32[520,256]{1,0:T(8,128)S(1)} %collective-permute-done.20.crossed, f32[528,256]{1,0:T(8,128)S(1)} %convert_element_type.27.refs_0_, f32[528,256]{1,0:T(8,128)S(1)} %convert_element_type.29.refs_1_), custom_call_target="tpu_custom_call" | custom-call | tf_op jit(solution)/shard_map/total/pallas_call | solution.py:23
  (61 shorter events, 6.1 us)
Async XLA Ops:
  0.6 18.9 %copy-start.6 = (f32[256]{0:T(256)S(1)}, f32[256]{0:T(256)}, u32[]{:S(2)}) copy-start(f32[256]{0:T(256)} %param.10) | copy-start | bytes 3076
  0.6 18.9 %copy-start.7 = (f32[256]{0:T(256)S(1)}, f32[256]{0:T(256)}, u32[]{:S(2)}) copy-start(f32[256]{0:T(256)} %param.11) | copy-start | bytes 3076
  1.4 23.4 %copy-start.2 = (f32[2,256,768]{2,1,0:T(8,128)S(1)}, f32[2,256,768]{2,1,0:T(8,128)}, u32[]{:S(2)}) copy-start(f32[2,256,768]{2,1,0:T(8,128)} %uniform.1) | copy-start | bytes 4718596
  1.4 23.4 %copy-start.8 = (s32[256]{0:T(256)S(1)}, s32[256]{0:T(256)}, u32[]{:S(2)}) copy-start(s32[256]{0:T(256)} %param.16) | copy-start | bytes 3076
  4.6 5.2 %collective-permute-start.1 = (f32[4,256]{1,0:T(4,128)S(1)}, f32[4,256]{1,0:T(4,128)S(1)}, u32[]{:S(2)}, u32[]{:S(2)}) collective-permute-start(f32[4,256]{1,0:T(4,128)S(1)} %get-tuple-element.45), channel_id=1, source_target_pairs={{0,4},{4,0},{8,12},{12,8},{16,20},{20,16},{24,28},{28,24},{1,5},{5... | collective-permute-start | bytes 12296 | tf_op jit(solution)/shard_map/ppermute | solution.py:406
  5.1 14.5 %collective-permute-start = (bf16[336,256]{1,0:T(8,128)(2,1)S(1)}, bf16[336,256]{1,0:T(8,128)(2,1)S(1)}, u32[]{:S(2)}, u32[]{:S(2)}) collective-permute-start(bf16[336,256]{1,0:T(8,128)(2,1)S(1)} %get-tuple-element.44), channel_id=1, source_target_pairs={{0,3},{1,2},{2,1},{3,0},{4,7},{5,6},{6,5},{7,4},{8,11},{9,10},{10,... | collective-permute-start | bytes 516104 | tf_op jit(solution)/shard_map/ppermute | solution.py:406
  9.8 4.6 %collective-permute-start.4 = (f32[8,256]{1,0:T(8,128)S(1)}, f32[8,256]{1,0:T(8,128)S(1)}, u32[]{:S(2)}, u32[]{:S(2)}) collective-permute-start(f32[8,256]{1,0:T(8,128)S(1)} %pad_maximum_fusion.1.refs_1_), channel_id=1, source_target_pairs={{0,24},{4,28},{8,16},{12,20},{16,8},{20,12},{24,0},{28,4},{1,25},{... | collective-permute-start | bytes 24584 | tf_op jit(solution)/shard_map/ppermute | solution.py:406
  12.3 13.5 %collective-permute-start.5 = (bf16[336,256]{1,0:T(8,128)(2,1)S(1)}, bf16[336,256]{1,0:T(8,128)(2,1)S(1)}, u32[]{:S(2)}, u32[]{:S(2)}) collective-permute-start(bf16[336,256]{1,0:T(8,128)(2,1)S(1)} %get-tuple-element.50), channel_id=1, source_target_pairs={{0,2},{1,3},{2,0},{3,1},{4,6},{5,7},{6,4},{7,5},{8,10},{9,11},{10,... | collective-permute-start | bytes 516104 | tf_op jit(solution)/shard_map/ppermute | solution.py:406
  14.4 11.4 %collective-permute-start.6 = (bf16[336,256]{1,0:T(8,128)(2,1)S(1)}, bf16[336,256]{1,0:T(8,128)(2,1)S(1)}, u32[]{:S(2)}, u32[]{:S(2)}) collective-permute-start(bf16[336,256]{1,0:T(8,128)(2,1)S(1)} %get-tuple-element.51), channel_id=1, source_target_pairs={{0,1},{1,0},{2,3},{3,2},{4,5},{5,4},{6,7},{7,6},{8,9},{9,8},{10,11... | collective-permute-start | bytes 516104 | tf_op jit(solution)/shard_map/ppermute | solution.py:406
  14.4 4.9 %collective-permute-start.3 = (f32[8,256]{1,0:T(8,128)S(1)}, f32[8,256]{1,0:T(8,128)S(1)}, u32[]{:S(2)}, u32[]{:S(2)}) collective-permute-start(f32[8,256]{1,0:T(8,128)S(1)} %pad_maximum_fusion.1.refs_1_), channel_id=1, source_target_pairs={{0,16},{4,20},{8,24},{12,28},{16,0},{20,4},{24,8},{28,12},{1,17},{... | collective-permute-start | bytes 24584 | tf_op jit(solution)/shard_map/ppermute | solution.py:406
  15.9 3.7 %collective-permute-start.2 = (f32[8,256]{1,0:T(8,128)S(1)}, f32[8,256]{1,0:T(8,128)S(1)}, u32[]{:S(2)}, u32[]{:S(2)}) collective-permute-start(f32[8,256]{1,0:T(8,128)S(1)} %pad_maximum_fusion.1.refs_1_), channel_id=1, source_target_pairs={{0,8},{4,12},{8,0},{12,4},{16,24},{20,28},{24,16},{28,20},{1,9},{5... | collective-permute-start | bytes 24584 | tf_op jit(solution)/shard_map/ppermute | solution.py:406
  19.0 5.9 %copy-start.4 = (f32[256,768]{1,0:T(8,128)S(1)}, f32[256,768]{1,0:T(8,128)}, u32[]{:S(2)}) copy-start(f32[256,768]{1,0:T(8,128)} %gauss.1) | copy-start | bytes 2359300
  20.4 5.7 %collective-permute-start.7 = (f32[22,256]{1,0:T(8,128)S(1)}, f32[22,256]{1,0:T(8,128)S(1)}, u32[]{:S(2)}, u32[]{:S(2)}) collective-permute-start(f32[22,256]{1,0:T(8,128)S(1)} %get-tuple-element.52), channel_id=1, source_target_pairs={{0,3},{1,2},{2,1},{3,0},{4,7},{5,6},{6,5},{7,4},{8,11},{9,10},{10,... | collective-permute-start | bytes 67592 | tf_op jit(solution)/shard_map/ppermute | solution.py:406
  21.9 4.8 %collective-permute-start.8 = (f32[22,256]{1,0:T(8,128)S(1)}, f32[22,256]{1,0:T(8,128)S(1)}, u32[]{:S(2)}, u32[]{:S(2)}) collective-permute-start(f32[22,256]{1,0:T(8,128)S(1)} %get-tuple-element.53), channel_id=1, source_target_pairs={{0,2},{1,3},{2,0},{3,1},{4,6},{5,7},{6,4},{7,5},{8,10},{9,11},{10,... | collective-permute-start | bytes 67592 | tf_op jit(solution)/shard_map/ppermute | solution.py:406
  24.6 3.8 %collective-permute-start.9 = (f32[22,256]{1,0:T(8,128)S(1)}, f32[22,256]{1,0:T(8,128)S(1)}, u32[]{:S(2)}, u32[]{:S(2)}) collective-permute-start(f32[22,256]{1,0:T(8,128)S(1)} %get-tuple-element.54), channel_id=1, source_target_pairs={{0,1},{1,0},{2,3},{3,2},{4,5},{5,4},{6,7},{7,6},{8,9},{9,8},{10,11... | collective-permute-start | bytes 67592 | tf_op jit(solution)/shard_map/ppermute | solution.py:406
  24.9 5.2 %copy-start.5 = (bf16[256,256]{1,0:T(8,128)(2,1)S(1)}, bf16[256,256]{1,0:T(8,128)(2,1)}, u32[]{:S(2)}) copy-start(bf16[256,256]{1,0:T(8,128)(2,1)} %encoder.1) | copy-start | bytes 393220
  28.5 14.3 %copy-start.1 = (bf16[256,4096]{1,0:T(8,128)(2,1)S(1)}, bf16[256,4096]{1,0:T(8,128)(2,1)}, u32[]{:S(2)}) copy-start(bf16[256,4096]{1,0:T(8,128)(2,1)} %templates.3) | copy-start | bytes 6291460
  28.5 14.3 %copy-start.3 = (bf16[256,768]{1,0:T(8,128)(2,1)S(1)}, bf16[256,768]{1,0:T(8,128)(2,1)}, u32[]{:S(2)}) copy-start(bf16[256,768]{1,0:T(8,128)(2,1)} %spectrum.1) | copy-start | bytes 1179652
  28.5 1.5 %collective-permute-start.10 = (bf16[384,256]{1,0:T(8,128)(2,1)S(1)}, bf16[384,256]{1,0:T(8,128)(2,1)S(1)}, u32[]{:S(2)}, u32[]{:S(2)}) collective-permute-start(bf16[384,256]{1,0:T(8,128)(2,1)S(1)} %halves.1), channel_id=1, source_target_pairs={{0,4},{4,0},{8,12},{12,8},{16,20},{20,16},{24,28},{28,24},{1,5},{5... | collective-permute-start | bytes 589832 | tf_op jit(solution)/shard_map/ppermute | solution.py:406
  31.3 6.6 %collective-permute-start.14 = (bf16[384,128]{1,0:T(8,128)(2,1)S(1)}, bf16[384,128]{1,0:T(8,128)(2,1)S(1)}, u32[]{:S(2)}, u32[]{:S(2)}) collective-permute-start(bf16[384,128]{1,0:T(8,128)(2,1)S(1)} %get-tuple-element.59.own), channel_id=1, source_target_pairs={{0,1},{1,0},{2,3},{3,2},{4,5},{5,4},{6,7},{7,6},{8,9},{9,8},{10,11... | collective-permute-start | bytes 294920 | tf_op jit(solution)/shard_map/ppermute | solution.py:406
  32.4 10.5 %collective-permute-start.13 = (bf16[384,128]{1,0:T(8,128)(2,1)S(1)}, bf16[384,128]{1,0:T(8,128)(2,1)S(1)}, u32[]{:S(2)}, u32[]{:S(2)}) collective-permute-start(bf16[384,128]{1,0:T(8,128)(2,1)S(1)} %get-tuple-element.59.own), channel_id=1, source_target_pairs={{0,2},{1,3},{2,0},{3,1},{4,6},{5,7},{6,4},{7,5},{8,10},{9,11},{10,... | collective-permute-start | bytes 294920 | tf_op jit(solution)/shard_map/ppermute | solution.py:406
  34.4 8.4 %collective-permute-start.12 = (bf16[384,128]{1,0:T(8,128)(2,1)S(1)}, bf16[384,128]{1,0:T(8,128)(2,1)S(1)}, u32[]{:S(2)}, u32[]{:S(2)}) collective-permute-start(bf16[384,128]{1,0:T(8,128)(2,1)S(1)} %get-tuple-element.59.own), channel_id=1, source_target_pairs={{0,3},{1,2},{2,1},{3,0},{4,7},{5,6},{6,5},{7,4},{8,11},{9,10},{10,... | collective-permute-start | bytes 294920 | tf_op jit(solution)/shard_map/ppermute | solution.py:406
  35.7 2.2 %collective-permute-start.11 = (bf16[256,128]{1,0:T(8,128)(2,1)S(1)}, bf16[256,128]{1,0:T(8,128)(2,1)S(1)}, u32[]{:S(2)}, u32[]{:S(2)}) collective-permute-start(bf16[256,128]{1,0:T(8,128)(2,1)S(1)} %get-tuple-element.60), channel_id=1, source_target_pairs={{0,4},{4,8},{8,12},{12,16},{16,20},{20,24},{24,28},{1,5},{5,9},{9,... | collective-permute-start | bytes 196616 | tf_op jit(solution)/shard_map/ppermute | solution.py:528
  48.7 2.2 %collective-permute-start.15 = (f32[520,256]{1,0:T(8,128)S(1)}, f32[520,256]{1,0:T(8,128)S(1)}, u32[]{:S(2)}, u32[]{:S(2)}) collective-permute-start(f32[520,256]{1,0:T(8,128)S(1)} %get-tuple-element.67), channel_id=1, source_target_pairs={{0,4},{4,0},{8,12},{12,8},{16,20},{20,16},{24,28},{28,24},{1,5},{5... | collective-permute-start | bytes 1597448 | tf_op jit(solution)/shard_map/ppermute | solution.py:406
  48.7 4.0 %collective-permute-start.17 = (f32[520,256]{1,0:T(8,128)S(1)}, f32[520,256]{1,0:T(8,128)S(1)}, u32[]{:S(2)}, u32[]{:S(2)}) collective-permute-start(f32[520,256]{1,0:T(8,128)S(1)} %get-tuple-element.69), channel_id=1, source_target_pairs={{0,4},{4,0},{8,12},{12,8},{16,20},{20,16},{24,28},{28,24},{1,5},{5... | collective-permute-start | bytes 1597448 | tf_op jit(solution)/shard_map/ppermute | solution.py:406
  49.2 8.8 %collective-permute-start.22 = (f32[520,256]{1,0:T(8,128)S(1)}, f32[520,256]{1,0:T(8,128)S(1)}, u32[]{:S(2)}, u32[]{:S(2)}) collective-permute-start(f32[520,256]{1,0:T(8,128)S(1)} %get-tuple-element.76), channel_id=1, source_target_pairs={{0,4},{4,0},{8,12},{12,8},{16,20},{20,16},{24,28},{28,24},{1,5},{5... | collective-permute-start | bytes 1597448 | tf_op jit(solution)/shard_map/ppermute | solution.py:406
  51.0 7.0 %collective-permute-start.16 = (f16[528,256]{1,0:T(8,128)(2,1)S(1)}, f16[528,256]{1,0:T(8,128)(2,1)S(1)}, u32[]{:S(2)}, u32[]{:S(2)}) collective-permute-start(f16[528,256]{1,0:T(8,128)(2,1)S(1)} %convert_element_type.24), channel_id=1, source_target_pairs={{0,8},{4,20},{8,0},{12,28},{16,24},{20,4},{24,16},{28,12},{1,9},{5... | collective-permute-start | bytes 811016 | tf_op jit(solution)/shard_map/ppermute | solution.py:574
  52.5 12.2 %collective-permute-start.20 = (f32[520,256]{1,0:T(8,128)S(1)}, f32[520,256]{1,0:T(8,128)S(1)}, u32[]{:S(2)}, u32[]{:S(2)}) collective-permute-start(f32[520,256]{1,0:T(8,128)S(1)} %get-tuple-element.73), channel_id=1, source_target_pairs={{0,4},{4,0},{8,12},{12,8},{16,20},{20,16},{24,28},{28,24},{1,5},{5... | collective-permute-start | bytes 1597448 | tf_op jit(solution)/shard_map/ppermute | solution.py:406
  52.8 8.7 %collective-permute-start.21 = (f16[528,256]{1,0:T(8,128)(2,1)S(1)}, f16[528,256]{1,0:T(8,128)(2,1)S(1)}, u32[]{:S(2)}, u32[]{:S(2)}) collective-permute-start(f16[528,256]{1,0:T(8,128)(2,1)S(1)} %convert_element_type.26), channel_id=1, source_target_pairs={{0,8},{4,20},{8,0},{12,28},{16,24},{20,4},{24,16},{28,12},{1,9},{5... | collective-permute-start | bytes 811016 | tf_op jit(solution)/shard_map/ppermute | solution.py:574
  54.4 3.6 %collective-permute-start.18 = (f32[1,768]{1,0:T(1,128)S(1)}, f32[1,768]{1,0:T(1,128)S(1)}, u32[]{:S(2)}, u32[]{:S(2)}) collective-permute-start(f32[1,768]{1,0:T(1,128)S(1)} %slice.10), channel_id=1, source_target_pairs={{0,1},{1,0},{2,3},{3,2},{4,5},{5,4},{6,7},{7,6},{8,9},{9,8},{10,11... | collective-permute-start | bytes 9224 | tf_op jit(solution)/shard_map/ppermute | solution.py:406
  58.2 6.5 %collective-permute-start.23 = (f16[528,256]{1,0:T(8,128)(2,1)S(1)}, f16[528,256]{1,0:T(8,128)(2,1)S(1)}, u32[]{:S(2)}, u32[]{:S(2)}) collective-permute-start(f16[528,256]{1,0:T(8,128)(2,1)S(1)} %convert_element_type.28), channel_id=1, source_target_pairs={{0,16},{4,12},{8,24},{12,4},{16,0},{20,28},{24,8},{28,20},{1,17},{... | collective-permute-start | bytes 811016 | tf_op jit(solution)/shard_map/ppermute | solution.py:574
  59.3 4.5 %collective-permute-start.19 = (f32[1,768]{1,0:T(1,128)S(1)}, f32[1,768]{1,0:T(1,128)S(1)}, u32[]{:S(2)}, u32[]{:S(2)}) collective-permute-start(f32[1,768]{1,0:T(1,128)S(1)} %add.14), channel_id=1, source_target_pairs={{0,2},{1,3},{2,0},{3,1},{4,6},{5,7},{6,4},{7,5},{8,10},{9,11},{10,... | collective-permute-start | bytes 9224 | tf_op jit(solution)/shard_map/ppermute | solution.py:406
  (1 other events, 1.6 us)

commit v7 on v6

--- a/solution.py
+++ b/solution.py
@@ -52,9 +52,9 @@
     return (size - 1 - lax.broadcasted_iota(jnp.int32, (size, 1), 0)).astype(f32)
 
 
-def pieces_kernel(nf, place, both, *refs):
-    messages, (own, flipped, frame_sums, frames_first) = refs[: nf - 1], refs[nf - 1 :]
-    frames, bins = flipped.shape
+def pieces_kernel(nf, place, both, small, *refs):
+    messages, (own, frame_sums, *summary, frames_first, all_gains) = refs[: nf - 1], refs[nf - 1 :]
+    frames, bins = frames_first.shape
     spectrum, encoder = both.at[:, 0:frames], both.at[:, frames:]
     piece = frames // nf
     half = encoder.shape[0] // 2
@@ -62,7 +62,6 @@
     spectral = spectrum[...].astype(f32)
     turned = jnp.transpose(spectral)
     frames_first[...] = turned
-    flipped[...] = turned.astype(bf16)
     for step in range(nf):
         target = own if step == 0 else messages[-step]
         start = pl.multiple_of((here ^ step) * piece, piece)
@@ -74,10 +73,11 @@
     total = jnp.sum(spectral, axis=0, keepdims=True)
     for row in range(frames // bins):
         frame_sums[row : row + 1, :] = total[:, row * bins : (row + 1) * bins]
-
-
-def summary_kernel(nf, place, flipped, small, gains, states, tm_message, all_gains):
-    frames, bins = flipped.shape
+    summarize(nf, place, frames_first, small, *summary, all_gains)
+
+
+def summarize(nf, place, frames_first, small, gains, states, tm_message, all_gains):
+    frames, bins = frames_first.shape
     piece = frames // nf
     here = place[0, 0]
     clip_row = small[:, bins:]
@@ -94,7 +94,7 @@
     gains[piece:, :] = gain[frames - TAIL :]
     rate = small[:, 0:bins]
     keep = log_keep(rate)
-    scaled = flipped[...].astype(f32) * wide(1.0 / gain, bins) * rate
+    scaled = frames_first[...] * wide(1.0 / gain, bins) * rate
     weights = jnp.exp(steps_down(piece) * keep)
     state = jnp.zeros((1, bins), f32)
     states[...] = jnp.zeros_like(states)
@@ -430,24 +430,16 @@
     state_rows = -(-(nf + 1) // 8) * 8
     height = 1 + frames // bins
 
-    *messages, own, flipped, frame_sums = call(
+    small = jnp.pad(decay_rate, (0, frames)) + jnp.pad(clip_ids, (bins, 0)).astype(f32)
+    *messages, own, frame_sums, gains, states, tm_message = call(
         functools.partial(pieces_kernel, nf),
         "pieces",
         [((rows + topics // 2, bins), bf16)] * (nf - 1)
-        + [((rows, bins), bf16), ((frames, bins), bf16), ((frames // bins, bins), f32)],
-        [((frames, bins), f32)],
+        + [((rows, bins), bf16), ((frames // bins, bins), f32), ((rows, LANES), f32)]
+        + [((state_rows, bins), f32), ((height, bins), f32)],
+        [((frames, bins), f32), ((frames, LANES), f32)],
         place,
         jnp.concatenate([spectrum, encoder], axis=1),
-        scalars=1,
-    )
-    small = jnp.pad(decay_rate, (0, frames)) + jnp.pad(clip_ids, (bins, 0)).astype(f32)
-    gains, states, tm_message = call(
-        functools.partial(summary_kernel, nf),
-        "summary",
-        [((rows, LANES), f32), ((state_rows, bins), f32), ((height, bins), f32)],
-        [((frames, LANES), f32)],
-        place,
-        flipped,
         small[None],
         scalars=1,
     )

time: 65.9 us -> 65.2 us (0.989)
    pallas_call x14 -> x13, Pallas kernels: 14.3 us -> 13.7 us  [call(): pl.pallas_call(kernel, name=name, out_shape=[jax.ShapeDtypeStruct(shape,...]
where the time goes in v7:
time: 65.2 us; the launch traced here: 65 us
  starting transfers between devices  30.1 us (46%)
  waiting for transfers between devices  15.8 us (24%)
  Pallas kernels  13.7 us (21%)
  other arithmetic  2.88 us (4%)
  local copies, waits for them, and re-layouts  1.63 us (2%)
  between operations  0.9 us (1%)
    ppermute x20, starting transfers between devices, exchanged(): lax.ppermute(value, axis, [(index, index ^ step) for index in range(size)])  24.7 us
    ppermute x20, waiting for transfers between devices, exchanged(): lax.ppermute(value, axis, [(index, index ^ step) for index in range(size)])  14.6 us
    pallas_call x13, Pallas kernels, call(): pl.pallas_call(kernel, name=name, out_shape=[jax.ShapeDtypeStruct(shape,...  13.7 us
    ppermute x3, starting transfers between devices, sent(): return lax.ppermute(message, 'tm', pairs).astype(f32)  4.19 us
    unnamed x18, local copies, waits for them, and re-layouts  1.63 us
  transfers between devices with their start and end apart: 24, of which 11 were waited for; matrix products, arithmetic and copies ran while one was open for 1% of the time, Pallas kernels for 7%

profile of v7, /device:TPU:0, one launch (start us, length us, event | category | flops | bytes accessed | tf_op | source)
XLA Modules:
  0.0 65.0 jit_solution(9920352079557166122)
XLA Ops:
  0.8 0.8 %convert_add_fusion = f32[1024]{0:T(1024)S(1)} fusion(s32[768]{0:T(1024)} %param.12, f32[256]{0:T(256)} %param.10), kind=kLoop, calls=%fused_computation.2 | loop fusion | flops 2048 | bytes 8192 | tf_op jit(solution)/shard_map/add | solution.py:433
  1.6 1.1 %pad_maximum_fusion.both = bf16[256,1024]{1,0:T(8,128)(2,1)S(1)} fusion(bf16[256,256]{1,0:T(8,128)(2,1)} %encoder.1, bf16[256,768]{1,0:T(8,128)(2,1)} %spectrum.1), kind=kLoop, calls=%fused_computation | loop fusion | flops 1048576 | bytes 1048576 | tf_op jit(solution)/shard_map/concatenate | solution.py:442
  2.7 1.2 %pieces.1 = (bf16[336,256]{1,0:T(8,128)(2,1)S(1)}, bf16[336,256]{1,0:T(8,128)(2,1)S(1)}, bf16[336,256]{1,0:T(8,128)(2,1)S(1)}, bf16[208,256]{1,0:T(8,128)(2,1)S(...) custom-call(s32[1,2]{1,0:T(1,128)S(1)} %add_bitcast_fusion.place, ...), custom_call_target="tpu_custom_call" | custom-call | tf_op jit(solution)/shard_map/pieces/pallas_call | solution.py:23
  4.4 4.7 %collective-permute-start = (bf16[336,256]{1,0:T(8,128)(2,1)S(1)}, bf16[336,256]{1,0:T(8,128)(2,1)S(1)}, u32[]{:S(2)}, u32[]{:S(2)}) collective-permute-start(bf16[336,256]{1,0:T(8,128)(2,1)S(1)} %get-tuple-element.42), channel_id=1, source_target_pairs={{0,3},{1,2},{2,1},{3,0},{4,7},{5,6},{6,5},{7,4},{8,11},{9,10},{10,... | collective-permute-start | bytes 516104 | tf_op jit(solution)/shard_map/ppermute | solution.py:406
  9.1 2.5 %collective-permute-start.4 = (f32[8,256]{1,0:T(8,128)S(1)}, f32[8,256]{1,0:T(8,128)S(1)}, u32[]{:S(2)}, u32[]{:S(2)}) collective-permute-start(f32[8,256]{1,0:T(8,128)S(1)} %pad_maximum_fusion.1.refs_1_), channel_id=1, source_target_pairs={{0,24},{4,28},{8,16},{12,20},{16,8},{20,12},{24,0},{28,4},{1,25},{... | collective-permute-start | bytes 24584 | tf_op jit(solution)/shard_map/ppermute | solution.py:406
  11.6 2.1 %collective-permute-done.4.refs_4_ = f32[8,256]{1,0:T(8,128)S(1)} collective-permute-done((f32[8,256]{1,0:T(8,128)S(1)}, f32[8,256]{1,0:T(8,128)S(1)}, u32[]{:S(2)}, u32[]{:S(2)}) %collective-permute-start.4) | collective-permute-done | bytes 8224 | tf_op jit(solution)/shard_map/ppermute | solution.py:406
  13.7 1.5 %collective-permute-start.3 = (f32[8,256]{1,0:T(8,128)S(1)}, f32[8,256]{1,0:T(8,128)S(1)}, u32[]{:S(2)}, u32[]{:S(2)}) collective-permute-start(f32[8,256]{1,0:T(8,128)S(1)} %pad_maximum_fusion.1.refs_1_), channel_id=1, source_target_pairs={{0,16},{4,20},{8,24},{12,28},{16,0},{20,4},{24,8},{28,12},{1,17},{... | collective-permute-start | bytes 24584 | tf_op jit(solution)/shard_map/ppermute | solution.py:406
  15.2 1.5 %collective-permute-start.2 = (f32[8,256]{1,0:T(8,128)S(1)}, f32[8,256]{1,0:T(8,128)S(1)}, u32[]{:S(2)}, u32[]{:S(2)}) collective-permute-start(f32[8,256]{1,0:T(8,128)S(1)} %pad_maximum_fusion.1.refs_1_), channel_id=1, source_target_pairs={{0,8},{4,12},{8,0},{12,4},{16,24},{20,28},{24,16},{28,20},{1,9},{5... | collective-permute-start | bytes 24584 | tf_op jit(solution)/shard_map/ppermute | solution.py:406
  16.7 1.6 %copy-done = bf16[256,4096]{1,0:T(8,128)(2,1)S(1)} copy-done((bf16[256,4096]{1,0:T(8,128)(2,1)S(1)}, bf16[256,4096]{1,0:T(8,128)(2,1)}, u32[]{:S(2)}) %copy-start) | copy-done | bytes 2097176
  18.9 0.8 %entry.1 = (f32[22,256]{1,0:T(8,128)S(1)}, f32[22,256]{1,0:T(8,128)S(1)}, f32[22,256]{1,0:T(8,128)S(1)}, f32[3,256]{1,0:T(4,128)S(1)}, f32[1,896]{1,0:T(1,128)S(1)}) custom-call(s32[1,2]{1,0:T(1,128)S(1)} %add_bitcast_fusion.place, f32[1,256]{1,0:T(1,128)S(1)} %bitcast.9, f32[1,256]{1,0:T(1,128)S(1)} %bitcast.10, f32[8,256]{1,0:T(8,128)S(1)} %get-tuple-element.40.states, ...), custom_call_target="tpu_custom_call" | custom-call | tf_op jit(solution)/shard_map/entry/pallas_call | solution.py:23
  19.7 1.5 %collective-permute-start.7 = (f32[22,256]{1,0:T(8,128)S(1)}, f32[22,256]{1,0:T(8,128)S(1)}, u32[]{:S(2)}, u32[]{:S(2)}) collective-permute-start(f32[22,256]{1,0:T(8,128)S(1)} %get-tuple-element.50), channel_id=1, source_target_pairs={{0,3},{1,2},{2,1},{3,0},{4,7},{5,6},{6,5},{7,4},{8,11},{9,10},{10,... | collective-permute-start | bytes 67592 | tf_op jit(solution)/shard_map/ppermute | solution.py:406
  21.3 2.7 %collective-permute-start.8 = (f32[22,256]{1,0:T(8,128)S(1)}, f32[22,256]{1,0:T(8,128)S(1)}, u32[]{:S(2)}, u32[]{:S(2)}) collective-permute-start(f32[22,256]{1,0:T(8,128)S(1)} %get-tuple-element.51), channel_id=1, source_target_pairs={{0,2},{1,3},{2,0},{3,1},{4,6},{5,7},{6,4},{7,5},{8,10},{9,11},{10,... | collective-permute-start | bytes 67592 | tf_op jit(solution)/shard_map/ppermute | solution.py:406
  24.2 0.9 %noise.1 = (f32[256,256]{1,0:T(8,128)S(1)}, f32[256,256]{1,0:T(8,128)S(1)}, f32[256,256]{1,0:T(8,128)S(1)}, f32[256,256]{1,0:T(8,128)S(1)}) custom-call(s32[1,2]{1,0:T(1,128)S(1)} %add_bitcast_fusion.place, f32[256,768]{1,0:T(8,128)S(1)} %copy-done.4, f32[2,256,768]{2,1,0:T(8,128)S(1)} %copy-done.2, s32[1,256]{1,0:T(1,128)S(1)} %bitcast.11), custom_call_target="tpu_custom_call" | custom-call | tf_op jit(solution)/shard_map/noise/pallas_call | solution.py:23
  26.0 1.8 %collective-permute-done.9.refs_5_.refs_2_ = f32[22,256]{1,0:T(8,128)S(1)} collective-permute-done((f32[22,256]{1,0:T(8,128)S(1)}, f32[22,256]{1,0:T(8,128)S(1)}, u32[]{:S(2)}, u32[]{:S(2)}) %collective-permute-start.9) | collective-permute-done | bytes 22560 | tf_op jit(solution)/shard_map/ppermute | solution.py:406
  28.6 0.7 %collective-permute-done.10.halves = bf16[384,256]{1,0:T(8,128)(2,1)S(1)} collective-permute-done((bf16[384,256]{1,0:T(8,128)(2,1)S(1)}, bf16[384,256]{1,0:T(8,128)(2,1)S(1)}, u32[]{:S(2)}, u32[]{:S(2)}) %collective-permute-start.10) | collective-permute-done | bytes 196640 | tf_op jit(solution)/shard_map/ppermute | solution.py:406
  29.4 1.3 %sampler.1 = (bf16[384,128]{1,0:T(8,128)(2,1)S(1)}, bf16[256,128]{1,0:T(8,128)(2,1)S(1)}) custom-call(s32[1,2]{1,0:T(1,128)S(1)} %add_bitcast_fusion.place, bf16[4,256,256]{2,1,0:T(8,128)(2,1)S(1)} %normed.1, bf16[256,256]{1,0:T(8,128)(2,1)S(1)} %copy-done.5, bf16[384,256]{1,0:T(8,128)(2,1)S(1)} %collective-permute-done.10.halves, ...), custom_call_target="tpu_custom_call" | custom-call | tf_op jit(solution)/shard_map/sampler/pallas_call | solution.py:23
  30.6 1.1 %collective-permute-start.14 = (bf16[384,128]{1,0:T(8,128)(2,1)S(1)}, bf16[384,128]{1,0:T(8,128)(2,1)S(1)}, u32[]{:S(2)}, u32[]{:S(2)}) collective-permute-start(bf16[384,128]{1,0:T(8,128)(2,1)S(1)} %get-tuple-element.57.own), channel_id=1, source_target_pairs={{0,1},{1,0},{2,3},{3,2},{4,5},{5,4},{6,7},{7,6},{8,9},{9,8},{10,11... | collective-permute-start | bytes 294920 | tf_op jit(solution)/shard_map/ppermute | solution.py:406
  31.7 2.0 %collective-permute-start.13 = (bf16[384,128]{1,0:T(8,128)(2,1)S(1)}, bf16[384,128]{1,0:T(8,128)(2,1)S(1)}, u32[]{:S(2)}, u32[]{:S(2)}) collective-permute-start(bf16[384,128]{1,0:T(8,128)(2,1)S(1)} %get-tuple-element.57.own), channel_id=1, source_target_pairs={{0,2},{1,3},{2,0},{3,1},{4,6},{5,7},{6,4},{7,5},{8,10},{9,11},{10,... | collective-permute-start | bytes 294920 | tf_op jit(solution)/shard_map/ppermute | solution.py:406
  33.7 1.3 %collective-permute-start.12 = (bf16[384,128]{1,0:T(8,128)(2,1)S(1)}, bf16[384,128]{1,0:T(8,128)(2,1)S(1)}, u32[]{:S(2)}, u32[]{:S(2)}) collective-permute-start(bf16[384,128]{1,0:T(8,128)(2,1)S(1)} %get-tuple-element.57.own), channel_id=1, source_target_pairs={{0,3},{1,2},{2,1},{3,0},{4,7},{5,6},{6,5},{7,4},{8,11},{9,10},{10,... | collective-permute-start | bytes 294920 | tf_op jit(solution)/shard_map/ppermute | solution.py:406
  35.1 1.3 %collective-permute-start.11 = (bf16[256,128]{1,0:T(8,128)(2,1)S(1)}, bf16[256,128]{1,0:T(8,128)(2,1)S(1)}, u32[]{:S(2)}, u32[]{:S(2)}) collective-permute-start(bf16[256,128]{1,0:T(8,128)(2,1)S(1)} %get-tuple-element.58), channel_id=1, source_target_pairs={{0,4},{4,8},{8,12},{12,16},{16,20},{20,24},{24,28},{1,5},{5,9},{9,... | collective-permute-start | bytes 196616 | tf_op jit(solution)/shard_map/ppermute | solution.py:520
  36.4 0.9 %collective-permute-done.11.rim = bf16[256,128]{1,0:T(8,128)(2,1)S(1)} collective-permute-done((bf16[256,128]{1,0:T(8,128)(2,1)S(1)}, bf16[256,128]{1,0:T(8,128)(2,1)S(1)}, u32[]{:S(2)}, u32[]{:S(2)}) %collective-permute-start.11) | collective-permute-done | bytes 65568 | tf_op jit(solution)/shard_map/ppermute | solution.py:520
  37.2 4.9 %collective-permute-done.13.refs_1_ = bf16[384,128]{1,0:T(8,128)(2,1)S(1)} collective-permute-done((bf16[384,128]{1,0:T(8,128)(2,1)S(1)}, bf16[384,128]{1,0:T(8,128)(2,1)S(1)}, u32[]{:S(2)}, u32[]{:S(2)}) %collective-permute-start.13) | collective-permute-done | bytes 98336 | tf_op jit(solution)/shard_map/ppermute | solution.py:406
  42.2 5.8 %rebuild.1 = (bf16[4096,768]{1,0:T(8,128)(2,1)S(1)}, bf16[768,256]{1,0:T(8,128)(2,1)S(1)}, f32[8,768]{1,0:T(8,128)S(1)}, f32[8,256]{1,0:T(8,128)S(1)}, f32[520,2...) custom-call(s32[1,2]{1,0:T(1,128)S(1)} %add_bitcast_fusion.place, ...), custom_call_target="tpu_custom_call" | custom-call | tf_op jit(solution)/shard_map/rebuild/pallas_call | solution.py:23
  48.6 1.5 %kept.1 = (f32[512,256]{1,0:T(8,128)S(1)}, f32[512,256]{1,0:T(8,128)S(1)}, f32[512,256]{1,0:T(8,128)S(1)}, f32[512,256]{1,0:T(8,128)S(1)}) custom-call(s32[1,2]{1,0:T(1,128)S(1)} %add_bitcast_fusion.place, bf16[4096,768]{1,0:T(8,128)(2,1)S(1)} %get-tuple-element.62.stacked, bf16[768,256]{1,0:T(8,128)(2,1)S(1)} %get-tuple-element.63.ratio), custom_call_target="tpu_custom_call" | custom-call | tf_op jit(solution)/shard_map/kept/pallas_call | solution.py:23
  50.3 1.6 %collective-permute-start.16 = (f16[528,256]{1,0:T(8,128)(2,1)S(1)}, f16[528,256]{1,0:T(8,128)(2,1)S(1)}, u32[]{:S(2)}, u32[]{:S(2)}) collective-permute-start(f16[528,256]{1,0:T(8,128)(2,1)S(1)} %convert_element_type.24), channel_id=1, source_target_pairs={{0,8},{4,20},{8,0},{12,28},{16,24},{20,4},{24,16},{28,12},{1,9},{5... | collective-permute-start | bytes 811016 | tf_op jit(solution)/shard_map/ppermute | solution.py:566
  52.2 1.6 %collective-permute-start.21 = (f16[528,256]{1,0:T(8,128)(2,1)S(1)}, f16[528,256]{1,0:T(8,128)(2,1)S(1)}, u32[]{:S(2)}, u32[]{:S(2)}) collective-permute-start(f16[528,256]{1,0:T(8,128)(2,1)S(1)} %convert_element_type.26), channel_id=1, source_target_pairs={{0,8},{4,20},{8,0},{12,28},{16,24},{20,4},{24,16},{28,12},{1,9},{5... | collective-permute-start | bytes 811016 | tf_op jit(solution)/shard_map/ppermute | solution.py:566
  53.7 1.9 %collective-permute-start.18 = (f32[1,768]{1,0:T(1,128)S(1)}, f32[1,768]{1,0:T(1,128)S(1)}, u32[]{:S(2)}, u32[]{:S(2)}) collective-permute-start(f32[1,768]{1,0:T(1,128)S(1)} %slice.10), channel_id=1, source_target_pairs={{0,1},{1,0},{2,3},{3,2},{4,5},{5,4},{6,7},{7,6},{8,9},{9,8},{10,11... | collective-permute-start | bytes 9224 | tf_op jit(solution)/shard_map/ppermute | solution.py:406
  55.6 1.7 %collective-permute-done.18 = f32[1,768]{1,0:T(1,128)S(1)} collective-permute-done((f32[1,768]{1,0:T(1,128)S(1)}, f32[1,768]{1,0:T(1,128)S(1)}, u32[]{:S(2)}, u32[]{:S(2)}) %collective-permute-start.18) | collective-permute-done | bytes 3104 | tf_op jit(solution)/shard_map/ppermute | solution.py:406
  57.5 1.1 %collective-permute-start.23 = (f16[528,256]{1,0:T(8,128)(2,1)S(1)}, f16[528,256]{1,0:T(8,128)(2,1)S(1)}, u32[]{:S(2)}, u32[]{:S(2)}) collective-permute-start(f16[528,256]{1,0:T(8,128)(2,1)S(1)} %convert_element_type.28), channel_id=1, source_target_pairs={{0,16},{4,12},{8,24},{12,4},{16,0},{20,28},{24,8},{28,20},{1,17},{... | collective-permute-start | bytes 811016 | tf_op jit(solution)/shard_map/ppermute | solution.py:566
  58.6 2.3 %collective-permute-start.19 = (f32[1,768]{1,0:T(1,128)S(1)}, f32[1,768]{1,0:T(1,128)S(1)}, u32[]{:S(2)}, u32[]{:S(2)}) collective-permute-start(f32[1,768]{1,0:T(1,128)S(1)} %add.14), channel_id=1, source_target_pairs={{0,2},{1,3},{2,0},{3,1},{4,6},{5,7},{6,4},{7,5},{8,10},{9,11},{10,... | collective-permute-start | bytes 9224 | tf_op jit(solution)/shard_map/ppermute | solution.py:406
  60.9 2.2 %collective-permute-done.19 = f32[1,768]{1,0:T(1,128)S(1)} collective-permute-done((f32[1,768]{1,0:T(1,128)S(1)}, f32[1,768]{1,0:T(1,128)S(1)}, u32[]{:S(2)}, u32[]{:S(2)}) %collective-permute-start.19) | collective-permute-done | bytes 3104 | tf_op jit(solution)/shard_map/ppermute | solution.py:406
  64.1 0.9 %total.1 = f32[512,256]{1,0:T(8,128)} custom-call(f32[512,256]{1,0:T(8,128)S(1)} %get-tuple-element.70.kept, f32[520,256]{1,0:T(8,128)S(1)} %collective-permute-done.20.crossed, f32[528,256]{1,0:T(8,128)S(1)} %convert_element_type.27.refs_0_, f32[528,256]{1,0:T(8,128)S(1)} %convert_element_type.29.refs_1_), custom_call_target="tpu_custom_call" | custom-call | tf_op jit(solution)/shard_map/total/pallas_call | solution.py:23
  (60 shorter events, 5.4 us)
Async XLA Ops:
  0.6 18.3 %copy-start.6 = (f32[256]{0:T(256)S(1)}, f32[256]{0:T(256)}, u32[]{:S(2)}) copy-start(f32[256]{0:T(256)} %param.10) | copy-start | bytes 3076
  0.6 18.2 %copy-start.7 = (f32[256]{0:T(256)S(1)}, f32[256]{0:T(256)}, u32[]{:S(2)}) copy-start(f32[256]{0:T(256)} %param.11) | copy-start | bytes 3076
  0.7 23.5 %copy-start.8 = (s32[256]{0:T(256)S(1)}, s32[256]{0:T(256)}, u32[]{:S(2)}) copy-start(s32[256]{0:T(256)} %param.16) | copy-start | bytes 3076
  0.7 23.5 %copy-start.2 = (f32[2,256,768]{2,1,0:T(8,128)S(1)}, f32[2,256,768]{2,1,0:T(8,128)}, u32[]{:S(2)}) copy-start(f32[2,256,768]{2,1,0:T(8,128)} %uniform.1) | copy-start | bytes 4718596
  3.9 5.2 %collective-permute-start.1 = (f32[4,256]{1,0:T(4,128)S(1)}, f32[4,256]{1,0:T(4,128)S(1)}, u32[]{:S(2)}, u32[]{:S(2)}) collective-permute-start(f32[4,256]{1,0:T(4,128)S(1)} %get-tuple-element.43), channel_id=1, source_target_pairs={{0,4},{4,0},{8,12},{12,8},{16,20},{20,16},{24,28},{28,24},{1,5},{5... | collective-permute-start | bytes 12296 | tf_op jit(solution)/shard_map/ppermute | solution.py:406
  4.4 14.5 %collective-permute-start = (bf16[336,256]{1,0:T(8,128)(2,1)S(1)}, bf16[336,256]{1,0:T(8,128)(2,1)S(1)}, u32[]{:S(2)}, u32[]{:S(2)}) collective-permute-start(bf16[336,256]{1,0:T(8,128)(2,1)S(1)} %get-tuple-element.42), channel_id=1, source_target_pairs={{0,3},{1,2},{2,1},{3,0},{4,7},{5,6},{6,5},{7,4},{8,11},{9,10},{10,... | collective-permute-start | bytes 516104 | tf_op jit(solution)/shard_map/ppermute | solution.py:406
  9.1 4.6 %collective-permute-start.4 = (f32[8,256]{1,0:T(8,128)S(1)}, f32[8,256]{1,0:T(8,128)S(1)}, u32[]{:S(2)}, u32[]{:S(2)}) collective-permute-start(f32[8,256]{1,0:T(8,128)S(1)} %pad_maximum_fusion.1.refs_1_), channel_id=1, source_target_pairs={{0,24},{4,28},{8,16},{12,20},{16,8},{20,12},{24,0},{28,4},{1,25},{... | collective-permute-start | bytes 24584 | tf_op jit(solution)/shard_map/ppermute | solution.py:406
  11.6 13.5 %collective-permute-start.5 = (bf16[336,256]{1,0:T(8,128)(2,1)S(1)}, bf16[336,256]{1,0:T(8,128)(2,1)S(1)}, u32[]{:S(2)}, u32[]{:S(2)}) collective-permute-start(bf16[336,256]{1,0:T(8,128)(2,1)S(1)} %get-tuple-element.48), channel_id=1, source_target_pairs={{0,2},{1,3},{2,0},{3,1},{4,6},{5,7},{6,4},{7,5},{8,10},{9,11},{10,... | collective-permute-start | bytes 516104 | tf_op jit(solution)/shard_map/ppermute | solution.py:406
  13.7 11.4 %collective-permute-start.6 = (bf16[336,256]{1,0:T(8,128)(2,1)S(1)}, bf16[336,256]{1,0:T(8,128)(2,1)S(1)}, u32[]{:S(2)}, u32[]{:S(2)}) collective-permute-start(bf16[336,256]{1,0:T(8,128)(2,1)S(1)} %get-tuple-element.49), channel_id=1, source_target_pairs={{0,1},{1,0},{2,3},{3,2},{4,5},{5,4},{6,7},{7,6},{8,9},{9,8},{10,11... | collective-permute-start | bytes 516104 | tf_op jit(solution)/shard_map/ppermute | solution.py:406
  13.7 4.9 %collective-permute-start.3 = (f32[8,256]{1,0:T(8,128)S(1)}, f32[8,256]{1,0:T(8,128)S(1)}, u32[]{:S(2)}, u32[]{:S(2)}) collective-permute-start(f32[8,256]{1,0:T(8,128)S(1)} %pad_maximum_fusion.1.refs_1_), channel_id=1, source_target_pairs={{0,16},{4,20},{8,24},{12,28},{16,0},{20,4},{24,8},{28,12},{1,17},{... | collective-permute-start | bytes 24584 | tf_op jit(solution)/shard_map/ppermute | solution.py:406
  15.2 3.7 %collective-permute-start.2 = (f32[8,256]{1,0:T(8,128)S(1)}, f32[8,256]{1,0:T(8,128)S(1)}, u32[]{:S(2)}, u32[]{:S(2)}) collective-permute-start(f32[8,256]{1,0:T(8,128)S(1)} %pad_maximum_fusion.1.refs_1_), channel_id=1, source_target_pairs={{0,8},{4,12},{8,0},{12,4},{16,24},{20,28},{24,16},{28,20},{1,9},{5... | collective-permute-start | bytes 24584 | tf_op jit(solution)/shard_map/ppermute | solution.py:406
  18.3 5.9 %copy-start.4 = (f32[256,768]{1,0:T(8,128)S(1)}, f32[256,768]{1,0:T(8,128)}, u32[]{:S(2)}) copy-start(f32[256,768]{1,0:T(8,128)} %gauss.1) | copy-start | bytes 2359300
  19.7 5.7 %collective-permute-start.7 = (f32[22,256]{1,0:T(8,128)S(1)}, f32[22,256]{1,0:T(8,128)S(1)}, u32[]{:S(2)}, u32[]{:S(2)}) collective-permute-start(f32[22,256]{1,0:T(8,128)S(1)} %get-tuple-element.50), channel_id=1, source_target_pairs={{0,3},{1,2},{2,1},{3,0},{4,7},{5,6},{6,5},{7,4},{8,11},{9,10},{10,... | collective-permute-start | bytes 67592 | tf_op jit(solution)/shard_map/ppermute | solution.py:406
  21.3 4.8 %collective-permute-start.8 = (f32[22,256]{1,0:T(8,128)S(1)}, f32[22,256]{1,0:T(8,128)S(1)}, u32[]{:S(2)}, u32[]{:S(2)}) collective-permute-start(f32[22,256]{1,0:T(8,128)S(1)} %get-tuple-element.51), channel_id=1, source_target_pairs={{0,2},{1,3},{2,0},{3,1},{4,6},{5,7},{6,4},{7,5},{8,10},{9,11},{10,... | collective-permute-start | bytes 67592 | tf_op jit(solution)/shard_map/ppermute | solution.py:406
  24.0 3.8 %collective-permute-start.9 = (f32[22,256]{1,0:T(8,128)S(1)}, f32[22,256]{1,0:T(8,128)S(1)}, u32[]{:S(2)}, u32[]{:S(2)}) collective-permute-start(f32[22,256]{1,0:T(8,128)S(1)} %get-tuple-element.52), channel_id=1, source_target_pairs={{0,1},{1,0},{2,3},{3,2},{4,5},{5,4},{6,7},{7,6},{8,9},{9,8},{10,11... | collective-permute-start | bytes 67592 | tf_op jit(solution)/shard_map/ppermute | solution.py:406
  24.2 5.2 %copy-start.5 = (bf16[256,256]{1,0:T(8,128)(2,1)S(1)}, bf16[256,256]{1,0:T(8,128)(2,1)}, u32[]{:S(2)}) copy-start(bf16[256,256]{1,0:T(8,128)(2,1)} %encoder.1) | copy-start | bytes 393220
  27.8 14.3 %copy-start.1 = (bf16[256,4096]{1,0:T(8,128)(2,1)S(1)}, bf16[256,4096]{1,0:T(8,128)(2,1)}, u32[]{:S(2)}) copy-start(bf16[256,4096]{1,0:T(8,128)(2,1)} %templates.3) | copy-start | bytes 6291460
  27.8 14.3 %copy-start.3 = (bf16[256,768]{1,0:T(8,128)(2,1)S(1)}, bf16[256,768]{1,0:T(8,128)(2,1)}, u32[]{:S(2)}) copy-start(bf16[256,768]{1,0:T(8,128)(2,1)} %spectrum.1) | copy-start | bytes 1179652
  27.8 1.5 %collective-permute-start.10 = (bf16[384,256]{1,0:T(8,128)(2,1)S(1)}, bf16[384,256]{1,0:T(8,128)(2,1)S(1)}, u32[]{:S(2)}, u32[]{:S(2)}) collective-permute-start(bf16[384,256]{1,0:T(8,128)(2,1)S(1)} %halves.1), channel_id=1, source_target_pairs={{0,4},{4,0},{8,12},{12,8},{16,20},{20,16},{24,28},{28,24},{1,5},{5... | collective-permute-start | bytes 589832 | tf_op jit(solution)/shard_map/ppermute | solution.py:406
  30.6 6.6 %collective-permute-start.14 = (bf16[384,128]{1,0:T(8,128)(2,1)S(1)}, bf16[384,128]{1,0:T(8,128)(2,1)S(1)}, u32[]{:S(2)}, u32[]{:S(2)}) collective-permute-start(bf16[384,128]{1,0:T(8,128)(2,1)S(1)} %get-tuple-element.57.own), channel_id=1, source_target_pairs={{0,1},{1,0},{2,3},{3,2},{4,5},{5,4},{6,7},{7,6},{8,9},{9,8},{10,11... | collective-permute-start | bytes 294920 | tf_op jit(solution)/shard_map/ppermute | solution.py:406
  31.7 10.5 %collective-permute-start.13 = (bf16[384,128]{1,0:T(8,128)(2,1)S(1)}, bf16[384,128]{1,0:T(8,128)(2,1)S(1)}, u32[]{:S(2)}, u32[]{:S(2)}) collective-permute-start(bf16[384,128]{1,0:T(8,128)(2,1)S(1)} %get-tuple-element.57.own), channel_id=1, source_target_pairs={{0,2},{1,3},{2,0},{3,1},{4,6},{5,7},{6,4},{7,5},{8,10},{9,11},{10,... | collective-permute-start | bytes 294920 | tf_op jit(solution)/shard_map/ppermute | solution.py:406
  33.7 8.4 %collective-permute-start.12 = (bf16[384,128]{1,0:T(8,128)(2,1)S(1)}, bf16[384,128]{1,0:T(8,128)(2,1)S(1)}, u32[]{:S(2)}, u32[]{:S(2)}) collective-permute-start(bf16[384,128]{1,0:T(8,128)(2,1)S(1)} %get-tuple-element.57.own), channel_id=1, source_target_pairs={{0,3},{1,2},{2,1},{3,0},{4,7},{5,6},{6,5},{7,4},{8,11},{9,10},{10,... | collective-permute-start | bytes 294920 | tf_op jit(solution)/shard_map/ppermute | solution.py:406
  35.1 2.2 %collective-permute-start.11 = (bf16[256,128]{1,0:T(8,128)(2,1)S(1)}, bf16[256,128]{1,0:T(8,128)(2,1)S(1)}, u32[]{:S(2)}, u32[]{:S(2)}) collective-permute-start(bf16[256,128]{1,0:T(8,128)(2,1)S(1)} %get-tuple-element.58), channel_id=1, source_target_pairs={{0,4},{4,8},{8,12},{12,16},{16,20},{20,24},{24,28},{1,5},{5,9},{9,... | collective-permute-start | bytes 196616 | tf_op jit(solution)/shard_map/ppermute | solution.py:520
  48.0 2.2 %collective-permute-start.15 = (f32[520,256]{1,0:T(8,128)S(1)}, f32[520,256]{1,0:T(8,128)S(1)}, u32[]{:S(2)}, u32[]{:S(2)}) collective-permute-start(f32[520,256]{1,0:T(8,128)S(1)} %get-tuple-element.65), channel_id=1, source_target_pairs={{0,4},{4,0},{8,12},{12,8},{16,20},{20,16},{24,28},{28,24},{1,5},{5... | collective-permute-start | bytes 1597448 | tf_op jit(solution)/shard_map/ppermute | solution.py:406
  48.1 4.0 %collective-permute-start.17 = (f32[520,256]{1,0:T(8,128)S(1)}, f32[520,256]{1,0:T(8,128)S(1)}, u32[]{:S(2)}, u32[]{:S(2)}) collective-permute-start(f32[520,256]{1,0:T(8,128)S(1)} %get-tuple-element.67), channel_id=1, source_target_pairs={{0,4},{4,0},{8,12},{12,8},{16,20},{20,16},{24,28},{28,24},{1,5},{5... | collective-permute-start | bytes 1597448 | tf_op jit(solution)/shard_map/ppermute | solution.py:406
  48.6 8.8 %collective-permute-start.22 = (f32[520,256]{1,0:T(8,128)S(1)}, f32[520,256]{1,0:T(8,128)S(1)}, u32[]{:S(2)}, u32[]{:S(2)}) collective-permute-start(f32[520,256]{1,0:T(8,128)S(1)} %get-tuple-element.74), channel_id=1, source_target_pairs={{0,4},{4,0},{8,12},{12,8},{16,20},{20,16},{24,28},{28,24},{1,5},{5... | collective-permute-start | bytes 1597448 | tf_op jit(solution)/shard_map/ppermute | solution.py:406
  50.3 7.0 %collective-permute-start.16 = (f16[528,256]{1,0:T(8,128)(2,1)S(1)}, f16[528,256]{1,0:T(8,128)(2,1)S(1)}, u32[]{:S(2)}, u32[]{:S(2)}) collective-permute-start(f16[528,256]{1,0:T(8,128)(2,1)S(1)} %convert_element_type.24), channel_id=1, source_target_pairs={{0,8},{4,20},{8,0},{12,28},{16,24},{20,4},{24,16},{28,12},{1,9},{5... | collective-permute-start | bytes 811016 | tf_op jit(solution)/shard_map/ppermute | solution.py:566
  51.9 12.3 %collective-permute-start.20 = (f32[520,256]{1,0:T(8,128)S(1)}, f32[520,256]{1,0:T(8,128)S(1)}, u32[]{:S(2)}, u32[]{:S(2)}) collective-permute-start(f32[520,256]{1,0:T(8,128)S(1)} %get-tuple-element.71), channel_id=1, source_target_pairs={{0,4},{4,0},{8,12},{12,8},{16,20},{20,16},{24,28},{28,24},{1,5},{5... | collective-permute-start | bytes 1597448 | tf_op jit(solution)/shard_map/ppermute | solution.py:406
  52.2 8.7 %collective-permute-start.21 = (f16[528,256]{1,0:T(8,128)(2,1)S(1)}, f16[528,256]{1,0:T(8,128)(2,1)S(1)}, u32[]{:S(2)}, u32[]{:S(2)}) collective-permute-start(f16[528,256]{1,0:T(8,128)(2,1)S(1)} %convert_element_type.26), channel_id=1, source_target_pairs={{0,8},{4,20},{8,0},{12,28},{16,24},{20,4},{24,16},{28,12},{1,9},{5... | collective-permute-start | bytes 811016 | tf_op jit(solution)/shard_map/ppermute | solution.py:566
  53.7 3.6 %collective-permute-start.18 = (f32[1,768]{1,0:T(1,128)S(1)}, f32[1,768]{1,0:T(1,128)S(1)}, u32[]{:S(2)}, u32[]{:S(2)}) collective-permute-start(f32[1,768]{1,0:T(1,128)S(1)} %slice.10), channel_id=1, source_target_pairs={{0,1},{1,0},{2,3},{3,2},{4,5},{5,4},{6,7},{7,6},{8,9},{9,8},{10,11... | collective-permute-start | bytes 9224 | tf_op jit(solution)/shard_map/ppermute | solution.py:406
  57.5 6.5 %collective-permute-start.23 = (f16[528,256]{1,0:T(8,128)(2,1)S(1)}, f16[528,256]{1,0:T(8,128)(2,1)S(1)}, u32[]{:S(2)}, u32[]{:S(2)}) collective-permute-start(f16[528,256]{1,0:T(8,128)(2,1)S(1)} %convert_element_type.28), channel_id=1, source_target_pairs={{0,16},{4,12},{8,24},{12,4},{16,0},{20,28},{24,8},{28,20},{1,17},{... | collective-permute-start | bytes 811016 | tf_op jit(solution)/shard_map/ppermute | solution.py:566
  58.6 4.5 %collective-permute-start.19 = (f32[1,768]{1,0:T(1,128)S(1)}, f32[1,768]{1,0:T(1,128)S(1)}, u32[]{:S(2)}, u32[]{:S(2)}) collective-permute-start(f32[1,768]{1,0:T(1,128)S(1)} %add.14), channel_id=1, source_target_pairs={{0,2},{1,3},{2,0},{3,1},{4,6},{5,7},{6,4},{7,5},{8,10},{9,11},{10,... | collective-permute-start | bytes 9224 | tf_op jit(solution)/shard_map/ppermute | solution.py:406
  (1 other events, 1.6 us)

commit v8 on v7

--- a/solution.py
+++ b/solution.py
@@ -449,7 +449,7 @@
     ]
     pair = jnp.concatenate([tm_message, exchanged(tm_message, "tm", 1)], axis=0)
     pairs = [pair] + [exchanged(pair, "tm", step) for step in range(2, nt, 2)]
-    nearest, pairs[-1] = lax.optimization_barrier((nearest, pairs[-1]))
+    nearest, *pairs[1:] = lax.optimization_barrier((nearest, *pairs[1:]))
     messages.append(exchanged(nearest, "freq", 1))
     stat_rows = columns // bins + frames // bins
     (stats,) = call(

time: 65.2 us -> 65.3 us (level)
  waiting for transfers between devices: 15.8 us -> 16.8 us
  starting transfers between devices: 30.1 us -> 29.2 us
    ppermute x20, starting transfers between devices: 24.7 us -> 23.7 us  [exchanged(): lax.ppermute(value, axis, [(index, index ^ step) for index in range(size)])]
    ppermute x20, waiting for transfers between devices: 14.6 us -> 15.6 us  [exchanged(): lax.ppermute(value, axis, [(index, index ^ step) for index in range(size)])]
  transfers between devices with their start and end apart: 24 -> 24, of which waited for: 11 -> 12; matrix products, arithmetic and copies ran while one was open for 1% -> 1% of each run, Pallas kernels for 7% -> 7%
where the time goes in v8:
time: 65.3 us; the launch traced here: 65.1 us
  starting transfers between devices  29.2 us (45%)
  waiting for transfers between devices  16.8 us (26%)
  Pallas kernels  13.7 us (21%)
  other arithmetic  2.88 us (4%)
  local copies, waits for them, and re-layouts  1.64 us (3%)
  between operations  0.9 us (1%)
    ppermute x20, starting transfers between devices, exchanged(): lax.ppermute(value, axis, [(index, index ^ step) for index in range(size)])  23.7 us
    ppermute x20, waiting for transfers between devices, exchanged(): lax.ppermute(value, axis, [(index, index ^ step) for index in range(size)])  15.6 us
    pallas_call x13, Pallas kernels, call(): pl.pallas_call(kernel, name=name, out_shape=[jax.ShapeDtypeStruct(shape,...  13.7 us
    ppermute x3, starting transfers between devices, sent(): return lax.ppermute(message, 'tm', pairs).astype(f32)  4.25 us
    unnamed x18, local copies, waits for them, and re-layouts  1.63 us
  transfers between devices with their start and end apart: 24, of which 12 were waited for; matrix products, arithmetic and copies ran while one was open for 1% of the time, Pallas kernels for 7%

profile of v8, /device:TPU:0, one launch (start us, length us, event | category | flops | bytes accessed | tf_op | source)
XLA Modules:
  0.0 65.1 jit_solution(830120224875468162)
XLA Ops:
  0.8 0.8 %convert_add_fusion = f32[1024]{0:T(1024)S(1)} fusion(s32[768]{0:T(1024)} %param.12, f32[256]{0:T(256)} %param.10), kind=kLoop, calls=%fused_computation.2 | loop fusion | flops 2048 | bytes 8192 | tf_op jit(solution)/shard_map/add | solution.py:433
  1.6 1.1 %pad_maximum_fusion.both = bf16[256,1024]{1,0:T(8,128)(2,1)S(1)} fusion(bf16[256,256]{1,0:T(8,128)(2,1)} %encoder.1, bf16[256,768]{1,0:T(8,128)(2,1)} %spectrum.1), kind=kLoop, calls=%fused_computation | loop fusion | flops 1048576 | bytes 1048576 | tf_op jit(solution)/shard_map/concatenate | solution.py:442
  2.7 1.2 %pieces.1 = (bf16[336,256]{1,0:T(8,128)(2,1)S(1)}, bf16[336,256]{1,0:T(8,128)(2,1)S(1)}, bf16[336,256]{1,0:T(8,128)(2,1)S(1)}, bf16[208,256]{1,0:T(8,128)(2,1)S(...) custom-call(s32[1,2]{1,0:T(1,128)S(1)} %add_bitcast_fusion.place, ...), custom_call_target="tpu_custom_call" | custom-call | tf_op jit(solution)/shard_map/pieces/pallas_call | solution.py:23
  4.4 4.7 %collective-permute-start = (bf16[336,256]{1,0:T(8,128)(2,1)S(1)}, bf16[336,256]{1,0:T(8,128)(2,1)S(1)}, u32[]{:S(2)}, u32[]{:S(2)}) collective-permute-start(bf16[336,256]{1,0:T(8,128)(2,1)S(1)} %get-tuple-element.44), channel_id=1, source_target_pairs={{0,3},{1,2},{2,1},{3,0},{4,7},{5,6},{6,5},{7,4},{8,11},{9,10},{10,... | collective-permute-start | bytes 516104 | tf_op jit(solution)/shard_map/ppermute | solution.py:406
  9.1 2.5 %collective-permute-start.4 = (f32[8,256]{1,0:T(8,128)S(1)}, f32[8,256]{1,0:T(8,128)S(1)}, u32[]{:S(2)}, u32[]{:S(2)}) collective-permute-start(f32[8,256]{1,0:T(8,128)S(1)} %pad_maximum_fusion.1.refs_1_), channel_id=1, source_target_pairs={{0,24},{4,28},{8,16},{12,20},{16,8},{20,12},{24,0},{28,4},{1,25},{... | collective-permute-start | bytes 24584 | tf_op jit(solution)/shard_map/ppermute | solution.py:406
  12.6 1.1 %collective-permute-done.4.refs_4_ = f32[8,256]{1,0:T(8,128)S(1)} collective-permute-done((f32[8,256]{1,0:T(8,128)S(1)}, f32[8,256]{1,0:T(8,128)S(1)}, u32[]{:S(2)}, u32[]{:S(2)}) %collective-permute-start.4) | collective-permute-done | bytes 8224 | tf_op jit(solution)/shard_map/ppermute | solution.py:406
  13.7 1.5 %collective-permute-done.3.refs_3_ = f32[8,256]{1,0:T(8,128)S(1)} collective-permute-done((f32[8,256]{1,0:T(8,128)S(1)}, f32[8,256]{1,0:T(8,128)S(1)}, u32[]{:S(2)}, u32[]{:S(2)}) %collective-permute-start.3) | collective-permute-done | bytes 8224 | tf_op jit(solution)/shard_map/ppermute | solution.py:406
  15.8 1.6 %copy-done = bf16[256,4096]{1,0:T(8,128)(2,1)S(1)} copy-done((bf16[256,4096]{1,0:T(8,128)(2,1)S(1)}, bf16[256,4096]{1,0:T(8,128)(2,1)}, u32[]{:S(2)}) %copy-start) | copy-done | bytes 2097176
  17.7 0.8 %entry.1 = (f32[22,256]{1,0:T(8,128)S(1)}, f32[22,256]{1,0:T(8,128)S(1)}, f32[22,256]{1,0:T(8,128)S(1)}, f32[3,256]{1,0:T(4,128)S(1)}, f32[1,896]{1,0:T(1,128)S(1)}) custom-call(s32[1,2]{1,0:T(1,128)S(1)} %add_bitcast_fusion.place, f32[1,256]{1,0:T(1,128)S(1)} %bitcast.9, f32[1,256]{1,0:T(1,128)S(1)} %bitcast.10, f32[8,256]{1,0:T(8,128)S(1)} %get-tuple-element.42.states, ...), custom_call_target="tpu_custom_call" | custom-call | tf_op jit(solution)/shard_map/entry/pallas_call | solution.py:23
  18.5 1.5 %collective-permute-start.7 = (f32[22,256]{1,0:T(8,128)S(1)}, f32[22,256]{1,0:T(8,128)S(1)}, u32[]{:S(2)}, u32[]{:S(2)}) collective-permute-start(f32[22,256]{1,0:T(8,128)S(1)} %get-tuple-element.54), channel_id=1, source_target_pairs={{0,3},{1,2},{2,1},{3,0},{4,7},{5,6},{6,5},{7,4},{8,11},{9,10},{10,... | collective-permute-start | bytes 67592 | tf_op jit(solution)/shard_map/ppermute | solution.py:406
  20.1 3.9 %collective-permute-start.8 = (f32[22,256]{1,0:T(8,128)S(1)}, f32[22,256]{1,0:T(8,128)S(1)}, u32[]{:S(2)}, u32[]{:S(2)}) collective-permute-start(f32[22,256]{1,0:T(8,128)S(1)} %get-tuple-element.55), channel_id=1, source_target_pairs={{0,2},{1,3},{2,0},{3,1},{4,6},{5,7},{6,4},{7,5},{8,10},{9,11},{10,... | collective-permute-start | bytes 67592 | tf_op jit(solution)/shard_map/ppermute | solution.py:406
  24.1 0.9 %noise.1 = (f32[256,256]{1,0:T(8,128)S(1)}, f32[256,256]{1,0:T(8,128)S(1)}, f32[256,256]{1,0:T(8,128)S(1)}, f32[256,256]{1,0:T(8,128)S(1)}) custom-call(s32[1,2]{1,0:T(1,128)S(1)} %add_bitcast_fusion.place, f32[256,768]{1,0:T(8,128)S(1)} %copy-done.4, f32[2,256,768]{2,1,0:T(8,128)S(1)} %copy-done.2, s32[1,256]{1,0:T(1,128)S(1)} %bitcast.11), custom_call_target="tpu_custom_call" | custom-call | tf_op jit(solution)/shard_map/noise/pallas_call | solution.py:23
  25.3 0.7 %collective-permute-done.6.refs_2_.refs_5_ = bf16[336,256]{1,0:T(8,128)(2,1)S(1)} collective-permute-done((bf16[336,256]{1,0:T(8,128)(2,1)S(1)}, bf16[336,256]{1,0:T(8,128)(2,1)S(1)}, u32[]{:S(2)}, u32[]{:S(2)}) %collective-permute-start.6) | collective-permute-done | bytes 172064 | tf_op jit(solution)/shard_map/ppermute | solution.py:406
  26.1 1.7 %collective-permute-done.9.refs_5_.refs_2_ = f32[22,256]{1,0:T(8,128)S(1)} collective-permute-done((f32[22,256]{1,0:T(8,128)S(1)}, f32[22,256]{1,0:T(8,128)S(1)}, u32[]{:S(2)}, u32[]{:S(2)}) %collective-permute-start.9) | collective-permute-done | bytes 22560 | tf_op jit(solution)/shard_map/ppermute | solution.py:406
  28.6 0.7 %collective-permute-done.10.halves = bf16[384,256]{1,0:T(8,128)(2,1)S(1)} collective-permute-done((bf16[384,256]{1,0:T(8,128)(2,1)S(1)}, bf16[384,256]{1,0:T(8,128)(2,1)S(1)}, u32[]{:S(2)}, u32[]{:S(2)}) %collective-permute-start.10) | collective-permute-done | bytes 196640 | tf_op jit(solution)/shard_map/ppermute | solution.py:406
  29.4 1.3 %sampler.1 = (bf16[384,128]{1,0:T(8,128)(2,1)S(1)}, bf16[256,128]{1,0:T(8,128)(2,1)S(1)}) custom-call(s32[1,2]{1,0:T(1,128)S(1)} %add_bitcast_fusion.place, bf16[4,256,256]{2,1,0:T(8,128)(2,1)S(1)} %normed.1, bf16[256,256]{1,0:T(8,128)(2,1)S(1)} %copy-done.5, bf16[384,256]{1,0:T(8,128)(2,1)S(1)} %collective-permute-done.10.halves, ...), custom_call_target="tpu_custom_call" | custom-call | tf_op jit(solution)/shard_map/sampler/pallas_call | solution.py:23
  30.6 1.1 %collective-permute-start.14 = (bf16[384,128]{1,0:T(8,128)(2,1)S(1)}, bf16[384,128]{1,0:T(8,128)(2,1)S(1)}, u32[]{:S(2)}, u32[]{:S(2)}) collective-permute-start(bf16[384,128]{1,0:T(8,128)(2,1)S(1)} %get-tuple-element.61.own), channel_id=1, source_target_pairs={{0,1},{1,0},{2,3},{3,2},{4,5},{5,4},{6,7},{7,6},{8,9},{9,8},{10,11... | collective-permute-start | bytes 294920 | tf_op jit(solution)/shard_map/ppermute | solution.py:406
  31.7 2.0 %collective-permute-start.13 = (bf16[384,128]{1,0:T(8,128)(2,1)S(1)}, bf16[384,128]{1,0:T(8,128)(2,1)S(1)}, u32[]{:S(2)}, u32[]{:S(2)}) collective-permute-start(bf16[384,128]{1,0:T(8,128)(2,1)S(1)} %get-tuple-element.61.own), channel_id=1, source_target_pairs={{0,2},{1,3},{2,0},{3,1},{4,6},{5,7},{6,4},{7,5},{8,10},{9,11},{10,... | collective-permute-start | bytes 294920 | tf_op jit(solution)/shard_map/ppermute | solution.py:406
  33.7 1.3 %collective-permute-start.12 = (bf16[384,128]{1,0:T(8,128)(2,1)S(1)}, bf16[384,128]{1,0:T(8,128)(2,1)S(1)}, u32[]{:S(2)}, u32[]{:S(2)}) collective-permute-start(bf16[384,128]{1,0:T(8,128)(2,1)S(1)} %get-tuple-element.61.own), channel_id=1, source_target_pairs={{0,3},{1,2},{2,1},{3,0},{4,7},{5,6},{6,5},{7,4},{8,11},{9,10},{10,... | collective-permute-start | bytes 294920 | tf_op jit(solution)/shard_map/ppermute | solution.py:406
  35.1 1.3 %collective-permute-start.11 = (bf16[256,128]{1,0:T(8,128)(2,1)S(1)}, bf16[256,128]{1,0:T(8,128)(2,1)S(1)}, u32[]{:S(2)}, u32[]{:S(2)}) collective-permute-start(bf16[256,128]{1,0:T(8,128)(2,1)S(1)} %get-tuple-element.62), channel_id=1, source_target_pairs={{0,4},{4,8},{8,12},{12,16},{16,20},{20,24},{24,28},{1,5},{5,9},{9,... | collective-permute-start | bytes 196616 | tf_op jit(solution)/shard_map/ppermute | solution.py:520
  36.4 0.9 %collective-permute-done.11.rim = bf16[256,128]{1,0:T(8,128)(2,1)S(1)} collective-permute-done((bf16[256,128]{1,0:T(8,128)(2,1)S(1)}, bf16[256,128]{1,0:T(8,128)(2,1)S(1)}, u32[]{:S(2)}, u32[]{:S(2)}) %collective-permute-start.11) | collective-permute-done | bytes 65568 | tf_op jit(solution)/shard_map/ppermute | solution.py:520
  37.2 4.9 %collective-permute-done.13.refs_1_ = bf16[384,128]{1,0:T(8,128)(2,1)S(1)} collective-permute-done((bf16[384,128]{1,0:T(8,128)(2,1)S(1)}, bf16[384,128]{1,0:T(8,128)(2,1)S(1)}, u32[]{:S(2)}, u32[]{:S(2)}) %collective-permute-start.13) | collective-permute-done | bytes 98336 | tf_op jit(solution)/shard_map/ppermute | solution.py:406
  42.2 5.8 %rebuild.1 = (bf16[4096,768]{1,0:T(8,128)(2,1)S(1)}, bf16[768,256]{1,0:T(8,128)(2,1)S(1)}, f32[8,768]{1,0:T(8,128)S(1)}, f32[8,256]{1,0:T(8,128)S(1)}, f32[520,2...) custom-call(s32[1,2]{1,0:T(1,128)S(1)} %add_bitcast_fusion.place, ...), custom_call_target="tpu_custom_call" | custom-call | tf_op jit(solution)/shard_map/rebuild/pallas_call | solution.py:23
  48.6 1.5 %kept.1 = (f32[512,256]{1,0:T(8,128)S(1)}, f32[512,256]{1,0:T(8,128)S(1)}, f32[512,256]{1,0:T(8,128)S(1)}, f32[512,256]{1,0:T(8,128)S(1)}) custom-call(s32[1,2]{1,0:T(1,128)S(1)} %add_bitcast_fusion.place, bf16[4096,768]{1,0:T(8,128)(2,1)S(1)} %get-tuple-element.66.stacked, bf16[768,256]{1,0:T(8,128)(2,1)S(1)} %get-tuple-element.67.ratio), custom_call_target="tpu_custom_call" | custom-call | tf_op jit(solution)/shard_map/kept/pallas_call | solution.py:23
  50.3 1.6 %collective-permute-start.16 = (f16[528,256]{1,0:T(8,128)(2,1)S(1)}, f16[528,256]{1,0:T(8,128)(2,1)S(1)}, u32[]{:S(2)}, u32[]{:S(2)}) collective-permute-start(f16[528,256]{1,0:T(8,128)(2,1)S(1)} %convert_element_type.24), channel_id=1, source_target_pairs={{0,8},{4,20},{8,0},{12,28},{16,24},{20,4},{24,16},{28,12},{1,9},{5... | collective-permute-start | bytes 811016 | tf_op jit(solution)/shard_map/ppermute | solution.py:566
  52.2 1.6 %collective-permute-start.21 = (f16[528,256]{1,0:T(8,128)(2,1)S(1)}, f16[528,256]{1,0:T(8,128)(2,1)S(1)}, u32[]{:S(2)}, u32[]{:S(2)}) collective-permute-start(f16[528,256]{1,0:T(8,128)(2,1)S(1)} %convert_element_type.26), channel_id=1, source_target_pairs={{0,8},{4,20},{8,0},{12,28},{16,24},{20,4},{24,16},{28,12},{1,9},{5... | collective-permute-start | bytes 811016 | tf_op jit(solution)/shard_map/ppermute | solution.py:566
  53.8 1.8 %collective-permute-start.18 = (f32[1,768]{1,0:T(1,128)S(1)}, f32[1,768]{1,0:T(1,128)S(1)}, u32[]{:S(2)}, u32[]{:S(2)}) collective-permute-start(f32[1,768]{1,0:T(1,128)S(1)} %slice.10), channel_id=1, source_target_pairs={{0,1},{1,0},{2,3},{3,2},{4,5},{5,4},{6,7},{7,6},{8,9},{9,8},{10,11... | collective-permute-start | bytes 9224 | tf_op jit(solution)/shard_map/ppermute | solution.py:406
  55.6 1.8 %collective-permute-done.18 = f32[1,768]{1,0:T(1,128)S(1)} collective-permute-done((f32[1,768]{1,0:T(1,128)S(1)}, f32[1,768]{1,0:T(1,128)S(1)}, u32[]{:S(2)}, u32[]{:S(2)}) %collective-permute-start.18) | collective-permute-done | bytes 3104 | tf_op jit(solution)/shard_map/ppermute | solution.py:406
  57.6 1.0 %collective-permute-start.23 = (f16[528,256]{1,0:T(8,128)(2,1)S(1)}, f16[528,256]{1,0:T(8,128)(2,1)S(1)}, u32[]{:S(2)}, u32[]{:S(2)}) collective-permute-start(f16[528,256]{1,0:T(8,128)(2,1)S(1)} %convert_element_type.28), channel_id=1, source_target_pairs={{0,16},{4,12},{8,24},{12,4},{16,0},{20,28},{24,8},{28,20},{1,17},{... | collective-permute-start | bytes 811016 | tf_op jit(solution)/shard_map/ppermute | solution.py:566
  58.6 2.3 %collective-permute-start.19 = (f32[1,768]{1,0:T(1,128)S(1)}, f32[1,768]{1,0:T(1,128)S(1)}, u32[]{:S(2)}, u32[]{:S(2)}) collective-permute-start(f32[1,768]{1,0:T(1,128)S(1)} %add.14), channel_id=1, source_target_pairs={{0,2},{1,3},{2,0},{3,1},{4,6},{5,7},{6,4},{7,5},{8,10},{9,11},{10,... | collective-permute-start | bytes 9224 | tf_op jit(solution)/shard_map/ppermute | solution.py:406
  60.9 2.2 %collective-permute-done.19 = f32[1,768]{1,0:T(1,128)S(1)} collective-permute-done((f32[1,768]{1,0:T(1,128)S(1)}, f32[1,768]{1,0:T(1,128)S(1)}, u32[]{:S(2)}, u32[]{:S(2)}) %collective-permute-start.19) | collective-permute-done | bytes 3104 | tf_op jit(solution)/shard_map/ppermute | solution.py:406
  64.2 0.9 %total.1 = f32[512,256]{1,0:T(8,128)} custom-call(f32[512,256]{1,0:T(8,128)S(1)} %get-tuple-element.74.kept, f32[520,256]{1,0:T(8,128)S(1)} %collective-permute-done.20.crossed, f32[528,256]{1,0:T(8,128)S(1)} %convert_element_type.27.refs_0_, f32[528,256]{1,0:T(8,128)S(1)} %convert_element_type.29.refs_1_), custom_call_target="tpu_custom_call" | custom-call | tf_op jit(solution)/shard_map/total/pallas_call | solution.py:23
  (60 shorter events, 6.1 us)
Async XLA Ops:
  0.6 17.1 %copy-start.6 = (f32[256]{0:T(256)S(1)}, f32[256]{0:T(256)}, u32[]{:S(2)}) copy-start(f32[256]{0:T(256)} %param.10) | copy-start | bytes 3076
  0.6 17.0 %copy-start.7 = (f32[256]{0:T(256)S(1)}, f32[256]{0:T(256)}, u32[]{:S(2)}) copy-start(f32[256]{0:T(256)} %param.11) | copy-start | bytes 3076
  0.7 23.4 %copy-start.8 = (s32[256]{0:T(256)S(1)}, s32[256]{0:T(256)}, u32[]{:S(2)}) copy-start(s32[256]{0:T(256)} %param.16) | copy-start | bytes 3076
  0.7 23.4 %copy-start.2 = (f32[2,256,768]{2,1,0:T(8,128)S(1)}, f32[2,256,768]{2,1,0:T(8,128)}, u32[]{:S(2)}) copy-start(f32[2,256,768]{2,1,0:T(8,128)} %uniform.1) | copy-start | bytes 4718596
  3.9 5.2 %collective-permute-start.1 = (f32[4,256]{1,0:T(4,128)S(1)}, f32[4,256]{1,0:T(4,128)S(1)}, u32[]{:S(2)}, u32[]{:S(2)}) collective-permute-start(f32[4,256]{1,0:T(4,128)S(1)} %get-tuple-element.45), channel_id=1, source_target_pairs={{0,4},{4,0},{8,12},{12,8},{16,20},{20,16},{24,28},{28,24},{1,5},{5... | collective-permute-start | bytes 12296 | tf_op jit(solution)/shard_map/ppermute | solution.py:406
  4.4 13.3 %collective-permute-start = (bf16[336,256]{1,0:T(8,128)(2,1)S(1)}, bf16[336,256]{1,0:T(8,128)(2,1)S(1)}, u32[]{:S(2)}, u32[]{:S(2)}) collective-permute-start(bf16[336,256]{1,0:T(8,128)(2,1)S(1)} %get-tuple-element.44), channel_id=1, source_target_pairs={{0,3},{1,2},{2,1},{3,0},{4,7},{5,6},{6,5},{7,4},{8,11},{9,10},{10,... | collective-permute-start | bytes 516104 | tf_op jit(solution)/shard_map/ppermute | solution.py:406
  9.1 4.6 %collective-permute-start.4 = (f32[8,256]{1,0:T(8,128)S(1)}, f32[8,256]{1,0:T(8,128)S(1)}, u32[]{:S(2)}, u32[]{:S(2)}) collective-permute-start(f32[8,256]{1,0:T(8,128)S(1)} %pad_maximum_fusion.1.refs_1_), channel_id=1, source_target_pairs={{0,24},{4,28},{8,16},{12,20},{16,8},{20,12},{24,0},{28,4},{1,25},{... | collective-permute-start | bytes 24584 | tf_op jit(solution)/shard_map/ppermute | solution.py:406
  11.6 3.7 %collective-permute-start.3 = (f32[8,256]{1,0:T(8,128)S(1)}, f32[8,256]{1,0:T(8,128)S(1)}, u32[]{:S(2)}, u32[]{:S(2)}) collective-permute-start(f32[8,256]{1,0:T(8,128)S(1)} %pad_maximum_fusion.1.refs_1_), channel_id=1, source_target_pairs={{0,16},{4,20},{8,24},{12,28},{16,0},{20,4},{24,8},{28,12},{1,17},{... | collective-permute-start | bytes 24584 | tf_op jit(solution)/shard_map/ppermute | solution.py:406
  12.1 3.7 %collective-permute-start.2 = (f32[8,256]{1,0:T(8,128)S(1)}, f32[8,256]{1,0:T(8,128)S(1)}, u32[]{:S(2)}, u32[]{:S(2)}) collective-permute-start(f32[8,256]{1,0:T(8,128)S(1)} %pad_maximum_fusion.1.refs_1_), channel_id=1, source_target_pairs={{0,8},{4,12},{8,0},{12,4},{16,24},{20,28},{24,16},{28,20},{1,9},{5... | collective-permute-start | bytes 24584 | tf_op jit(solution)/shard_map/ppermute | solution.py:406
  12.6 12.7 %collective-permute-start.5 = (bf16[336,256]{1,0:T(8,128)(2,1)S(1)}, bf16[336,256]{1,0:T(8,128)(2,1)S(1)}, u32[]{:S(2)}, u32[]{:S(2)}) collective-permute-start(bf16[336,256]{1,0:T(8,128)(2,1)S(1)} %get-tuple-element.52), channel_id=1, source_target_pairs={{0,2},{1,3},{2,0},{3,1},{4,6},{5,7},{6,4},{7,5},{8,10},{9,11},{10,... | collective-permute-start | bytes 516104 | tf_op jit(solution)/shard_map/ppermute | solution.py:406
  15.8 10.3 %collective-permute-start.6 = (bf16[336,256]{1,0:T(8,128)(2,1)S(1)}, bf16[336,256]{1,0:T(8,128)(2,1)S(1)}, u32[]{:S(2)}, u32[]{:S(2)}) collective-permute-start(bf16[336,256]{1,0:T(8,128)(2,1)S(1)} %get-tuple-element.53), channel_id=1, source_target_pairs={{0,1},{1,0},{2,3},{3,2},{4,5},{5,4},{6,7},{7,6},{8,9},{9,8},{10,11... | collective-permute-start | bytes 516104 | tf_op jit(solution)/shard_map/ppermute | solution.py:406
  17.4 6.7 %copy-start.4 = (f32[256,768]{1,0:T(8,128)S(1)}, f32[256,768]{1,0:T(8,128)}, u32[]{:S(2)}) copy-start(f32[256,768]{1,0:T(8,128)} %gauss.1) | copy-start | bytes 2359300
  18.5 7.5 %collective-permute-start.7 = (f32[22,256]{1,0:T(8,128)S(1)}, f32[22,256]{1,0:T(8,128)S(1)}, u32[]{:S(2)}, u32[]{:S(2)}) collective-permute-start(f32[22,256]{1,0:T(8,128)S(1)} %get-tuple-element.54), channel_id=1, source_target_pairs={{0,3},{1,2},{2,1},{3,0},{4,7},{5,6},{6,5},{7,4},{8,11},{9,10},{10,... | collective-permute-start | bytes 67592 | tf_op jit(solution)/shard_map/ppermute | solution.py:406
  20.1 6.0 %collective-permute-start.8 = (f32[22,256]{1,0:T(8,128)S(1)}, f32[22,256]{1,0:T(8,128)S(1)}, u32[]{:S(2)}, u32[]{:S(2)}) collective-permute-start(f32[22,256]{1,0:T(8,128)S(1)} %get-tuple-element.55), channel_id=1, source_target_pairs={{0,2},{1,3},{2,0},{3,1},{4,6},{5,7},{6,4},{7,5},{8,10},{9,11},{10,... | collective-permute-start | bytes 67592 | tf_op jit(solution)/shard_map/ppermute | solution.py:406
  24.0 3.8 %collective-permute-start.9 = (f32[22,256]{1,0:T(8,128)S(1)}, f32[22,256]{1,0:T(8,128)S(1)}, u32[]{:S(2)}, u32[]{:S(2)}) collective-permute-start(f32[22,256]{1,0:T(8,128)S(1)} %get-tuple-element.56), channel_id=1, source_target_pairs={{0,1},{1,0},{2,3},{3,2},{4,5},{5,4},{6,7},{7,6},{8,9},{9,8},{10,11... | collective-permute-start | bytes 67592 | tf_op jit(solution)/shard_map/ppermute | solution.py:406
  24.1 5.3 %copy-start.5 = (bf16[256,256]{1,0:T(8,128)(2,1)S(1)}, bf16[256,256]{1,0:T(8,128)(2,1)}, u32[]{:S(2)}) copy-start(bf16[256,256]{1,0:T(8,128)(2,1)} %encoder.1) | copy-start | bytes 393220
  27.8 14.3 %copy-start.1 = (bf16[256,4096]{1,0:T(8,128)(2,1)S(1)}, bf16[256,4096]{1,0:T(8,128)(2,1)}, u32[]{:S(2)}) copy-start(bf16[256,4096]{1,0:T(8,128)(2,1)} %templates.3) | copy-start | bytes 6291460
  27.8 14.3 %copy-start.3 = (bf16[256,768]{1,0:T(8,128)(2,1)S(1)}, bf16[256,768]{1,0:T(8,128)(2,1)}, u32[]{:S(2)}) copy-start(bf16[256,768]{1,0:T(8,128)(2,1)} %spectrum.1) | copy-start | bytes 1179652
  27.8 1.5 %collective-permute-start.10 = (bf16[384,256]{1,0:T(8,128)(2,1)S(1)}, bf16[384,256]{1,0:T(8,128)(2,1)S(1)}, u32[]{:S(2)}, u32[]{:S(2)}) collective-permute-start(bf16[384,256]{1,0:T(8,128)(2,1)S(1)} %halves.1), channel_id=1, source_target_pairs={{0,4},{4,0},{8,12},{12,8},{16,20},{20,16},{24,28},{28,24},{1,5},{5... | collective-permute-start | bytes 589832 | tf_op jit(solution)/shard_map/ppermute | solution.py:406
  30.6 6.6 %collective-permute-start.14 = (bf16[384,128]{1,0:T(8,128)(2,1)S(1)}, bf16[384,128]{1,0:T(8,128)(2,1)S(1)}, u32[]{:S(2)}, u32[]{:S(2)}) collective-permute-start(bf16[384,128]{1,0:T(8,128)(2,1)S(1)} %get-tuple-element.61.own), channel_id=1, source_target_pairs={{0,1},{1,0},{2,3},{3,2},{4,5},{5,4},{6,7},{7,6},{8,9},{9,8},{10,11... | collective-permute-start | bytes 294920 | tf_op jit(solution)/shard_map/ppermute | solution.py:406
  31.7 10.5 %collective-permute-start.13 = (bf16[384,128]{1,0:T(8,128)(2,1)S(1)}, bf16[384,128]{1,0:T(8,128)(2,1)S(1)}, u32[]{:S(2)}, u32[]{:S(2)}) collective-permute-start(bf16[384,128]{1,0:T(8,128)(2,1)S(1)} %get-tuple-element.61.own), channel_id=1, source_target_pairs={{0,2},{1,3},{2,0},{3,1},{4,6},{5,7},{6,4},{7,5},{8,10},{9,11},{10,... | collective-permute-start | bytes 294920 | tf_op jit(solution)/shard_map/ppermute | solution.py:406
  33.7 8.4 %collective-permute-start.12 = (bf16[384,128]{1,0:T(8,128)(2,1)S(1)}, bf16[384,128]{1,0:T(8,128)(2,1)S(1)}, u32[]{:S(2)}, u32[]{:S(2)}) collective-permute-start(bf16[384,128]{1,0:T(8,128)(2,1)S(1)} %get-tuple-element.61.own), channel_id=1, source_target_pairs={{0,3},{1,2},{2,1},{3,0},{4,7},{5,6},{6,5},{7,4},{8,11},{9,10},{10,... | collective-permute-start | bytes 294920 | tf_op jit(solution)/shard_map/ppermute | solution.py:406
  35.1 2.2 %collective-permute-start.11 = (bf16[256,128]{1,0:T(8,128)(2,1)S(1)}, bf16[256,128]{1,0:T(8,128)(2,1)S(1)}, u32[]{:S(2)}, u32[]{:S(2)}) collective-permute-start(bf16[256,128]{1,0:T(8,128)(2,1)S(1)} %get-tuple-element.62), channel_id=1, source_target_pairs={{0,4},{4,8},{8,12},{12,16},{16,20},{20,24},{24,28},{1,5},{5,9},{9,... | collective-permute-start | bytes 196616 | tf_op jit(solution)/shard_map/ppermute | solution.py:520
  48.0 2.2 %collective-permute-start.15 = (f32[520,256]{1,0:T(8,128)S(1)}, f32[520,256]{1,0:T(8,128)S(1)}, u32[]{:S(2)}, u32[]{:S(2)}) collective-permute-start(f32[520,256]{1,0:T(8,128)S(1)} %get-tuple-element.69), channel_id=1, source_target_pairs={{0,4},{4,0},{8,12},{12,8},{16,20},{20,16},{24,28},{28,24},{1,5},{5... | collective-permute-start | bytes 1597448 | tf_op jit(solution)/shard_map/ppermute | solution.py:406
  48.1 4.0 %collective-permute-start.17 = (f32[520,256]{1,0:T(8,128)S(1)}, f32[520,256]{1,0:T(8,128)S(1)}, u32[]{:S(2)}, u32[]{:S(2)}) collective-permute-start(f32[520,256]{1,0:T(8,128)S(1)} %get-tuple-element.71), channel_id=1, source_target_pairs={{0,4},{4,0},{8,12},{12,8},{16,20},{20,16},{24,28},{28,24},{1,5},{5... | collective-permute-start | bytes 1597448 | tf_op jit(solution)/shard_map/ppermute | solution.py:406
  48.6 8.9 %collective-permute-start.22 = (f32[520,256]{1,0:T(8,128)S(1)}, f32[520,256]{1,0:T(8,128)S(1)}, u32[]{:S(2)}, u32[]{:S(2)}) collective-permute-start(f32[520,256]{1,0:T(8,128)S(1)} %get-tuple-element.78), channel_id=1, source_target_pairs={{0,4},{4,0},{8,12},{12,8},{16,20},{20,16},{24,28},{28,24},{1,5},{5... | collective-permute-start | bytes 1597448 | tf_op jit(solution)/shard_map/ppermute | solution.py:406
  50.3 7.1 %collective-permute-start.16 = (f16[528,256]{1,0:T(8,128)(2,1)S(1)}, f16[528,256]{1,0:T(8,128)(2,1)S(1)}, u32[]{:S(2)}, u32[]{:S(2)}) collective-permute-start(f16[528,256]{1,0:T(8,128)(2,1)S(1)} %convert_element_type.24), channel_id=1, source_target_pairs={{0,8},{4,20},{8,0},{12,28},{16,24},{20,4},{24,16},{28,12},{1,9},{5... | collective-permute-start | bytes 811016 | tf_op jit(solution)/shard_map/ppermute | solution.py:566
  51.9 12.3 %collective-permute-start.20 = (f32[520,256]{1,0:T(8,128)S(1)}, f32[520,256]{1,0:T(8,128)S(1)}, u32[]{:S(2)}, u32[]{:S(2)}) collective-permute-start(f32[520,256]{1,0:T(8,128)S(1)} %get-tuple-element.75), channel_id=1, source_target_pairs={{0,4},{4,0},{8,12},{12,8},{16,20},{20,16},{24,28},{28,24},{1,5},{5... | collective-permute-start | bytes 1597448 | tf_op jit(solution)/shard_map/ppermute | solution.py:406
  52.2 8.7 %collective-permute-start.21 = (f16[528,256]{1,0:T(8,128)(2,1)S(1)}, f16[528,256]{1,0:T(8,128)(2,1)S(1)}, u32[]{:S(2)}, u32[]{:S(2)}) collective-permute-start(f16[528,256]{1,0:T(8,128)(2,1)S(1)} %convert_element_type.26), channel_id=1, source_target_pairs={{0,8},{4,20},{8,0},{12,28},{16,24},{20,4},{24,16},{28,12},{1,9},{5... | collective-permute-start | bytes 811016 | tf_op jit(solution)/shard_map/ppermute | solution.py:566
  53.8 3.6 %collective-permute-start.18 = (f32[1,768]{1,0:T(1,128)S(1)}, f32[1,768]{1,0:T(1,128)S(1)}, u32[]{:S(2)}, u32[]{:S(2)}) collective-permute-start(f32[1,768]{1,0:T(1,128)S(1)} %slice.10), channel_id=1, source_target_pairs={{0,1},{1,0},{2,3},{3,2},{4,5},{5,4},{6,7},{7,6},{8,9},{9,8},{10,11... | collective-permute-start | bytes 9224 | tf_op jit(solution)/shard_map/ppermute | solution.py:406
  57.6 6.5 %collective-permute-start.23 = (f16[528,256]{1,0:T(8,128)(2,1)S(1)}, f16[528,256]{1,0:T(8,128)(2,1)S(1)}, u32[]{:S(2)}, u32[]{:S(2)}) collective-permute-start(f16[528,256]{1,0:T(8,128)(2,1)S(1)} %convert_element_type.28), channel_id=1, source_target_pairs={{0,16},{4,12},{8,24},{12,4},{16,0},{20,28},{24,8},{28,20},{1,17},{... | collective-permute-start | bytes 811016 | tf_op jit(solution)/shard_map/ppermute | solution.py:566
  58.6 4.5 %collective-permute-start.19 = (f32[1,768]{1,0:T(1,128)S(1)}, f32[1,768]{1,0:T(1,128)S(1)}, u32[]{:S(2)}, u32[]{:S(2)}) collective-permute-start(f32[1,768]{1,0:T(1,128)S(1)} %add.14), channel_id=1, source_target_pairs={{0,2},{1,3},{2,0},{3,1},{4,6},{5,7},{6,4},{7,5},{8,10},{9,11},{10,... | collective-permute-start | bytes 9224 | tf_op jit(solution)/shard_map/ppermute | solution.py:406
  (1 other events, 1.6 us)
